TPU v7x, 128 devices: a whole 4x4x4 slice. The times are simulated.
128 devices in a mesh: tm: 32 (over y, z_hi, x), pol: 4 (over z_lo, core).
Axes of the slice: x: 4, y: 4, z: 4 (z_hi: 2, z_lo: 2; z = z_hi * 2 + z_lo), core: 2. Of those that a mesh axis runs over, the one named last changes fastest.
Arguments:
- voltages: bfloat16 [128, 1572864], P('pol', 'tm'), may hold values from -22 to 22
- phase_bin: int32 [192], replicated, may hold values from 0 to 7, as said below
Outputs:
- visibilities: bfloat16 [4096, 8, 2, 128, 128], P('tm', None, None, 'pol')
Inputs may be any that keep to these rules, and one draw needn't show every extreme that they name: `phase_bin`: each of the 8 bins holds exactly 24 spectra.
All inputs are finite; a program needn't handle non-finite values.
Results may differ from a plain program's by a relative error of at most 0.019.
Values may be sent and summed in bfloat16 or wider, within the bound.
No kernel may reach another device: no remote copies, remote signals or barrier semaphores. Data moves between devices by JAX's collectives and lax.ppermute only.
A program may use at most 320 MiB of HBM per device.

v0:
```python
import math

import jax
import jax.numpy as jnp
from jax import lax
from jax.sharding import PartitionSpec as P

FFT_LEN = 8192
TAPS = 4
NBINS = 8
CHANNELS = 4096


def passed_along(x, axis, by):
    devices = lax.axis_size(axis)
    pairs = [(i, i + by) for i in range(devices) if 0 <= i + by < devices]
    return lax.ppermute(x, axis, pairs)


def filter_window():
    length = TAPS * FFT_LEN
    place = jnp.arange(length, dtype=jnp.float32)
    center = (place - length / 2 + 0.5) / FFT_LEN
    taper = 0.5 - 0.5 * jnp.cos(2.0 * math.pi * (place + 0.5) / length)
    return (jnp.sinc(center) * taper).reshape(TAPS, FFT_LEN)


def dft_table(first, count):
    samples = jnp.arange(FFT_LEN, dtype=jnp.int32)
    columns = first + jnp.arange(count, dtype=jnp.int32)
    phase = samples[:, None] * columns[None, :] % FFT_LEN
    angle = phase.astype(jnp.float32) * (2.0 * math.pi / FFT_LEN)
    return jnp.concatenate([jnp.cos(angle), -jnp.sin(angle)], axis=1).astype(jnp.bfloat16)


def transform(spectra_rows):
    block_width = min(512, CHANNELS)
    real_parts = []
    imag_parts = []
    for number in range(CHANNELS // block_width):
        table = dft_table(number * block_width, block_width)
        product = jnp.dot(spectra_rows, table, preferred_element_type=jnp.float32)
        real_parts.append(product[:, :block_width])
        imag_parts.append(product[:, block_width:])
    return (jnp.concatenate(real_parts, axis=1), jnp.concatenate(imag_parts, axis=1))


def bin_grams(left_data, right_data, per_bin):
    left_rows = left_data.shape[2]
    right_rows = right_data.shape[2]
    width = left_data.shape[3]
    left = left_data.reshape(2, NBINS, per_bin, left_rows, width)
    right = right_data.reshape(2, NBINS, per_bin, right_rows, width)
    left_side = jnp.concatenate([left[0], left[1]], axis=1)
    right_real = jnp.concatenate([right[0], right[1]], axis=1)
    right_imag = jnp.concatenate([-right[1], right[0]], axis=1)
    real_sum = jnp.einsum(
        "bsic,bsjc->cbij", left_side, right_real, preferred_element_type=jnp.float32
    )
    imag_sum = jnp.einsum(
        "bsic,bsjc->cbij", left_side, right_imag, preferred_element_type=jnp.float32
    )
    return (jnp.stack([real_sum, imag_sum], axis=2) / per_bin).astype(jnp.bfloat16)


def on_device(voltages, phase_bin):
    paths_dev = voltages.shape[0]
    local_spectra = voltages.shape[1] // FFT_LEN
    time_devs = lax.axis_size("tm")
    path_devs = lax.axis_size("pol")
    blocks = voltages.reshape(paths_dev, local_spectra, FFT_LEN)
    earlier = passed_along(blocks[:, local_spectra - (TAPS - 1) :], "tm", 1)
    padded = jnp.concatenate([earlier, blocks], axis=1)
    window = filter_window()
    filtered = jnp.zeros((paths_dev, local_spectra, FFT_LEN), jnp.float32)
    for tap in range(TAPS):
        filtered = filtered + window[tap] * padded[:, tap : tap + local_spectra].astype(jnp.float32)
    filtered = filtered.astype(jnp.bfloat16)
    spectra_rows = jnp.transpose(filtered, (1, 0, 2)).reshape(local_spectra * paths_dev, FFT_LEN)
    real_part, imag_part = transform(spectra_rows)
    real_part = real_part.reshape(local_spectra, paths_dev, CHANNELS)
    imag_part = imag_part.reshape(local_spectra, paths_dev, CHANNELS)
    local_power = jnp.sum(real_part * real_part + imag_part * imag_part, axis=0)
    bandpass = lax.psum(local_power.astype(jnp.bfloat16), "tm").astype(jnp.float32)
    total_spectra = local_spectra * time_devs
    equalizer = lax.rsqrt(bandpass / total_spectra + 1e-06)
    scaled = jnp.stack([real_part * equalizer, imag_part * equalizer]).astype(jnp.bfloat16)
    ordering = jnp.argsort(phase_bin, stable=True)
    per_bin = total_spectra // NBINS
    quarter = CHANNELS // (time_devs * path_devs)
    split = scaled.reshape(2, local_spectra, paths_dev, time_devs, path_devs, quarter)
    turned = lax.all_to_all(
        lax.all_to_all(split, "tm", split_axis=3, concat_axis=1, tiled=True),
        "pol",
        split_axis=4,
        concat_axis=2,
        tiled=True,
    )
    turned = turned.reshape(2, total_spectra, paths_dev * path_devs, quarter)
    ordered = jnp.take(turned, ordering, axis=1)
    whole = bin_grams(ordered, ordered, per_bin)
    return lax.all_to_all(whole, "pol", split_axis=3, concat_axis=0, tiled=True)


def solution(mesh):
    in_specs = (P("pol", "tm"), P())
    out_specs = P("tm", None, None, "pol", None)
    return jax.shard_map(
        on_device, mesh=mesh, in_specs=in_specs, out_specs=out_specs, check_vma=False
    )
```

profile of v0, /device:TPU:1, one launch (start us, length us, event | category | flops | bytes accessed | tf_op | source)
XLA Modules:
  0.0 1487.8 jit_solution(7006945730580305178)
XLA Ops:
  23.4 69.0 %cosine_convert_fusion = (bf16[8192,512]{1,0:T(8,128)(2,1)S(1)}, bf16[8192,512]{1,0:T(8,128)(2,1)}) fusion(s32[512]{0:T(512)S(1)} %iota_add_fusion.2), kind=kLoop, calls=%fused_computation.84 | loop fusion | flops 71303168 | bytes 16779264 | tf_op jit(solution)/shard_map/convert.2
  92.3 69.1 %cosine_convert_fusion.1 = (bf16[8192,512]{1,0:T(8,128)(2,1)}, bf16[8192,512]{1,0:T(8,128)(2,1)}) fusion(s32[512]{0:T(512)S(1)} %iota_add_fusion.3), kind=kLoop, calls=%fused_computation.88 | loop fusion | flops 71303168 | bytes 16779264 | tf_op jit(solution)/shard_map/convert.4
  161.4 69.1 %cosine_convert_fusion.2 = (bf16[8192,512]{1,0:T(8,128)(2,1)}, bf16[8192,512]{1,0:T(8,128)(2,1)}) fusion(s32[512]{0:T(512)S(1)} %iota_add_fusion.4), kind=kLoop, calls=%fused_computation.92 | loop fusion | flops 71303168 | bytes 16779264 | tf_op jit(solution)/shard_map/convert.6
  230.5 69.1 %cosine_convert_fusion.3 = (bf16[8192,512]{1,0:T(8,128)(2,1)}, bf16[8192,512]{1,0:T(8,128)(2,1)}) fusion(s32[512]{0:T(512)S(1)} %iota_add_fusion.5), kind=kLoop, calls=%fused_computation.96 | loop fusion | flops 71303168 | bytes 16779264 | tf_op jit(solution)/shard_map/convert.8
  299.6 69.1 %cosine_convert_fusion.4 = (bf16[8192,512]{1,0:T(8,128)(2,1)}, bf16[8192,512]{1,0:T(8,128)(2,1)}) fusion(s32[512]{0:T(512)S(1)} %iota_add_fusion.6), kind=kLoop, calls=%fused_computation.100 | loop fusion | flops 71303168 | bytes 16779264 | tf_op jit(solution)/shard_map/convert.10
  368.7 69.3 %cosine_convert_fusion.5 = (bf16[8192,512]{1,0:T(8,128)(2,1)}, bf16[8192,512]{1,0:T(8,128)(2,1)}) fusion(s32[512]{0:T(512)S(1)} %iota_add_fusion.7), kind=kLoop, calls=%fused_computation.104 | loop fusion | flops 71303168 | bytes 16779264 | tf_op jit(solution)/shard_map/convert.12
  438.0 69.1 %cosine_convert_fusion.6 = (bf16[8192,512]{1,0:T(8,128)(2,1)}, bf16[8192,512]{1,0:T(8,128)(2,1)}) fusion(s32[512]{0:T(512)S(1)} %iota_add_fusion.8), kind=kLoop, calls=%fused_computation.108 | loop fusion | flops 71303168 | bytes 16779264 | tf_op jit(solution)/shard_map/convert.14
  507.0 68.8 %negate_convert_fusion.7 = (bf16[8192,512]{1,0:T(8,128)(2,1)}, bf16[8192,512]{1,0:T(8,128)(2,1)}) fusion(), kind=kLoop, calls=%fused_computation.111 | loop fusion | flops 71303168 | bytes 16777216 | tf_op jit(solution)/shard_map/convert.17
  585.9 10.0 fusion.25
  623.6 10.1 fusion.41
  633.6 9.6 fusion.37
  676.2 9.9 reshape.102
  686.1 311.8 %all-reduce.2.cloned.1.call-done = bf16[32,4096]{1,0:T(8,128)(2,1)} async-done(((bf16[32,4096]{1,0:T(8,128)(2,1)}), bf16[32,4096]{1,0:T(8,128)(2,1)}) %all-reduce.2.cloned.1.call-update) | async-done | bytes 262160 | tf_op jit(solution)/shard_map/psum | solution.py:84
  1001.2 23.5 %fusion.82 = (bf16[1,6,32,32,4,32]{5,2,4,1,0,3:T(8,128)(2,1)S(1)}, bf16[1,6,32,32,4,32]{5,2,4,1,0,3:T(8,128)(2,1)S(1)}) fusion(f32[1,6,32,32,4,32]{5,4,3,2,1,0:T(4,128)} %reshape.101, f32[32,32,4,32]{3,0,2,1:T(8,128)S(1)} %copy.24, f32[1,6,32,32,4,32]{5,4,3,2,1,0:T(4,128)} %reshape.102), kind=kLoop, calls=%fused_computation.127 | loop fusion | flops 3145728 | bytes 9961472 | tf_op jit(solution)/shard_map/convert
  1030.6 16.2 %reshape.113 = bf16[32,2,24576]{2,1,0:T(2,128)(2,1)S(1)} reshape(bf16[32,2,6,4,32,32]{5,4,3,2,1,0:T(8,128)(2,1)} %fusion.130) | data formatting | bytes 6291456
  1046.8 31.9 %all_to_all.51 = bf16[32,2,24576]{2,1,0:T(2,128)(2,1)} all-to-all(bf16[32,2,24576]{2,1,0:T(2,128)(2,1)S(1)} %reshape.113), channel_id=1, replica_groups=mesh['tm'=32,'pol'=4] {'tm'}, dimensions={0} | all-to-all | bytes 6291456 | tf_op jit(solution)/shard_map/all_to_all | solution.py:93
  1078.8 14.5 reshape.114
  1106.5 16.4 %copy.28 = bf16[2,192,32,1,4,32]{1,5,3,2,0,4:T(8,128)(2,1)} copy(bf16[2,192,32,1,4,32]{5,2,4,1,0,3:T(8,128)(2,1)} %bitcast.38) | data formatting | bytes 6291456 | tf_op jit(solution)/shard_map/all_to_all | solution.py:93
  1122.9 28.5 %all-to-all-start.1 = ((bf16[2,192,32,1,4,32]{1,5,3,2,0,4:T(8,128)(2,1)}), bf16[2,192,32,1,4,32]{1,5,3,2,0,4:T(8,128)(2,1)}, u32[]{:S(2)}, u32[]{:S(2)}) async-start(bf16[2,192,32,1,4,32]{1,5,3,2,0,4:T(8,128)(2,1)} %copy.28), calls=%async_computation.1 | async-start | bytes 8388608 | tf_op jit(solution)/shard_map/all_to_all | solution.py:92
  1154.6 44.2 %all-to-all-done.1 = bf16[2,192,32,1,4,32]{1,5,3,2,0,4:T(8,128)(2,1)} async-done(((bf16[2,192,32,1,4,32]{1,5,3,2,0,4:T(8,128)(2,1)}), bf16[2,192,32,1,4,32]{1,5,3,2,0,4:T(8,128)(2,1)}, u32[]{:S(2)}, u32[]{:S(2)}) %all-to-all-start.1) | async-done | bytes 3145760 | tf_op jit(solution)/shard_map/all_to_all | solution.py:92
  1232.3 13.3 fusion
  1245.6 35.7 %copy.33 = bf16[32,8,2,128,128]{4,1,0,2,3:T(8,128)(2,1)S(1)} copy(bf16[32,8,2,128,128]{4,3,1,0,2:T(8,128)(2,1)S(1)} %fusion) | data formatting | bytes 33554432 | tf_op jit(solution)/shard_map/convert_element_type | solution.py:63
  1281.3 185.9 %all_to_all.52 = bf16[32,8,2,128,128]{4,1,0,2,3:T(8,128)(2,1)S(1)} all-to-all(bf16[32,8,2,128,128]{4,1,0,2,3:T(8,128)(2,1)S(1)} %copy.33), channel_id=1, replica_groups=mesh['tm'=32,'pol'=4] {'pol'}, dimensions={3} | all-to-all | bytes 33554432 | tf_op jit(solution)/shard_map/all_to_all | solution.py:102
  1467.3 13.4 copy.34
  (88 shorter events, 146.4 us)
Async XLA Ops:
  6.5 991.3 %all-reduce.2.cloned.1.call-start = ((), (), s32[]{:S(2)}) async-start(), calls=%async_computation.3 | async-start | bytes 524288 | tf_op jit(solution)/shard_map/psum | solution.py:84
  18.4 557.4 %collective-permute-start = (bf16[32,3,8192]{2,0,1:T(8,128)(2,1)S(1)}, bf16[32,3,8192]{2,0,1:T(8,128)(2,1)S(1)}, u32[]{:S(2)}, u32[]{:S(2)}) collective-permute-start(bf16[32,3,8192]{2,0,1:T(8,128)(2,1)S(1)} %copy.21), channel_id=1, source_target_pairs={{0,4},{4,8},{8,12},{12,16},{16,20},{20,24},{24,28},{28,32},{32,36}... | collective-permute-start | bytes 4718600 | tf_op jit(solution)/shard_map/ppermute | solution.py:17
  507.0 70.2 %copy-start = (bf16[32,6,8192]{2,1,0:T(8,128)(2,1)S(1)}, bf16[32,6,8192]{2,1,0:T(8,128)(2,1)}, u32[]{:S(2)}) copy-start(bf16[32,6,8192]{2,1,0:T(8,128)(2,1)} %reshape.99) | copy-start | bytes 9437188
  585.9 28.3 %copy-start.2 = (bf16[6,32,8192]{2,1,0:T(8,128)(2,1)}, bf16[6,32,8192]{2,1,0:T(8,128)(2,1)S(1)}, u32[]{:S(2)}) copy-start(bf16[6,32,8192]{2,1,0:T(8,128)(2,1)S(1)} %copy.23) | copy-start | bytes 9437188
  604.9 18.6 %slice-start = ((s8[8388608]{0:T(1024)(128)(4,1)}), s8[4194304]{0:T(1024)(128)(4,1)S(1)}, s32[]{:S(2)}) async-start(s8[8388608]{0:T(1024)(128)(4,1)} %bitcast.46), calls=%async_computation.4 | async-start | bytes 8388608
  614.3 9.3 slice-start.1
  623.6 19.7 %slice-start.2 = ((s8[8388608]{0:T(1024)(128)(4,1)}), s8[4194304]{0:T(1024)(128)(4,1)S(1)}, s32[]{:S(2)}) async-start(s8[8388608]{0:T(1024)(128)(4,1)} %bitcast.48), calls=%async_computation.6 | async-start | bytes 8388608
  633.6 9.6 slice-start.3
  633.6 9.6 copy-start.3
  651.5 8.4 copy-start.9
  651.5 8.4 copy-start.8
  651.5 8.5 copy-start.7
  651.5 8.6 copy-start.6
  659.8 1.1 copy-start.5
  659.8 1.4 copy-start.4
  661.2 1.7 copy-start.1
  1122.9 28.5 %copy-start.10 = (s32[192]{0:T(256)S(1)}, s32[192]{0:T(256)}, u32[]{:S(2)}) copy-start(s32[192]{0:T(256)} %param.3) | copy-start | bytes 2308
  1122.9 75.8 %all-to-all-start.1 = ((bf16[2,192,32,1,4,32]{1,5,3,2,0,4:T(8,128)(2,1)}), bf16[2,192,32,1,4,32]{1,5,3,2,0,4:T(8,128)(2,1)}, u32[]{:S(2)}, u32[]{:S(2)}) async-start(bf16[2,192,32,1,4,32]{1,5,3,2,0,4:T(8,128)(2,1)} %copy.28), calls=%async_computation.1 | async-start | bytes 8388608 | tf_op jit(solution)/shard_map/all_to_all | solution.py:92
Sparse Core Ops, SparseCore 0:
  668.0 329.8 all-reduce.1
where the time goes:
time: 1490 us
  other arithmetic  613 us (41%)
  waiting for transfers between devices  356 us (24%)
  blocking collectives  218 us (15%)
  local copies, waits for them, and re-layouts  167 us (11%)
  matrix products  87.2 us (6%)
  starting transfers between devices  32.7 us (2%)
    another operation x9, other arithmetic  576 us
    psum x1, waiting for transfers between devices, on_device(): lax.psum(local_power.astype(jnp.bfloat16), 'tm').astype(jnp.float32)  312 us
    all_to_all x1, blocking collectives, on_device(): return lax.all_to_all(whole, 'pol', split_axis=3, concat_axis=0, tiled=True)  186 us
    dot_general x8, matrix products, transform(): product = jnp.dot(spectra_rows, table, preferred_element_type=jnp.float32)  72.7 us
    all_to_all x1, waiting for transfers between devices, on_device(): lax.all_to_all(lax.all_to_all(split, 'tm', split_axis=3, concat_axis=1, t...  44.2 us
    convert_element_type x1, local copies, waits for them, and re-layouts, bin_grams(): (jnp.stack([real_sum, imag_sum], axis=2) / per_bin).astype(jnp.bfloat16)  35.7 us
    unnamed x39, local copies, waits for them, and re-layouts  34.8 us
    all_to_all x1, blocking collectives, on_device(): lax.all_to_all(split, 'tm', split_axis=3, concat_axis=1, tiled=True)  31.9 us
  transfers between devices with their start and end apart: 3, of which 2 were waited for; matrix products, arithmetic and copies ran while one was open for 39% of the time, Pallas kernels for 0%

commit v1 on v0

v1 whole, which is shorter than its diff:
```python
import functools
import math

import jax
import jax.numpy as jnp
import ml_dtypes
import numpy as np
from jax import lax
from jax.experimental import pallas as pl
from jax.experimental.pallas import tpu as pltpu
from jax.sharding import PartitionSpec as P

FFT_LEN = 8192
TAPS = 4
NBINS = 8
CHANNELS = 4096
RADIX = 8
INNER = FFT_LEN // RADIX
LANES = 128
HALF = 3
NT = (((1,), (1,)), ((), ()))


def filter_window():
    length = TAPS * FFT_LEN
    place = np.arange(length, dtype=np.float64)
    center = (place - length / 2 + 0.5) / FFT_LEN
    taper = 0.5 - 0.5 * np.cos(2.0 * math.pi * (place + 0.5) / length)
    return (np.sinc(center) * taper).reshape(TAPS, FFT_LEN).astype(np.float32)


def twiddles():
    angle = 2.0 * math.pi * np.outer(np.arange(RADIX), np.arange(INNER)) / FFT_LEN
    return np.concatenate([np.cos(angle), np.sin(angle)]).astype(np.float32)


def inner_table(time_devs):
    angle = 2.0 * math.pi * (np.outer(np.arange(INNER // 2), np.arange(INNER)) % INNER) / INNER
    real_rows = np.concatenate([np.cos(angle), np.sin(angle)], axis=1)
    imag_rows = np.concatenate([-np.sin(angle), np.cos(angle)], axis=1)
    rows = np.stack([part.reshape(time_devs, -1, 2 * INNER) for part in (real_rows, imag_rows)], axis=1)
    return rows.reshape(INNER, 2 * INNER).astype(ml_dtypes.bfloat16)


def spectra_kernel(first_ref, second_ref, window_ref, twiddle_ref, table_ref, out_ref, z_ref):
    paths = first_ref.shape[0]
    root = math.sqrt(0.5)

    def block(lane, carry):
        for s in range(HALF):
            f = []
            for n1 in range(RADIX):
                total = None
                for tap in range(TAPS):
                    number = s + tap
                    source = first_ref if number < HALF else second_ref
                    start = (number % HALF) * FFT_LEN + n1 * INNER
                    at = pl.ds(pl.multiple_of(start + lane * LANES, LANES), LANES)
                    w_at = pl.ds(pl.multiple_of(n1 * INNER + lane * LANES, LANES), LANES)
                    term = window_ref[tap : tap + 1, w_at] * source[:, at].astype(jnp.float32)
                    total = term if total is None else total + term
                f.append(total.astype(jnp.bfloat16).astype(jnp.float32))
            a = [f[n] + f[n + 4] for n in range(4)]
            b = [f[n] - f[n + 4] for n in range(4)]
            low, high = root * (b[1] - b[3]), root * (b[1] + b[3])
            y1 = (b[0] + low, -b[2] - high)
            y3 = (b[0] - low, b[2] - high)
            y2 = (a[0] - a[2], a[3] - a[1])
            even, odd = a[0] + a[2], a[1] + a[3]
            y = [(even + odd, None), y1, y2, y3, (even - odd, None)]
            y += [(re, -im) for re, im in (y3, y2, y1)]
            for k1 in range(RADIX):
                re, im = y[k1]
                at = pl.ds(pl.multiple_of(lane * LANES, LANES), LANES)
                if k1 == 0:
                    z_re, z_im = re, jnp.zeros_like(re)
                else:
                    cos = twiddle_ref[k1 : k1 + 1, at]
                    sin = twiddle_ref[RADIX + k1 : RADIX + k1 + 1, at]
                    if im is None:
                        z_re, z_im = re * cos, -re * sin
                    else:
                        z_re, z_im = re * cos + im * sin, im * cos - re * sin
                row = ((k1 // 4) * HALF + s) * 4 * paths + (k1 % 4) * paths
                z_ref[row : row + paths, at] = z_re.astype(jnp.bfloat16)
                at = pl.ds(pl.multiple_of(INNER + lane * LANES, LANES), LANES)
                z_ref[row : row + paths, at] = z_im.astype(jnp.bfloat16)
        return carry

    lax.fori_loop(0, INNER // LANES, block, 0)

    rows = 256

    def product(number, carry):
        at = pl.ds(pl.multiple_of(number * rows, rows), rows)
        out_ref[at, :] = lax.dot_general(
            table_ref[at, :], z_ref[...], NT, preferred_element_type=jnp.float32
        ).astype(jnp.bfloat16)
        return carry

    lax.fori_loop(0, INNER // rows, product, 0)


def spectra(first, first_at, second, second_at, window, twiddle, table):
    paths = first.shape[0]
    width = HALF * FFT_LEN
    lanes = RADIX * HALF * paths
    return pl.pallas_call(
        spectra_kernel,
        grid=(1,),
        out_shape=jax.ShapeDtypeStruct((INNER, lanes), jnp.bfloat16),
        in_specs=[
            pl.BlockSpec((paths, width), lambda i: (0, first_at)),
            pl.BlockSpec((paths, width), lambda i: (0, second_at)),
            pl.BlockSpec(window.shape, lambda i: (0, 0)),
            pl.BlockSpec(twiddle.shape, lambda i: (0, 0)),
            pl.BlockSpec(table.shape, lambda i: (0, 0)),
        ],
        out_specs=pl.BlockSpec((INNER, lanes), lambda i: (0, 0)),
        scratch_shapes=[pltpu.VMEM((lanes, 2 * INNER), jnp.bfloat16)],
        compiler_params=pltpu.CompilerParams(vmem_limit_bytes=48 * 1024 * 1024),
        cost_estimate=pl.CostEstimate(
            flops=2 * INNER * 2 * INNER * lanes, bytes_accessed=9 * 2**20, transcendentals=0
        ),
        name="spectra",
    )(first, second, window, twiddle, table)


def gram_kernel(per_bin, *refs):
    parts = (refs[0:4], refs[4:8])
    place_ref, own_ref, mask_ref, out_ref, g_ref = refs[8:]
    times, rows, _ = parts[0][0].shape
    chans = rows // 2
    group = 8

    @pl.when(pl.program_id(1) == 0)
    def _():
        def regroup(number, carry):
            t_at = pl.ds(number * group, group)
            at = pl.ds(pl.multiple_of(number * group * rows, group * rows), group * rows)
            for half, sources in enumerate(parts):
                for s in range(HALF):
                    lanes = slice(s * LANES, (s + 1) * LANES)
                    left = jnp.concatenate(
                        [r[t_at, :, lanes].reshape(group * rows, LANES) for r in sources], axis=1
                    )
                    moved = jnp.dot(left, place_ref[...], preferred_element_type=jnp.float32)
                    for low in range(4):
                        g_ref[half * HALF + s, low, at, :] = moved[:, low * LANES : (low + 1) * LANES]
            return carry

        lax.fori_loop(0, times // group, regroup, 0)

    per_step = out_ref.shape[0]
    total = times * 2 * HALF
    for step in range(per_step):
        chan = pl.program_id(1) * per_step + step
        for low in range(4):
            re = jnp.concatenate(
                [g_ref[s, low, pl.ds(chan, times, stride=rows), :] for s in range(2 * HALF)], axis=0
            )
            im = jnp.concatenate(
                [g_ref[s, low, pl.ds(chans + chan, times, stride=rows), :] for s in range(2 * HALF)], axis=0
            )
            power = jnp.sum(re * re + im * im, axis=0, keepdims=True)
            equalizer = lax.rsqrt(power / total + 1e-06)
            re = (re * equalizer).astype(jnp.bfloat16)
            im = (im * equalizer).astype(jnp.bfloat16)
            both = jnp.concatenate([re, im], axis=0)
            turned = jnp.concatenate([-im, re], axis=0)
            left = lax.dot_general(own_ref[...], both, NT, preferred_element_type=jnp.float32)
            left = jnp.concatenate([left.astype(jnp.bfloat16)] * NBINS, axis=0) * mask_ref[...]
            right = jnp.concatenate([both, turned], axis=1)
            result = jnp.dot(left, right, preferred_element_type=jnp.float32) * (1.0 / per_bin)
            result = result.astype(jnp.bfloat16)
            shape = (NBINS, own_ref.shape[0], LANES)
            out_ref[step, 0, low, :, 0] = result[:, :LANES].reshape(shape)
            out_ref[step, 0, low, :, 1] = result[:, LANES:].reshape(shape)


def grams(early, late, place, own, mask, per_bin):
    times, rows, lanes = early[0].shape
    chans = rows // 2
    paths = own.shape[0]
    per_step = 2
    block = pl.BlockSpec((times, rows, lanes // 2), lambda i, j: (0, 0, i))
    return pl.pallas_call(
        functools.partial(gram_kernel, per_bin),
        grid=(2, chans // per_step),
        out_shape=jax.ShapeDtypeStruct((chans, 2, 4, NBINS, 2, paths, LANES), jnp.bfloat16),
        in_specs=[block] * 8
        + [
            pl.BlockSpec(place.shape, lambda i, j: (0, 0)),
            pl.BlockSpec(own.shape, lambda i, j: (0, 0)),
            pl.BlockSpec(mask.shape, lambda i, j: (0, 0)),
        ],
        out_specs=pl.BlockSpec(
            (per_step, 1, 4, NBINS, 2, paths, LANES), lambda i, j: (j, i, 0, 0, 0, 0, 0)
        ),
        scratch_shapes=[pltpu.VMEM((2 * HALF, 4, times * rows, LANES), jnp.float32)],
        compiler_params=pltpu.CompilerParams(vmem_limit_bytes=48 * 1024 * 1024),
        cost_estimate=pl.CostEstimate(
            flops=9 * 2**30, bytes_accessed=30 * 2**20, transcendentals=0
        ),
        name="grams",
    )(*early, *late, place, own, mask)


def swapped(x, by):
    return lax.ppermute(x, "pol", [(i, i ^ by) for i in range(4)])


def on_device(voltages, phase_bin):
    paths, samples = voltages.shape
    time_devs = lax.axis_size("tm")
    path_devs = lax.axis_size("pol")
    total = time_devs * 2 * HALF
    width = HALF * FFT_LEN
    halo = lax.ppermute(
        voltages[:, samples - width :], "tm", [(i, i + 1) for i in range(time_devs - 1)]
    )
    window = jnp.asarray(filter_window())
    twiddle = jnp.asarray(twiddles())
    table = jnp.asarray(inner_table(time_devs))

    me = lax.axis_index("pol")
    src = jnp.arange(4 * LANES, dtype=jnp.int32)[:, None]
    dst = jnp.arange(4 * LANES, dtype=jnp.int32)[None, :]
    device = jnp.bitwise_xor(src // LANES, me)
    target = (src % LANES) // paths * LANES + device * paths + src % paths
    place = (target == dst).astype(jnp.bfloat16)
    own = (
        jnp.arange(paths, dtype=jnp.int32)[:, None] + me * paths
        == jnp.arange(LANES, dtype=jnp.int32)[None, :]
    ).astype(jnp.bfloat16)
    labels = phase_bin.reshape(time_devs, 2, HALF)
    labels = jnp.concatenate([labels[:, 1].T.reshape(-1), labels[:, 0].T.reshape(-1)])
    mask = labels[None, :] == jnp.arange(NBINS, dtype=jnp.int32)[:, None]
    mask = jnp.repeat(jnp.concatenate([mask, mask], axis=1), paths, axis=0).astype(jnp.bfloat16)

    def exchanged(x):
        x = x.reshape(time_devs, INNER // time_devs, -1)
        return lax.all_to_all(x, "tm", split_axis=0, concat_axis=0, tiled=True)

    late = exchanged(spectra(voltages, 0, voltages, 1, window, twiddle, table))
    late_z = swapped(late, 2)
    early = exchanged(spectra(halo, 0, voltages, 0, window, twiddle, table))
    early_z = swapped(early, 2)
    late = (late, swapped(late, 1), late_z, swapped(late_z, 1))
    early = (early, swapped(early, 1), early_z, swapped(early_z, 1))
    out = grams(late, early, place, own, mask, total // NBINS)
    return out.reshape(CHANNELS // time_devs, NBINS, 2, paths, paths * path_devs)


def solution(mesh):
    in_specs = (P("pol", "tm"), P())
    out_specs = P("tm", None, None, "pol", None)
    return jax.shard_map(
        on_device, mesh=mesh, in_specs=in_specs, out_specs=out_specs, check_vma=False
    )
```

time: 1490 us -> 217 us (0.15)
  other arithmetic: 613 us -> 0.4 us
  waiting for transfers between devices: 356 us -> 108 us
  blocking collectives: 218 us -> 0 us
  local copies, waits for them, and re-layouts: 167 us -> 5.11 us
  matrix products: 87.2 us -> 0 us
  Pallas kernels: 0 us -> 70.2 us
    another operation x9 -> x0, other arithmetic: 576 us -> none
    psum x1 -> x0, waiting for transfers between devices: 312 us -> none  [on_device(): lax.psum(local_power.astype(jnp.bfloat16), 'tm').astype(jnp.float32)]
    all_to_all x2 -> x0, blocking collectives: 218 us -> none  [the longest x1 186 us: on_device(): return lax.all_to_all(whole, 'pol', split_axis=3, concat_axis=0, tiled=True)]
    dot_general x10 -> x0, matrix products: 87.2 us -> none  [the longest x8 72.7 us: transform(): product = jnp.dot(spectra_rows, table, preferred_element_type=jnp.float32)]
    pallas_call x0 -> x3, Pallas kernels: none -> 70.2 us  [the longest x1 47.7 us: grams(): pl.pallas_call(functools.partial(gram_kernel, per_bin), grid=(2, chans //...]
    ppermute x1 -> x7, waiting for transfers between devices: 0.01 us -> 69.8 us  [the longest x6 59.5 us: swapped(): return lax.ppermute(x, 'pol', [(i, i ^ by) for i in range(4)])]
    all_to_all x5 -> x0, local copies, waits for them, and re-layouts: 47.8 us -> none  [the longest x3 29.7 us: on_device(): lax.all_to_all(split, 'tm', split_axis=3, concat_axis=1, tiled=True)]
    convert_element_type x1 -> x0, local copies, waits for them, and re-layouts: 35.7 us -> none  [bin_grams(): (jnp.stack([real_sum, imag_sum], axis=2) / per_bin).astype(jnp.bfloat16)]
  transfers between devices with their start and end apart: 3 -> 9, of which waited for: 2 -> 6; matrix products, arithmetic and copies ran while one was open for 39% -> 0% of each run, Pallas kernels for 0% -> 10%
where the time goes in v1:
time: 217 us; the launch traced here: 216 us
  waiting for transfers between devices  108 us (50%)
  Pallas kernels  70.2 us (32%)
  starting transfers between devices  32.8 us (15%)
  local copies, waits for them, and re-layouts  5.11 us (2%)
    ppermute x6, waiting for transfers between devices, swapped(): return lax.ppermute(x, 'pol', [(i, i ^ by) for i in range(4)])  59.5 us
    pallas_call x1, Pallas kernels, grams(): pl.pallas_call(functools.partial(gram_kernel, per_bin), grid=(2, chans //...  47.7 us
    all_to_all x2, waiting for transfers between devices, exchanged(): return lax.all_to_all(x, 'tm', split_axis=0, concat_axis=0, tiled=True)  37.8 us
    pallas_call x2, Pallas kernels, spectra(): pl.pallas_call(spectra_kernel, grid=(1,), out_shape=jax.ShapeDtypeStruct(...  22.5 us
    all_to_all x2, starting transfers between devices, exchanged(): return lax.all_to_all(x, 'tm', split_axis=0, concat_axis=0, tiled=True)  18.5 us
    ppermute x1, waiting for transfers between devices, on_device(): lax.ppermute(voltages[:, samples - width:], 'tm', [(i, i + 1) for i in ra...  10.3 us
    ppermute x6, starting transfers between devices, swapped(): return lax.ppermute(x, 'pol', [(i, i ^ by) for i in range(4)])  10.2 us
  transfers between devices with their start and end apart: 9, of which 6 were waited for; matrix products, arithmetic and copies ran while one was open for 0% of the time, Pallas kernels for 10%

profile of v1, /device:TPU:1, one launch (start us, length us, event | category | flops | bytes accessed | tf_op | source)
XLA Modules:
  0.0 216.3 jit_solution(8335333391651715349)
XLA Ops:
  0.0 2.8 %slice.9 = bf16[32,24576]{1,0:T(8,128)(2,1)} slice(bf16[32,49152]{1,0:T(8,128)(2,1)} %second_ref.3), slice={[0:32], [24576:49152]} | slice | bytes 3145728 | tf_op jit(solution)/shard_map/slice | solution.py:220
  2.8 4.0 %collective-permute-start.3 = (bf16[32,24576]{1,0:T(8,128)(2,1)}, bf16[32,24576]{1,0:T(8,128)(2,1)S(1)}, u32[]{:S(2)}, u32[]{:S(2)}) collective-permute-start(bf16[32,24576]{1,0:T(8,128)(2,1)} %slice.9), channel_id=1, source_target_pairs={{0,4},{4,8},{8,12},{12,16},{16,20},{20,24},{24,28},{28,32},{32,36}... | collective-permute-start | bytes 4718600 | tf_op jit(solution)/shard_map/ppermute | solution.py:219
  6.9 0.9 copy-done.1
  7.8 0.8 copy-done.3
  8.6 11.1 %spectra.2 = bf16[1024,768]{1,0:T(8,128)(2,1)} custom-call(bf16[32,49152]{1,0:T(8,128)(2,1)S(1)} %copy-done, bf16[32,49152]{1,0:T(8,128)(2,1)S(1)} %copy-done, f32[4,8192]{1,0:T(4,128)S(1)} %copy-done.1, f32[16,1024]{1,0:T(8,128)S(1)} %copy-done.3, bf16[1024,2048]{1,0:T(8,128)(2,1)} %constant.66.clone.table_ref), custom_call_target="tpu_custom_call" | custom-call | flops 3221225472 | bytes 9437184 | tf_op jit(solution)/shard_map/spectra/pallas_call | solution.py:108
  19.7 10.1 %all-to-all-start = ((bf16[32,32,768]{2,1,0:T(8,128)(2,1)}), bf16[32,32,768]{2,1,0:T(8,128)(2,1)S(1)}, u32[]{:S(2)}, u32[]{:S(2)}) async-start(bf16[32,32,768]{2,1,0:T(8,128)(2,1)} %bitcast), calls=%async_computation | async-start | bytes 3145728 | tf_op jit(solution)/shard_map/all_to_all | solution.py:243
  29.8 10.3 %collective-permute-done.3.first_ref = bf16[32,24576]{1,0:T(8,128)(2,1)S(1)} collective-permute-done((bf16[32,24576]{1,0:T(8,128)(2,1)}, bf16[32,24576]{1,0:T(8,128)(2,1)S(1)}, u32[]{:S(2)}, u32[]{:S(2)}) %collective-permute-start.3) | collective-permute-done | bytes 1572896 | tf_op jit(solution)/shard_map/ppermute | solution.py:219
  40.1 11.4 %spectra.3 = bf16[1024,768]{1,0:T(8,128)(2,1)} custom-call(bf16[32,24576]{1,0:T(8,128)(2,1)S(1)} %collective-permute-done.3.first_ref, bf16[32,49152]{1,0:T(8,128)(2,1)} %second_ref.3, f32[4,8192]{1,0:T(4,128)S(1)} %copy-done.2, f32[16,1024]{1,0:T(8,128)S(1)} %copy-done.4, bf16[1024,2048]{1,0:T(8,128)(2,1)} %constant.66.clone.table_ref), custom_call_target="tpu_custom_call" | custom-call | flops 3221225472 | bytes 9437184 | tf_op jit(solution)/shard_map/spectra/pallas_call | solution.py:108
  51.6 18.1 %all-to-all-done.refs_0_ = bf16[32,32,768]{2,1,0:T(8,128)(2,1)S(1)} async-done(((bf16[32,32,768]{2,1,0:T(8,128)(2,1)}), bf16[32,32,768]{2,1,0:T(8,128)(2,1)S(1)}, u32[]{:S(2)}, u32[]{:S(2)}) %all-to-all-start) | async-done | bytes 1572896 | tf_op jit(solution)/shard_map/all_to_all | solution.py:243
  69.7 8.4 %all-to-all-start.1 = ((bf16[32,32,768]{2,1,0:T(8,128)(2,1)}), bf16[32,32,768]{2,1,0:T(8,128)(2,1)}, u32[]{:S(2)}, u32[]{:S(2)}) async-start(bf16[32,32,768]{2,1,0:T(8,128)(2,1)} %bitcast.1), calls=%async_computation.1 | async-start | bytes 3145728 | tf_op jit(solution)/shard_map/all_to_all | solution.py:243
  78.1 0.2 collective-permute-start.1
  78.3 19.7 %all-to-all-done.1.refs_4_ = bf16[32,32,768]{2,1,0:T(8,128)(2,1)} async-done(((bf16[32,32,768]{2,1,0:T(8,128)(2,1)}), bf16[32,32,768]{2,1,0:T(8,128)(2,1)}, u32[]{:S(2)}, u32[]{:S(2)}) %all-to-all-start.1) | async-done | bytes 1572896 | tf_op jit(solution)/shard_map/all_to_all | solution.py:243
  98.0 5.5 %collective-permute-start = (bf16[32,32,768]{2,1,0:T(8,128)(2,1)S(1)}, bf16[32,32,768]{2,1,0:T(8,128)(2,1)}, u32[]{:S(2)}, u32[]{:S(2)}) collective-permute-start(bf16[32,32,768]{2,1,0:T(8,128)(2,1)S(1)} %all-to-all-done.refs_0_), channel_id=1, source_target_pairs={{0,1},{1,0},{2,3},{3,2},{4,5},{5,4},{6,7},{7,6},{8,9},{9,8},{10,11... | collective-permute-start | bytes 4718600 | tf_op jit(solution)/shard_map/ppermute | solution.py:210
  103.5 26.2 %collective-permute-done.1.refs_2_ = bf16[32,32,768]{2,1,0:T(8,128)(2,1)S(1)} collective-permute-done((bf16[32,32,768]{2,1,0:T(8,128)(2,1)S(1)}, bf16[32,32,768]{2,1,0:T(8,128)(2,1)S(1)}, u32[]{:S(2)}, u32[]{:S(2)}) %collective-permute-start.1) | collective-permute-done | bytes 1572896 | tf_op jit(solution)/shard_map/ppermute | solution.py:210
  129.7 2.9 %collective-permute-start.2 = (bf16[32,32,768]{2,1,0:T(8,128)(2,1)S(1)}, bf16[32,32,768]{2,1,0:T(8,128)(2,1)}, u32[]{:S(2)}, u32[]{:S(2)}) collective-permute-start(bf16[32,32,768]{2,1,0:T(8,128)(2,1)S(1)} %collective-permute-done.1.refs_2_), channel_id=1, source_target_pairs={{0,1},{1,0},{2,3},{3,2},{4,5},{5,4},{6,7},{7,6},{8,9},{9,8},{10,11... | collective-permute-start | bytes 4718600 | tf_op jit(solution)/shard_map/ppermute | solution.py:210
  132.6 30.9 %collective-permute-done.5.refs_6_ = bf16[32,32,768]{2,1,0:T(8,128)(2,1)} collective-permute-done((bf16[32,32,768]{2,1,0:T(8,128)(2,1)}, bf16[32,32,768]{2,1,0:T(8,128)(2,1)}, u32[]{:S(2)}, u32[]{:S(2)}) %collective-permute-start.5) | collective-permute-done | bytes 1572896 | tf_op jit(solution)/shard_map/ppermute | solution.py:210
  163.5 1.6 collective-permute-start.6
  165.1 0.2 reshape.136
  165.4 0.1 reshape.137
  165.6 0.1 reshape.138
  165.7 0.1 pad_add_fusion
  165.9 0.2 fusion.refs_8_
  166.1 2.4 %collective-permute-done.6.refs_7_ = bf16[32,32,768]{2,1,0:T(8,128)(2,1)} collective-permute-done((bf16[32,32,768]{2,1,0:T(8,128)(2,1)}, bf16[32,32,768]{2,1,0:T(8,128)(2,1)}, u32[]{:S(2)}, u32[]{:S(2)}) %collective-permute-start.6) | collective-permute-done | bytes 1572896 | tf_op jit(solution)/shard_map/ppermute | solution.py:210
  168.5 47.7 %grams.1 = bf16[16,2,4,8,2,32,128]{6,5,4,3,2,1,0:T(8,128)(2,1)} custom-call(bf16[32,32,768]{2,1,0:T(8,128)(2,1)S(1)} %all-to-all-done.refs_0_, bf16[32,32,768]{2,1,0:T(8,128)(2,1)} %collective-permute-done.refs_1_, bf16[32,32,768]{2,1,0:T(8,128)(2,1)S(1)} %collective-permute-done.1.refs_2_, bf16[32,32,768]{2,1,0:T(8,128)(2,1)} %collective-permute-done.2.refs_3_, ...), custom_call_target="tpu_custom_call" | custom-call | flops 9663676416 | bytes 31457280 | tf_op jit(solution)/shard_map/grams/pallas_call | solution.py:187
  (24 shorter events, 0.4 us)
Async XLA Ops:
  0.0 6.9 %copy-start = (bf16[32,49152]{1,0:T(8,128)(2,1)S(1)}, bf16[32,49152]{1,0:T(8,128)(2,1)}, u32[]{:S(2)}) copy-start(bf16[32,49152]{1,0:T(8,128)(2,1)} %second_ref.3) | copy-start | bytes 9437188
  2.8 37.3 %collective-permute-start.3 = (bf16[32,24576]{1,0:T(8,128)(2,1)}, bf16[32,24576]{1,0:T(8,128)(2,1)S(1)}, u32[]{:S(2)}, u32[]{:S(2)}) collective-permute-start(bf16[32,24576]{1,0:T(8,128)(2,1)} %slice.9), channel_id=1, source_target_pairs={{0,4},{4,8},{8,12},{12,16},{16,20},{20,24},{24,28},{28,32},{32,36}... | collective-permute-start | bytes 4718600 | tf_op jit(solution)/shard_map/ppermute | solution.py:219
  6.9 0.9 copy-start.1
  7.8 0.8 copy-start.3
  19.7 20.4 %copy-start.2 = (f32[4,8192]{1,0:T(4,128)S(1)}, f32[4,8192]{1,0:T(4,128)}, u32[]{:S(2)}) copy-start(f32[4,8192]{1,0:T(4,128)} %constant.64.clone.window_ref) | copy-start | bytes 393220
  19.7 20.4 %copy-start.4 = (f32[16,1024]{1,0:T(8,128)S(1)}, f32[16,1024]{1,0:T(8,128)}, u32[]{:S(2)}) copy-start(f32[16,1024]{1,0:T(8,128)} %constant.65.clone.twiddle_ref) | copy-start | bytes 196612
  19.7 50.0 %all-to-all-start = ((bf16[32,32,768]{2,1,0:T(8,128)(2,1)}), bf16[32,32,768]{2,1,0:T(8,128)(2,1)S(1)}, u32[]{:S(2)}, u32[]{:S(2)}) async-start(bf16[32,32,768]{2,1,0:T(8,128)(2,1)} %bitcast), calls=%async_computation | async-start | bytes 3145728 | tf_op jit(solution)/shard_map/all_to_all | solution.py:243
  69.7 95.5 %copy-start.5 = (s32[192]{0:T(256)S(1)}, s32[192]{0:T(256)}, u32[]{:S(2)}) copy-start(s32[192]{0:T(256)} %param.6) | copy-start | bytes 2308
  69.7 28.3 %all-to-all-start.1 = ((bf16[32,32,768]{2,1,0:T(8,128)(2,1)}), bf16[32,32,768]{2,1,0:T(8,128)(2,1)}, u32[]{:S(2)}, u32[]{:S(2)}) async-start(bf16[32,32,768]{2,1,0:T(8,128)(2,1)} %bitcast.1), calls=%async_computation.1 | async-start | bytes 3145728 | tf_op jit(solution)/shard_map/all_to_all | solution.py:243
  78.1 51.6 %collective-permute-start.1 = (bf16[32,32,768]{2,1,0:T(8,128)(2,1)S(1)}, bf16[32,32,768]{2,1,0:T(8,128)(2,1)S(1)}, u32[]{:S(2)}, u32[]{:S(2)}) collective-permute-start(bf16[32,32,768]{2,1,0:T(8,128)(2,1)S(1)} %all-to-all-done.refs_0_), channel_id=1, source_target_pairs={{0,2},{1,3},{2,0},{3,1},{4,6},{5,7},{6,4},{7,5},{8,10},{9,11},{10,... | collective-permute-start | bytes 4718600 | tf_op jit(solution)/shard_map/ppermute | solution.py:210
  98.0 65.5 %collective-permute-start.5 = (bf16[32,32,768]{2,1,0:T(8,128)(2,1)}, bf16[32,32,768]{2,1,0:T(8,128)(2,1)}, u32[]{:S(2)}, u32[]{:S(2)}) collective-permute-start(bf16[32,32,768]{2,1,0:T(8,128)(2,1)} %all-to-all-done.1.refs_4_), channel_id=1, source_target_pairs={{0,2},{1,3},{2,0},{3,1},{4,6},{5,7},{6,4},{7,5},{8,10},{9,11},{10,... | collective-permute-start | bytes 4718600 | tf_op jit(solution)/shard_map/ppermute | solution.py:210
  98.0 68.1 %collective-permute-start = (bf16[32,32,768]{2,1,0:T(8,128)(2,1)S(1)}, bf16[32,32,768]{2,1,0:T(8,128)(2,1)}, u32[]{:S(2)}, u32[]{:S(2)}) collective-permute-start(bf16[32,32,768]{2,1,0:T(8,128)(2,1)S(1)} %all-to-all-done.refs_0_), channel_id=1, source_target_pairs={{0,1},{1,0},{2,3},{3,2},{4,5},{5,4},{6,7},{7,6},{8,9},{9,8},{10,11... | collective-permute-start | bytes 4718600 | tf_op jit(solution)/shard_map/ppermute | solution.py:210
  103.5 62.6 %collective-permute-start.4 = (bf16[32,32,768]{2,1,0:T(8,128)(2,1)}, bf16[32,32,768]{2,1,0:T(8,128)(2,1)}, u32[]{:S(2)}, u32[]{:S(2)}) collective-permute-start(bf16[32,32,768]{2,1,0:T(8,128)(2,1)} %all-to-all-done.1.refs_4_), channel_id=1, source_target_pairs={{0,1},{1,0},{2,3},{3,2},{4,5},{5,4},{6,7},{7,6},{8,9},{9,8},{10,11... | collective-permute-start | bytes 4718600 | tf_op jit(solution)/shard_map/ppermute | solution.py:210
  129.7 36.4 %collective-permute-start.2 = (bf16[32,32,768]{2,1,0:T(8,128)(2,1)S(1)}, bf16[32,32,768]{2,1,0:T(8,128)(2,1)}, u32[]{:S(2)}, u32[]{:S(2)}) collective-permute-start(bf16[32,32,768]{2,1,0:T(8,128)(2,1)S(1)} %collective-permute-done.1.refs_2_), channel_id=1, source_target_pairs={{0,1},{1,0},{2,3},{3,2},{4,5},{5,4},{6,7},{7,6},{8,9},{9,8},{10,11... | collective-permute-start | bytes 4718600 | tf_op jit(solution)/shard_map/ppermute | solution.py:210
  163.5 5.0 %collective-permute-start.6 = (bf16[32,32,768]{2,1,0:T(8,128)(2,1)}, bf16[32,32,768]{2,1,0:T(8,128)(2,1)}, u32[]{:S(2)}, u32[]{:S(2)}) collective-permute-start(bf16[32,32,768]{2,1,0:T(8,128)(2,1)} %collective-permute-done.5.refs_6_), channel_id=1, source_target_pairs={{0,1},{1,0},{2,3},{3,2},{4,5},{5,4},{6,7},{7,6},{8,9},{9,8},{10,11... | collective-permute-start | bytes 4718600 | tf_op jit(solution)/shard_map/ppermute | solution.py:210

commit v2 on v1

v2 whole, which is shorter than its diff:
```python
import functools
import math

import jax
import jax.numpy as jnp
import ml_dtypes
import numpy as np
from jax import lax
from jax.experimental import pallas as pl
from jax.experimental.pallas import tpu as pltpu
from jax.sharding import PartitionSpec as P

FFT_LEN = 8192
TAPS = 4
NBINS = 8
CHANNELS = 4096
RADIX = 16
INNER = FFT_LEN // RADIX
LANES = 128
HALF = 3
NT = (((1,), (1,)), ((), ()))


def filter_window():
    length = TAPS * FFT_LEN
    place = np.arange(length, dtype=np.float64)
    center = (place - length / 2 + 0.5) / FFT_LEN
    taper = 0.5 - 0.5 * np.cos(2.0 * math.pi * (place + 0.5) / length)
    return (np.sinc(center) * taper).reshape(TAPS, FFT_LEN).astype(np.float32)


def twiddles():
    angle = 2.0 * math.pi * np.outer(np.arange(RADIX), np.arange(INNER)) / FFT_LEN
    return np.concatenate([np.cos(angle), np.sin(angle)]).astype(np.float32)


def inner_table(time_devs):
    angle = 2.0 * math.pi * (np.outer(np.arange(INNER // 2), np.arange(INNER)) % INNER) / INNER
    real_rows = np.concatenate([np.cos(angle), np.sin(angle)], axis=1)
    imag_rows = np.concatenate([-np.sin(angle), np.cos(angle)], axis=1)
    rows = np.stack([part.reshape(time_devs, -1, 2 * INNER) for part in (real_rows, imag_rows)], axis=1)
    rows = rows.reshape(4, 2, 4, -1).transpose(1, 0, 2, 3)
    return rows.reshape(INNER, 2 * INNER).astype(ml_dtypes.bfloat16)


def real_transform8(f):
    root = math.sqrt(0.5)
    a = [f[n] + f[n + 4] for n in range(4)]
    b = [f[n] - f[n + 4] for n in range(4)]
    low, high = root * (b[1] - b[3]), root * (b[1] + b[3])
    even, odd = a[0] + a[2], a[1] + a[3]
    return [
        (even + odd, None),
        (b[0] + low, -b[2] - high),
        (a[0] - a[2], a[3] - a[1]),
        (b[0] - low, b[2] - high),
        (even - odd, None),
    ]


def real_transform16(f):
    e = real_transform8(f[0::2])
    o = real_transform8(f[1::2])
    y = [None] * 9
    y[0] = (e[0][0] + o[0][0], None)
    y[8] = (e[0][0] - o[0][0], None)
    y[4] = (e[4][0], -o[4][0])
    for k in range(1, 4):
        cos, sin = math.cos(math.pi * k / 8), math.sin(math.pi * k / 8)
        re = o[k][0] * cos + o[k][1] * sin
        im = o[k][1] * cos - o[k][0] * sin
        y[k] = (e[k][0] + re, e[k][1] + im)
        y[8 - k] = (e[k][0] - re, im - e[k][1])
    return y


def spectra_kernel(first_ref, second_ref, window_ref, twiddle_ref, table_ref, side_ref, *refs):
    out_refs, z_ref = refs[:-1], refs[-1]
    paths = first_ref.shape[0]
    strip = 16

    def block(lane, carry):
        for s in range(HALF):
            for top in range(0, paths, strip):
                f = []
                for n1 in range(RADIX):
                    total = None
                    for tap in range(TAPS):
                        number = s + tap
                        source = first_ref if number < HALF else second_ref
                        start = number % HALF * FFT_LEN + n1 * INNER
                        at = pl.ds(pl.multiple_of(start + lane * LANES, LANES), LANES)
                        w_at = pl.ds(pl.multiple_of(n1 * INNER + lane * LANES, LANES), LANES)
                        volts = source[top : top + strip, at].astype(jnp.float32)
                        term = window_ref[tap : tap + 1, w_at] * volts
                        total = term if total is None else total + term
                    f.append(total.astype(jnp.bfloat16).astype(jnp.float32))
                y = real_transform16(f)
                re_at = pl.ds(pl.multiple_of(lane * LANES, LANES), LANES)
                im_at = pl.ds(pl.multiple_of(INNER + lane * LANES, LANES), LANES)
                for k1 in range(RADIX):
                    re, im = y[min(k1, RADIX - k1)]
                    if k1 > RADIX - k1:
                        im = -im
                    if k1 == 0:
                        z_re, z_im = re, jnp.zeros_like(re)
                    else:
                        cos = twiddle_ref[k1 : k1 + 1, re_at]
                        sin = twiddle_ref[RADIX + k1 : RADIX + k1 + 1, re_at]
                        if im is None:
                            z_re, z_im = re * cos, -re * sin
                        else:
                            z_re, z_im = re * cos + im * sin, im * cos - re * sin
                    row = ((k1 // 4) * HALF + s) * 4 * paths + (k1 % 4) * paths + top
                    z_ref[row : row + strip, re_at] = z_re.astype(jnp.bfloat16)
                    z_ref[row : row + strip, im_at] = z_im.astype(jnp.bfloat16)
        return carry

    lax.fori_loop(0, INNER // LANES, block, 0)

    rows = INNER // 2

    def product(number, carry):
        at = pl.ds(pl.multiple_of((number ^ side_ref[0]) * rows, rows), rows)
        result = lax.dot_general(
            table_ref[at, :], z_ref[...], NT, preferred_element_type=jnp.float32
        ).astype(jnp.bfloat16)

        for part, ref in enumerate(out_refs):
            @pl.when(number == part)
            def _():
                ref[...] = result

        return carry

    lax.fori_loop(0, 2, product, 0)


def spectra(first, second, second_at, window, twiddle, table, side):
    paths = first.shape[0]
    lanes = RADIX * HALF * paths
    out = jax.ShapeDtypeStruct((INNER // 2, lanes), jnp.bfloat16)
    return pl.pallas_call(
        spectra_kernel,
        grid=(1,),
        out_shape=[out] * 2,
        in_specs=[
            pl.BlockSpec((paths, HALF * FFT_LEN), lambda i: (0, 0)),
            pl.BlockSpec((paths, HALF * FFT_LEN), lambda i: (0, second_at)),
            pl.BlockSpec(window.shape, lambda i: (0, 0)),
            pl.BlockSpec(twiddle.shape, lambda i: (0, 0)),
            pl.BlockSpec(table.shape, lambda i: (0, 0)),
            pl.BlockSpec(memory_space=pltpu.SMEM),
        ],
        out_specs=[pl.BlockSpec(out.shape, lambda i: (0, 0))] * 2,
        scratch_shapes=[pltpu.VMEM((lanes, 2 * INNER), jnp.bfloat16)],
        compiler_params=pltpu.CompilerParams(vmem_limit_bytes=48 * 1024 * 1024),
        cost_estimate=pl.CostEstimate(
            flops=2**20, bytes_accessed=2**20, transcendentals=0
        ),
        name="spectra",
    )(first, second, window, twiddle, table, side)


def gram_kernel(*refs):
    parts = [refs[4 * n : 4 * n + 4] for n in range(4)]
    place_ref, own_ref, mask_ref, rank_ref = refs[16:20]
    out_ref, g_ref, o_ref = refs[-3:]
    times, rows, width = parts[0][0].shape
    chans = rows // 2
    total = 4 * HALF * times
    groups = width // (HALF * LANES)

    @pl.when(pl.program_id(0) == 0)
    def _():
        def regroup(number, carry):
            s = lax.rem(number, HALF)
            low = number // HALF * 4
            lanes = pl.ds(pl.multiple_of(number * LANES, LANES), LANES)
            left = jnp.concatenate(
                [
                    jnp.concatenate([r[:, :, lanes].reshape(times * rows, LANES) for r in sources], axis=1)
                    for sources in parts
                ],
                axis=0,
            )
            moved = jnp.dot(left, place_ref[...], preferred_element_type=jnp.float32)
            mine = left[:, :LANES].astype(jnp.float32)
            for n in range(len(parts)):
                for t in range(times):
                    rank = rank_ref[(n * HALF + s) * times + t]
                    at = pl.ds(pl.multiple_of(rank * rows, rows), rows)
                    here = slice((n * times + t) * rows, (n * times + t + 1) * rows)
                    o_ref[number // HALF, at, :] = mine[here]
                    for l in range(4):
                        g_ref[low + l, at, :] = moved[here, l * LANES : (l + 1) * LANES]
            return carry

        lax.fori_loop(0, groups * HALF, regroup, 0)

    chan = pl.program_id(0)
    side = total // 2
    paths = LANES // 4
    shape = (NBINS // 2, paths, LANES)

    def scaled(ref, low):
        re = ref[low, pl.ds(chan, total, stride=rows), :]
        im = ref[low, pl.ds(chans + chan, total, stride=rows), :]
        power = jnp.sum(re * re + im * im, axis=0, keepdims=True)
        equalizer = lax.rsqrt(power / total + 1e-06) * math.sqrt(NBINS / total)
        return (re * equalizer).astype(jnp.bfloat16), (im * equalizer).astype(jnp.bfloat16)

    halves = [slice(half * side, (half + 1) * side) for half in range(2)]
    for group in range(groups):
        re, im = scaled(o_ref, group)
        turned_own = [
            lax.dot_general(
                own_ref[...], jnp.concatenate([re[at], im[at]], axis=0), NT, preferred_element_type=jnp.float32
            ).astype(jnp.bfloat16)
            for at in halves
        ]
        for l in range(4):
            low = group * 4 + l
            re, im = scaled(g_ref, low)
            for half, at in enumerate(halves):
                left = turned_own[half][l * paths : (l + 1) * paths]
                left = jnp.concatenate([left] * (NBINS // 2), axis=0) * mask_ref[...]
                both = jnp.concatenate([re[at], im[at]], axis=0)
                turned = jnp.concatenate([-im[at], re[at]], axis=0)
                right = jnp.concatenate([both, turned], axis=1)
                result = jnp.dot(left, right, preferred_element_type=jnp.float32).astype(jnp.bfloat16)
                bins = slice(half * NBINS // 2, (half + 1) * NBINS // 2)
                out_ref[0, low, bins, 0] = result[:, :LANES].reshape(shape)
                out_ref[0, low, bins, 1] = result[:, LANES:].reshape(shape)


def grams(sources, place, own, mask, rank, part, before):
    times, rows, _ = sources[0].shape
    chans = rows // 2
    paths = own.shape[0] // 4
    lanes = RADIX // 2 * HALF * paths
    lows = RADIX // 2

    def block(x):
        at = part if x.shape[2] > lanes else 0
        return pl.BlockSpec((times, rows, lanes), lambda j: (0, 0, at))

    args = (*sources, place, own, mask, rank)
    in_specs = [block(x) for x in sources] + [
        pl.BlockSpec(place.shape, lambda j: (0, 0)),
        pl.BlockSpec(own.shape, lambda j: (0, 0)),
        pl.BlockSpec(mask.shape, lambda j: (0, 0)),
        pl.BlockSpec(memory_space=pltpu.SMEM),
    ]
    aliases = {}
    if before is not None:
        aliases = {len(args): 0}
        args += (before,)
        in_specs.append(pl.BlockSpec(memory_space=pl.ANY))
    return pl.pallas_call(
        gram_kernel,
        grid=(chans,),
        out_shape=jax.ShapeDtypeStruct((chans, RADIX, NBINS, 2, paths, LANES), jnp.bfloat16),
        in_specs=in_specs,
        out_specs=pl.BlockSpec((1, lows, NBINS, 2, paths, LANES), lambda j: (j, part, 0, 0, 0, 0)),
        scratch_shapes=[
            pltpu.VMEM((lows, rank.shape[0] * rows, LANES), jnp.float32),
            pltpu.VMEM((lows // 4, rank.shape[0] * rows, LANES), jnp.float32),
        ],
        input_output_aliases=aliases,
        compiler_params=pltpu.CompilerParams(vmem_limit_bytes=48 * 1024 * 1024),
        cost_estimate=pl.CostEstimate(flops=9 * 2**29, bytes_accessed=15 * 2**20, transcendentals=0),
        name="grams",
    )(*args)


def follows(x, *others):
    return pl.pallas_call(
        lambda *refs: None,
        out_shape=jax.ShapeDtypeStruct(x.shape, x.dtype),
        in_specs=[pl.BlockSpec(memory_space=pl.ANY)] * (1 + len(others)),
        out_specs=pl.BlockSpec(memory_space=pl.ANY),
        input_output_aliases={0: 0},
        cost_estimate=pl.CostEstimate(flops=0, bytes_accessed=0, transcendentals=0),
        name="follows",
    )(x, *others)


def swapped(x, by):
    return lax.ppermute(x, "pol", [(i, i ^ by) for i in range(4)])


def on_device(voltages, phase_bin):
    paths, samples = voltages.shape
    time_devs = lax.axis_size("tm")
    path_devs = lax.axis_size("pol")
    total = time_devs * 2 * HALF
    width = HALF * FFT_LEN
    pairs = [(i, i + 1) for i in range(time_devs - 1)]
    halo = lax.ppermute(voltages[:, samples - width :], "tm", pairs)
    window = jnp.asarray(filter_window())
    twiddle = jnp.asarray(twiddles())
    table = jnp.asarray(inner_table(time_devs))

    me = lax.axis_index("pol")
    src = jnp.arange(4 * LANES, dtype=jnp.int32)[:, None]
    dst = jnp.arange(4 * LANES, dtype=jnp.int32)[None, :]
    device = jnp.bitwise_xor(src // LANES, me)
    target = (src % LANES) // paths * LANES + device * paths + src % paths
    place = (target == dst).astype(jnp.bfloat16)
    own = jnp.eye(LANES, dtype=jnp.bfloat16)
    t_at = lax.axis_index("tm")
    side = t_at // 4 % 2
    labels = phase_bin.reshape(4, 2, 4, 2, HALF)
    labels = jnp.where(side == 0, labels, labels[:, ::-1])[:, :, :, ::-1]
    labels = labels.transpose(3, 1, 4, 0, 2).reshape(-1)
    number = jnp.arange(total, dtype=jnp.int32)
    ahead = (labels[:, None] == labels[None, :]) & (number[:, None] > number[None, :])
    rank = labels * (total // NBINS) + jnp.sum(ahead.astype(jnp.int32), axis=1)
    rank = jnp.clip(rank, 0, total - 1)
    mask = np.arange(NBINS // 2)[:, None] == np.arange(total // 2)[None, :] // (total // NBINS)
    mask = jnp.asarray(np.repeat(np.tile(mask, (1, 2)), paths, axis=0).astype(ml_dtypes.bfloat16))

    groups = [[y * 8 + z * 4 + x for y in range(4) for x in range(4)] for z in range(2)]
    across = []
    for t in range(time_devs):
        for q in range(path_devs):
            across.append((t * path_devs + q, (t ^ 4) * path_devs + (q ^ 2)))

    def exchanged(x):
        x = x.reshape(time_devs // 2, INNER // time_devs, -1)
        return lax.all_to_all(
            x, "tm", split_axis=0, concat_axis=0, axis_index_groups=groups, tiled=True
        )

    def crossed(x):
        return lax.ppermute(x, ("tm", "pol"), across)

    def after(x, *others):
        return lax.optimization_barrier((x, *others))[0]

    def own_set(x, z):
        return (x, swapped(x, 1), z, swapped(z, 1))

    def cross_set(x, z):
        return (z, swapped(z, 1), x, swapped(x, 1))

    side = side.reshape(1).astype(jnp.int32)
    late, late_x = spectra(voltages, voltages, 1, window, twiddle, table, side)
    late_x = crossed(late_x)
    late = exchanged(late)
    late_z = swapped(late, 2)
    late_c = swapped(late, 1)
    late_x = exchanged(after(late_x, late))
    halo = after(halo, late_x)
    early, early_x = spectra(halo, voltages, 0, window, twiddle, table, side)
    late_xz = swapped(late_x, 2)
    late_xc = swapped(late_x, 1)
    late_zc = swapped(late_z, 1)
    early_x = crossed(early_x)
    early = exchanged(after(early, late_z))
    early_z = swapped(early, 2)
    early_x = exchanged(after(early_x, early, late_xz, late_c, late_xc, late_zc))
    half = early_x.shape[2] // 2
    low_z = swapped(after(early_x[:, :, :half], early_z), 2)
    late_xzc = swapped(late_xz, 1)
    early_c = swapped(early, 1)
    early_zc = swapped(early_z, 1)
    early_xc = swapped(early_x, 1)
    high_z = swapped(after(early_x[:, :, half:], low_z), 2)
    common = (late, late_c, late_z, late_zc, late_xz, late_xzc, late_x, late_xc)
    common += (early, early_c, early_z, early_zc)
    low = (low_z, swapped(low_z, 1), early_x, early_xc)
    out = grams(common + low, place, own, mask, rank, 0, None)
    high_z = follows(high_z, out)
    high = (high_z, swapped(high_z, 1), early_x, early_xc)
    out = grams(common + high, place, own, mask, rank, 1, out)
    return out.reshape(CHANNELS // time_devs, NBINS, 2, paths, paths * path_devs)


def solution(mesh):
    in_specs = (P("pol", "tm"), P())
    out_specs = P("tm", None, None, "pol", None)
    return jax.shard_map(
        on_device, mesh=mesh, in_specs=in_specs, out_specs=out_specs, check_vma=False
    )
```

time: 217 us -> 194 us (0.89)
  waiting for transfers between devices: 108 us -> 59 us
  blocking collectives: 0 us -> 37.3 us
  Pallas kernels: 70.2 us -> 52.9 us
  local copies, waits for them, and re-layouts: 5.11 us -> 10 us
    ppermute x6 -> x14, waiting for transfers between devices: 59.5 us -> 15.2 us  [swapped(): return lax.ppermute(x, 'pol', [(i, i ^ by) for i in range(4)])]
    all_to_all x0 -> x1, blocking collectives: none -> 37.3 us  [exchanged(): lax.all_to_all(x, 'tm', split_axis=0, concat_axis=0, axis_index_groups=gr...]
    pallas_call x3 -> x5, Pallas kernels: 70.2 us -> 52.9 us  [the longest x2 38.8 us: grams(): pl.pallas_call(gram_kernel, grid=(chans,), out_shape=jax.ShapeDtypeStruct...]
    all_to_all x2 -> x3, starting transfers between devices: 18.5 us -> 13 us  [exchanged(): lax.all_to_all(x, 'tm', split_axis=0, concat_axis=0, axis_index_groups=gr...]
    ppermute x1 -> x3, starting transfers between devices: 4.03 us -> 9.17 us  [the longest x1 5.13 us: on_device(): halo = lax.ppermute(voltages[:, samples - width:], 'tm', pairs)]
    unnamed x12 -> x34, local copies, waits for them, and re-layouts: 1.75 us -> 5.6 us
    ppermute x1 -> x3, waiting for transfers between devices: 10.3 us -> 7.56 us  [the longest x2 7.56 us: crossed(): return lax.ppermute(x, ('tm', 'pol'), across)]
    all_to_all x2 -> x3, waiting for transfers between devices: 37.8 us -> 36.1 us  [exchanged(): lax.all_to_all(x, 'tm', split_axis=0, concat_axis=0, axis_index_groups=gr...]
  transfers between devices with their start and end apart: 9 -> 20, of which waited for: 6 -> 10; matrix products, arithmetic and copies ran while one was open for 0% -> 1% of each run, Pallas kernels for 10% -> 17%
where the time goes in v2:
time: 194 us
  waiting for transfers between devices  59 us (30%)
  Pallas kernels  52.9 us (27%)
  blocking collectives  37.3 us (19%)
  starting transfers between devices  33.9 us (17%)
  local copies, waits for them, and re-layouts  10 us (5%)
    pallas_call x2, Pallas kernels, grams(): pl.pallas_call(gram_kernel, grid=(chans,), out_shape=jax.ShapeDtypeStruct...  38.8 us
    all_to_all x1, blocking collectives, exchanged(): lax.all_to_all(x, 'tm', split_axis=0, concat_axis=0, axis_index_groups=gr...  37.3 us
    all_to_all x3, waiting for transfers between devices, exchanged(): lax.all_to_all(x, 'tm', split_axis=0, concat_axis=0, axis_index_groups=gr...  36.1 us
    ppermute x14, waiting for transfers between devices, swapped(): return lax.ppermute(x, 'pol', [(i, i ^ by) for i in range(4)])  15.2 us
    pallas_call x2, Pallas kernels, spectra(): pl.pallas_call(spectra_kernel, grid=(1,), out_shape=[out] * 2, in_specs=[...  14.1 us
    all_to_all x3, starting transfers between devices, exchanged(): lax.all_to_all(x, 'tm', split_axis=0, concat_axis=0, axis_index_groups=gr...  13 us
    ppermute x14, starting transfers between devices, swapped(): return lax.ppermute(x, 'pol', [(i, i ^ by) for i in range(4)])  11.7 us
    ppermute x2, waiting for transfers between devices, crossed(): return lax.ppermute(x, ('tm', 'pol'), across)  7.56 us
  transfers between devices with their start and end apart: 20, of which 10 were waited for; matrix products, arithmetic and copies ran while one was open for 1% of the time, Pallas kernels for 17%

profile of v2, /device:TPU:1, one launch (start us, length us, event | category | flops | bytes accessed | tf_op | source)
XLA Modules:
  0.0 193.7 jit_solution(18056702507118136482)
XLA Ops:
  0.0 2.8 %slice.9 = bf16[32,24576]{1,0:T(8,128)(2,1)} slice(bf16[32,49152]{1,0:T(8,128)(2,1)} %second_ref.3), slice={[0:32], [24576:49152]} | slice | bytes 3145728 | tf_op jit(solution)/shard_map/slice | solution.py:300
  2.8 5.1 %collective-permute-start.7 = (bf16[32,24576]{1,0:T(8,128)(2,1)}, bf16[32,24576]{1,0:T(8,128)(2,1)}, u32[]{:S(2)}, u32[]{:S(2)}) collective-permute-start(bf16[32,24576]{1,0:T(8,128)(2,1)} %slice.9), channel_id=1, source_target_pairs={{0,4},{4,8},{8,12},{12,16},{16,20},{20,24},{24,28},{28,32},{32,36}... | collective-permute-start | bytes 4718600 | tf_op jit(solution)/shard_map/ppermute | solution.py:300
  10.1 5.8 %spectra.2 = (bf16[256,1536]{1,0:T(8,128)(2,1)S(1)}, bf16[256,1536]{1,0:T(8,128)(2,1)S(1)}) custom-call(bf16[32,49152]{1,0:T(8,128)(2,1)S(1)} %copy-done, bf16[32,49152]{1,0:T(8,128)(2,1)S(1)} %copy-done, f32[4,8192]{1,0:T(4,128)S(1)} %copy-done.6, f32[32,512]{1,0:T(8,128)S(1)} %copy-done.9, bf16[512,1024]{1,0:T(8,128)(2,1)S(1)} %copy-done.1, s32[1]{0:T(128)} %bitcast.side_ref), custom_call_target="tpu_custom_call" | custom-call | flops 1048576 | bytes 1048576 | tf_op jit(solution)/shard_map/spectra/pallas_call | solution.py:143
  15.9 2.7 %collective-permute-start.3 = (bf16[256,1536]{1,0:T(8,128)(2,1)S(1)}, bf16[256,1536]{1,0:T(8,128)(2,1)}, u32[]{:S(2)}, u32[]{:S(2)}) collective-permute-start(bf16[256,1536]{1,0:T(8,128)(2,1)S(1)} %get-tuple-element.16), channel_id=1, source_target_pairs={{0,18},{1,19},{2,16},{3,17},{4,22},{5,23},{6,20},{7,21},{8,26},{9,... | collective-permute-start | bytes 2359304 | tf_op jit(solution)/shard_map/ppermute | solution.py:337
  18.6 37.3 %all_to_all.20.refs_0_ = bf16[16,16,1536]{2,1,0:T(8,128)(2,1)S(1)} all-to-all(bf16[16,16,1536]{2,1,0:T(8,128)(2,1)S(1)} %bitcast.8), channel_id=1, replica_groups={{0,4,8,12,32,36,40,44,64,68,72,76,96,100,104,108},{16,20,24,28,48,52,56..., dimensions={0} | all-to-all | bytes 1572864 | tf_op jit(solution)/shard_map/all_to_all | solution.py:332
  56.4 6.4 %collective-permute-done.3 = bf16[256,1536]{1,0:T(8,128)(2,1)} collective-permute-done((bf16[256,1536]{1,0:T(8,128)(2,1)S(1)}, bf16[256,1536]{1,0:T(8,128)(2,1)}, u32[]{:S(2)}, u32[]{:S(2)}) %collective-permute-start.3) | collective-permute-done | bytes 786464 | tf_op jit(solution)/shard_map/ppermute | solution.py:337
  62.9 5.1 %all-to-all-start.1 = ((bf16[16,16,1536]{2,1,0:T(8,128)(2,1)}), bf16[16,16,1536]{2,1,0:T(8,128)(2,1)}, u32[]{:S(2)}, u32[]{:S(2)}) async-start(bf16[16,16,1536]{2,1,0:T(8,128)(2,1)} %bitcast.2), calls=%async_computation.1 | async-start | bytes 1572864 | tf_op jit(solution)/shard_map/all_to_all | solution.py:332
  68.9 12.6 %all-to-all-done.1.refs_6_ = bf16[16,16,1536]{2,1,0:T(8,128)(2,1)} async-done(((bf16[16,16,1536]{2,1,0:T(8,128)(2,1)}), bf16[16,16,1536]{2,1,0:T(8,128)(2,1)}, u32[]{:S(2)}, u32[]{:S(2)}) %all-to-all-start.1) | async-done | bytes 786464 | tf_op jit(solution)/shard_map/all_to_all | solution.py:332
  81.4 2.0 %collective-permute-start.6 = (bf16[16,16,1536]{2,1,0:T(8,128)(2,1)}, bf16[16,16,1536]{2,1,0:T(8,128)(2,1)}, u32[]{:S(2)}, u32[]{:S(2)}) collective-permute-start(bf16[16,16,1536]{2,1,0:T(8,128)(2,1)} %all-to-all-done.1.refs_6_), channel_id=1, source_target_pairs={{0,1},{1,0},{2,3},{3,2},{4,5},{5,4},{6,7},{7,6},{8,9},{9,8},{10,11... | collective-permute-start | bytes 2359304 | tf_op jit(solution)/shard_map/ppermute | solution.py:290
  83.5 1.6 collective-permute-start.4
  86.3 8.3 %spectra.3 = (bf16[256,1536]{1,0:T(8,128)(2,1)S(1)}, bf16[256,1536]{1,0:T(8,128)(2,1)}) custom-call(bf16[32,24576]{1,0:T(8,128)(2,1)} %collective-permute-done.7.first_ref, bf16[32,49152]{1,0:T(8,128)(2,1)} %second_ref.3, f32[4,8192]{1,0:T(4,128)S(1)} %copy-done.7, f32[32,512]{1,0:T(8,128)S(1)} %copy-done.10, bf16[512,1024]{1,0:T(8,128)(2,1)S(1)} %copy-done.2, ...), custom_call_target="tpu_custom_call" | custom-call | flops 1048576 | bytes 1048576 | tf_op jit(solution)/shard_map/spectra/pallas_call | solution.py:143
  94.6 1.3 collective-permute-start.11
  95.9 4.3 %all-to-all-start.2 = ((bf16[16,16,1536]{2,1,0:T(8,128)(2,1)}), bf16[16,16,1536]{2,1,0:T(8,128)(2,1)}, u32[]{:S(2)}, u32[]{:S(2)}) async-start(bf16[16,16,1536]{2,1,0:T(8,128)(2,1)} %bitcast.7), calls=%async_computation.2 | async-start | bytes 1572864 | tf_op jit(solution)/shard_map/all_to_all | solution.py:332
  100.3 3.0 %collective-permute-done.4.refs_4_ = bf16[16,16,1536]{2,1,0:T(8,128)(2,1)} collective-permute-done((bf16[16,16,1536]{2,1,0:T(8,128)(2,1)}, bf16[16,16,1536]{2,1,0:T(8,128)(2,1)}, u32[]{:S(2)}, u32[]{:S(2)}) %collective-permute-start.4) | collective-permute-done | bytes 786464 | tf_op jit(solution)/shard_map/ppermute | solution.py:290
  103.2 10.7 %all-to-all-done.2.refs_8_ = bf16[16,16,1536]{2,1,0:T(8,128)(2,1)} async-done(((bf16[16,16,1536]{2,1,0:T(8,128)(2,1)}), bf16[16,16,1536]{2,1,0:T(8,128)(2,1)}, u32[]{:S(2)}, u32[]{:S(2)}) %all-to-all-start.2) | async-done | bytes 786464 | tf_op jit(solution)/shard_map/all_to_all | solution.py:332
  115.9 3.6 %all-to-all-start.3 = ((bf16[16,16,1536]{2,1,0:T(8,128)(2,1)}), bf16[16,16,1536]{2,1,0:T(8,128)(2,1)S(1)}, u32[]{:S(2)}, u32[]{:S(2)}) async-start(bf16[16,16,1536]{2,1,0:T(8,128)(2,1)} %bitcast.9), calls=%async_computation.3 | async-start | bytes 1572864 | tf_op jit(solution)/shard_map/all_to_all | solution.py:332
  119.8 12.9 %all-to-all-done.3.refs_14_ = bf16[16,16,1536]{2,1,0:T(8,128)(2,1)S(1)} async-done(((bf16[16,16,1536]{2,1,0:T(8,128)(2,1)}), bf16[16,16,1536]{2,1,0:T(8,128)(2,1)S(1)}, u32[]{:S(2)}, u32[]{:S(2)}) %all-to-all-start.3) | async-done | bytes 786464 | tf_op jit(solution)/shard_map/all_to_all | solution.py:332
  133.8 4.3 %collective-permute-done.9.refs_10_ = bf16[16,16,1536]{2,1,0:T(8,128)(2,1)} collective-permute-done((bf16[16,16,1536]{2,1,0:T(8,128)(2,1)}, bf16[16,16,1536]{2,1,0:T(8,128)(2,1)}, u32[]{:S(2)}, u32[]{:S(2)}) %collective-permute-start.9) | collective-permute-done | bytes 786464 | tf_op jit(solution)/shard_map/ppermute | solution.py:290
  138.5 2.2 %collective-permute-start.5 = (bf16[16,16,1536]{2,1,0:T(8,128)(2,1)}, bf16[16,16,1536]{2,1,0:T(8,128)(2,1)S(1)}, u32[]{:S(2)}, u32[]{:S(2)}) collective-permute-start(bf16[16,16,1536]{2,1,0:T(8,128)(2,1)} %collective-permute-done.4.refs_4_), channel_id=1, source_target_pairs={{0,1},{1,0},{2,3},{3,2},{4,5},{5,4},{6,7},{7,6},{8,9},{9,8},{10,11... | collective-permute-start | bytes 2359304 | tf_op jit(solution)/shard_map/ppermute | solution.py:290
  141.5 5.5 %collective-permute-done.12.refs_12_ = bf16[16,16,768]{2,1,0:T(8,128)(2,1)S(1)} collective-permute-done((bf16[16,16,768]{2,1,0:T(8,128)(2,1)}, bf16[16,16,768]{2,1,0:T(8,128)(2,1)S(1)}, u32[]{:S(2)}, u32[]{:S(2)}) %collective-permute-start.12) | collective-permute-done | bytes 393248 | tf_op jit(solution)/shard_map/ppermute | solution.py:290
  147.0 2.8 %collective-permute-start.14 = (bf16[16,16,768]{2,1,0:T(8,128)(2,1)S(1)}, bf16[16,16,768]{2,1,0:T(8,128)(2,1)S(1)}, u32[]{:S(2)}, u32[]{:S(2)}) collective-permute-start(bf16[16,16,768]{2,1,0:T(8,128)(2,1)S(1)} %collective-permute-done.12.refs_12_), channel_id=1, source_target_pairs={{0,1},{1,0},{2,3},{3,2},{4,5},{5,4},{6,7},{7,6},{8,9},{9,8},{10,11... | collective-permute-start | bytes 1179656 | tf_op jit(solution)/shard_map/ppermute | solution.py:290
  151.7 19.3 %grams.2.refs_1_.refs_20_ = bf16[8,16,8,2,32,128]{5,4,3,2,1,0:T(8,128)(2,1)} custom-call(bf16[16,16,1536]{2,1,0:T(8,128)(2,1)S(1)} %all_to_all.20.refs_0_, bf16[16,16,1536]{2,1,0:T(8,128)(2,1)S(1)} %collective-permute-done.refs_1_, bf16[16,16,1536]{2,1,0:T(8,128)(2,1)S(1)} %collective-permute-done.1.refs_2_, ...), custom_call_target="tpu_custom_call" | custom-call | flops 4831838208 | bytes 15728640 | tf_op jit(solution)/shard_map/grams/pallas_call | solution.py:260
  171.4 1.6 collective-permute-done.16.refs_13_
  174.2 19.5 %grams.3 = bf16[8,16,8,2,32,128]{5,4,3,2,1,0:T(8,128)(2,1)} custom-call(bf16[16,16,1536]{2,1,0:T(8,128)(2,1)S(1)} %all_to_all.20.refs_0_, bf16[16,16,1536]{2,1,0:T(8,128)(2,1)S(1)} %collective-permute-done.refs_1_, bf16[16,16,1536]{2,1,0:T(8,128)(2,1)S(1)} %collective-permute-done.1.refs_2_, ...), custom_call_target="tpu_custom_call", output_to_operand_aliasing={{}: (20, {})} | custom-call | flops 4831838208 | bytes 15728640 | tf_op jit(solution)/shard_map/grams/pallas_call | solution.py:260
  (68 shorter events, 12.6 us)
Async XLA Ops:
  2.8 82.6 %collective-permute-start.7 = (bf16[32,24576]{1,0:T(8,128)(2,1)}, bf16[32,24576]{1,0:T(8,128)(2,1)}, u32[]{:S(2)}, u32[]{:S(2)}) collective-permute-start(bf16[32,24576]{1,0:T(8,128)(2,1)} %slice.9), channel_id=1, source_target_pairs={{0,4},{4,8},{8,12},{12,16},{16,20},{20,24},{24,28},{28,32},{32,36}... | collective-permute-start | bytes 4718600 | tf_op jit(solution)/shard_map/ppermute | solution.py:300
  15.9 69.5 %copy-start.2 = (bf16[512,1024]{1,0:T(8,128)(2,1)S(1)}, bf16[512,1024]{1,0:T(8,128)(2,1)}, u32[]{:S(2)}) copy-start(bf16[512,1024]{1,0:T(8,128)(2,1)} %constant.101.clone.table_ref) | copy-start | bytes 3145732
  15.9 69.5 %copy-start.7 = (f32[4,8192]{1,0:T(4,128)S(1)}, f32[4,8192]{1,0:T(4,128)}, u32[]{:S(2)}) copy-start(f32[4,8192]{1,0:T(4,128)} %constant.99.clone.window_ref) | copy-start | bytes 393220
  15.9 47.0 %collective-permute-start.3 = (bf16[256,1536]{1,0:T(8,128)(2,1)S(1)}, bf16[256,1536]{1,0:T(8,128)(2,1)}, u32[]{:S(2)}, u32[]{:S(2)}) collective-permute-start(bf16[256,1536]{1,0:T(8,128)(2,1)S(1)} %get-tuple-element.16), channel_id=1, source_target_pairs={{0,18},{1,19},{2,16},{3,17},{4,22},{5,23},{6,20},{7,21},{8,26},{9,... | collective-permute-start | bytes 2359304 | tf_op jit(solution)/shard_map/ppermute | solution.py:337
  55.9 29.2 %collective-permute-start.1 = (bf16[16,16,1536]{2,1,0:T(8,128)(2,1)S(1)}, bf16[16,16,1536]{2,1,0:T(8,128)(2,1)S(1)}, u32[]{:S(2)}, u32[]{:S(2)}) collective-permute-start(bf16[16,16,1536]{2,1,0:T(8,128)(2,1)S(1)} %all_to_all.20.refs_0_), channel_id=1, source_target_pairs={{0,2},{1,3},{2,0},{3,1},{4,6},{5,7},{6,4},{7,5},{8,10},{9,11},{10,... | collective-permute-start | bytes 2359304 | tf_op jit(solution)/shard_map/ppermute | solution.py:290
  62.9 56.8 %copy-start.16 = (s32[192]{0:T(256)S(1)}, s32[192]{0:T(256)}, u32[]{:S(2)}) copy-start(s32[192]{0:T(256)} %param.7) | copy-start | bytes 2308
  62.9 18.6 %all-to-all-start.1 = ((bf16[16,16,1536]{2,1,0:T(8,128)(2,1)}), bf16[16,16,1536]{2,1,0:T(8,128)(2,1)}, u32[]{:S(2)}, u32[]{:S(2)}) async-start(bf16[16,16,1536]{2,1,0:T(8,128)(2,1)} %bitcast.2), calls=%async_computation.1 | async-start | bytes 1572864 | tf_op jit(solution)/shard_map/all_to_all | solution.py:332
  68.0 32.2 %collective-permute-start = (bf16[16,16,1536]{2,1,0:T(8,128)(2,1)S(1)}, bf16[16,16,1536]{2,1,0:T(8,128)(2,1)S(1)}, u32[]{:S(2)}, u32[]{:S(2)}) collective-permute-start(bf16[16,16,1536]{2,1,0:T(8,128)(2,1)S(1)} %all_to_all.20.refs_0_), channel_id=1, source_target_pairs={{0,1},{1,0},{2,3},{3,2},{4,5},{5,4},{6,7},{7,6},{8,9},{9,8},{10,11... | collective-permute-start | bytes 2359304 | tf_op jit(solution)/shard_map/ppermute | solution.py:290
  81.4 18.8 %collective-permute-start.6 = (bf16[16,16,1536]{2,1,0:T(8,128)(2,1)}, bf16[16,16,1536]{2,1,0:T(8,128)(2,1)}, u32[]{:S(2)}, u32[]{:S(2)}) collective-permute-start(bf16[16,16,1536]{2,1,0:T(8,128)(2,1)} %all-to-all-done.1.refs_6_), channel_id=1, source_target_pairs={{0,1},{1,0},{2,3},{3,2},{4,5},{5,4},{6,7},{7,6},{8,9},{9,8},{10,11... | collective-permute-start | bytes 2359304 | tf_op jit(solution)/shard_map/ppermute | solution.py:290
  83.5 19.8 %collective-permute-start.4 = (bf16[16,16,1536]{2,1,0:T(8,128)(2,1)}, bf16[16,16,1536]{2,1,0:T(8,128)(2,1)}, u32[]{:S(2)}, u32[]{:S(2)}) collective-permute-start(bf16[16,16,1536]{2,1,0:T(8,128)(2,1)} %all-to-all-done.1.refs_6_), channel_id=1, source_target_pairs={{0,2},{1,3},{2,0},{3,1},{4,6},{5,7},{6,4},{7,5},{8,10},{9,11},{10,... | collective-permute-start | bytes 2359304 | tf_op jit(solution)/shard_map/ppermute | solution.py:290
  85.1 15.1 %collective-permute-start.2 = (bf16[16,16,1536]{2,1,0:T(8,128)(2,1)S(1)}, bf16[16,16,1536]{2,1,0:T(8,128)(2,1)}, u32[]{:S(2)}, u32[]{:S(2)}) collective-permute-start(bf16[16,16,1536]{2,1,0:T(8,128)(2,1)S(1)} %collective-permute-done.1.refs_2_), channel_id=1, source_target_pairs={{0,1},{1,0},{2,3},{3,2},{4,5},{5,4},{6,7},{7,6},{8,9},{9,8},{10,11... | collective-permute-start | bytes 2359304 | tf_op jit(solution)/shard_map/ppermute | solution.py:290
  94.6 57.1 %copy-start.8 = (bf16[128,192]{1,0:T(8,128)(2,1)S(1)}, bf16[128,192]{1,0:T(8,128)(2,1)}, u32[]{:S(2)}) copy-start(bf16[128,192]{1,0:T(8,128)(2,1)} %constant.102.clone.refs_18_) | copy-start | bytes 147460
  94.6 20.4 %collective-permute-start.11 = (bf16[256,1536]{1,0:T(8,128)(2,1)}, bf16[256,1536]{1,0:T(8,128)(2,1)S(1)}, u32[]{:S(2)}, u32[]{:S(2)}) collective-permute-start(bf16[256,1536]{1,0:T(8,128)(2,1)} %get-tuple-element.21), channel_id=1, source_target_pairs={{0,18},{1,19},{2,16},{3,17},{4,22},{5,23},{6,20},{7,21},{8,26},{9,... | collective-permute-start | bytes 2359304 | tf_op jit(solution)/shard_map/ppermute | solution.py:337
  95.9 18.0 %all-to-all-start.2 = ((bf16[16,16,1536]{2,1,0:T(8,128)(2,1)}), bf16[16,16,1536]{2,1,0:T(8,128)(2,1)}, u32[]{:S(2)}, u32[]{:S(2)}) async-start(bf16[16,16,1536]{2,1,0:T(8,128)(2,1)} %bitcast.7), calls=%async_computation.2 | async-start | bytes 1572864 | tf_op jit(solution)/shard_map/all_to_all | solution.py:332
  115.9 16.8 %all-to-all-start.3 = ((bf16[16,16,1536]{2,1,0:T(8,128)(2,1)}), bf16[16,16,1536]{2,1,0:T(8,128)(2,1)S(1)}, u32[]{:S(2)}, u32[]{:S(2)}) async-start(bf16[16,16,1536]{2,1,0:T(8,128)(2,1)} %bitcast.9), calls=%async_computation.3 | async-start | bytes 1572864 | tf_op jit(solution)/shard_map/all_to_all | solution.py:332
  119.5 18.5 %collective-permute-start.9 = (bf16[16,16,1536]{2,1,0:T(8,128)(2,1)}, bf16[16,16,1536]{2,1,0:T(8,128)(2,1)}, u32[]{:S(2)}, u32[]{:S(2)}) collective-permute-start(bf16[16,16,1536]{2,1,0:T(8,128)(2,1)} %all-to-all-done.2.refs_8_), channel_id=1, source_target_pairs={{0,2},{1,3},{2,0},{3,1},{4,6},{5,7},{6,4},{7,5},{8,10},{9,11},{10,... | collective-permute-start | bytes 2359304 | tf_op jit(solution)/shard_map/ppermute | solution.py:290
  138.1 9.0 %collective-permute-start.12 = (bf16[16,16,768]{2,1,0:T(8,128)(2,1)}, bf16[16,16,768]{2,1,0:T(8,128)(2,1)S(1)}, u32[]{:S(2)}, u32[]{:S(2)}) collective-permute-start(bf16[16,16,768]{2,1,0:T(8,128)(2,1)} %get-tuple-element.23), channel_id=1, source_target_pairs={{0,2},{1,3},{2,0},{3,1},{4,6},{5,7},{6,4},{7,5},{8,10},{9,11},{10,... | collective-permute-start | bytes 1179656 | tf_op jit(solution)/shard_map/ppermute | solution.py:290
  138.5 11.5 %collective-permute-start.5 = (bf16[16,16,1536]{2,1,0:T(8,128)(2,1)}, bf16[16,16,1536]{2,1,0:T(8,128)(2,1)S(1)}, u32[]{:S(2)}, u32[]{:S(2)}) collective-permute-start(bf16[16,16,1536]{2,1,0:T(8,128)(2,1)} %collective-permute-done.4.refs_4_), channel_id=1, source_target_pairs={{0,1},{1,0},{2,3},{3,2},{4,5},{5,4},{6,7},{7,6},{8,9},{9,8},{10,11... | collective-permute-start | bytes 2359304 | tf_op jit(solution)/shard_map/ppermute | solution.py:290
  140.7 9.6 %collective-permute-start.8 = (bf16[16,16,1536]{2,1,0:T(8,128)(2,1)}, bf16[16,16,1536]{2,1,0:T(8,128)(2,1)S(1)}, u32[]{:S(2)}, u32[]{:S(2)}) collective-permute-start(bf16[16,16,1536]{2,1,0:T(8,128)(2,1)} %all-to-all-done.2.refs_8_), channel_id=1, source_target_pairs={{0,1},{1,0},{2,3},{3,2},{4,5},{5,4},{6,7},{7,6},{8,9},{9,8},{10,11... | collective-permute-start | bytes 2359304 | tf_op jit(solution)/shard_map/ppermute | solution.py:290
  140.8 9.5 %collective-permute-start.10 = (bf16[16,16,1536]{2,1,0:T(8,128)(2,1)}, bf16[16,16,1536]{2,1,0:T(8,128)(2,1)S(1)}, u32[]{:S(2)}, u32[]{:S(2)}) collective-permute-start(bf16[16,16,1536]{2,1,0:T(8,128)(2,1)} %collective-permute-done.9.refs_10_), channel_id=1, source_target_pairs={{0,1},{1,0},{2,3},{3,2},{4,5},{5,4},{6,7},{7,6},{8,9},{9,8},{10,11... | collective-permute-start | bytes 2359304 | tf_op jit(solution)/shard_map/ppermute | solution.py:290
  141.2 9.1 %collective-permute-start.15 = (bf16[16,16,1536]{2,1,0:T(8,128)(2,1)}, bf16[16,16,1536]{2,1,0:T(8,128)(2,1)S(1)}, u32[]{:S(2)}, u32[]{:S(2)}) collective-permute-start(bf16[16,16,1536]{2,1,0:T(8,128)(2,1)} %copy-done.11), channel_id=1, source_target_pairs={{0,1},{1,0},{2,3},{3,2},{4,5},{5,4},{6,7},{7,6},{8,9},{9,8},{10,11... | collective-permute-start | bytes 2359304 | tf_op jit(solution)/shard_map/ppermute | solution.py:290
  147.0 4.1 %collective-permute-start.14 = (bf16[16,16,768]{2,1,0:T(8,128)(2,1)S(1)}, bf16[16,16,768]{2,1,0:T(8,128)(2,1)S(1)}, u32[]{:S(2)}, u32[]{:S(2)}) collective-permute-start(bf16[16,16,768]{2,1,0:T(8,128)(2,1)S(1)} %collective-permute-done.12.refs_12_), channel_id=1, source_target_pairs={{0,1},{1,0},{2,3},{3,2},{4,5},{5,4},{6,7},{7,6},{8,9},{9,8},{10,11... | collective-permute-start | bytes 1179656 | tf_op jit(solution)/shard_map/ppermute | solution.py:290
  150.0 21.0 %collective-permute-start.13 = (bf16[16,16,768]{2,1,0:T(8,128)(2,1)}, bf16[16,16,768]{2,1,0:T(8,128)(2,1)}, u32[]{:S(2)}, u32[]{:S(2)}) collective-permute-start(bf16[16,16,768]{2,1,0:T(8,128)(2,1)} %get-tuple-element.24), channel_id=1, source_target_pairs={{0,2},{1,3},{2,0},{3,1},{4,6},{5,7},{6,4},{7,5},{8,10},{9,11},{10,... | collective-permute-start | bytes 1179656 | tf_op jit(solution)/shard_map/ppermute | solution.py:290
  171.1 2.0 %collective-permute-start.16 = (bf16[16,16,768]{2,1,0:T(8,128)(2,1)}, bf16[16,16,768]{2,1,0:T(8,128)(2,1)S(1)}, u32[]{:S(2)}, u32[]{:S(2)}) collective-permute-start(bf16[16,16,768]{2,1,0:T(8,128)(2,1)} %follows.1.refs_12_), channel_id=1, source_target_pairs={{0,1},{1,0},{2,3},{3,2},{4,5},{5,4},{6,7},{7,6},{8,9},{9,8},{10,11... | collective-permute-start | bytes 1179656 | tf_op jit(solution)/shard_map/ppermute | solution.py:290
  (13 other events, 52.0 us)

commit v3 on v2

--- a/solution.py
+++ b/solution.py
@@ -17,6 +17,7 @@
 RADIX = 16
 INNER = FFT_LEN // RADIX
 LANES = 128
+VMEM_BYTES = 60 * 1024 * 1024
 HALF = 3
 NT = (((1,), (1,)), ((), ()))
 
@@ -74,24 +75,22 @@
     return y
 
 
-def spectra_kernel(first_ref, second_ref, window_ref, twiddle_ref, table_ref, side_ref, *refs):
+def spectra_kernel(spectra_taps, outs, volts_ref, window_ref, twiddle_ref, table_ref, side_ref, *refs):
     out_refs, z_ref = refs[:-1], refs[-1]
-    paths = first_ref.shape[0]
+    paths = volts_ref.shape[0]
     strip = 16
 
     def block(lane, carry):
-        for s in range(HALF):
+        for s, taps in enumerate(spectra_taps):
             for top in range(0, paths, strip):
                 f = []
                 for n1 in range(RADIX):
                     total = None
-                    for tap in range(TAPS):
-                        number = s + tap
-                        source = first_ref if number < HALF else second_ref
-                        start = number % HALF * FFT_LEN + n1 * INNER
+                    for tap, number in taps:
+                        start = number * FFT_LEN + n1 * INNER
                         at = pl.ds(pl.multiple_of(start + lane * LANES, LANES), LANES)
                         w_at = pl.ds(pl.multiple_of(n1 * INNER + lane * LANES, LANES), LANES)
-                        volts = source[top : top + strip, at].astype(jnp.float32)
+                        volts = volts_ref[top : top + strip, at].astype(jnp.float32)
                         term = window_ref[tap : tap + 1, w_at] * volts
                         total = term if total is None else total + term
                     f.append(total.astype(jnp.bfloat16).astype(jnp.float32))
@@ -111,7 +110,8 @@
                             z_re, z_im = re * cos, -re * sin
                         else:
                             z_re, z_im = re * cos + im * sin, im * cos - re * sin
-                    row = ((k1 // 4) * HALF + s) * 4 * paths + (k1 % 4) * paths + top
+                    row = ((s // HALF * (RADIX // 4) + k1 // 4) * HALF + s % HALF) * 4 * paths
+                    row += (k1 % 4) * paths + top
                     z_ref[row : row + strip, re_at] = z_re.astype(jnp.bfloat16)
                     z_ref[row : row + strip, im_at] = z_im.astype(jnp.bfloat16)
         return carry
@@ -126,44 +126,37 @@
             table_ref[at, :], z_ref[...], NT, preferred_element_type=jnp.float32
         ).astype(jnp.bfloat16)
 
-        for part, ref in enumerate(out_refs):
+        for (part, start), ref in zip(outs, out_refs):
             @pl.when(number == part)
             def _():
-                ref[...] = result
+                ref[...] = result[:, start : start + ref.shape[1]]
 
         return carry
 
     lax.fori_loop(0, 2, product, 0)
 
 
-def spectra(first, second, second_at, window, twiddle, table, side):
-    paths = first.shape[0]
-    lanes = RADIX * HALF * paths
-    out = jax.ShapeDtypeStruct((INNER // 2, lanes), jnp.bfloat16)
+def spectra(volts, window, twiddle, table, side, spectra_taps, outs):
+    paths = volts.shape[0]
+    lanes = RADIX * len(spectra_taps) * paths
+    out = [jax.ShapeDtypeStruct((INNER // 2, count), jnp.bfloat16) for _, _, count in outs]
+    whole = lambda x: pl.BlockSpec(x.shape, lambda i: (0, 0))
     return pl.pallas_call(
-        spectra_kernel,
+        functools.partial(spectra_kernel, spectra_taps, [o[:2] for o in outs]),
         grid=(1,),
-        out_shape=[out] * 2,
-        in_specs=[
-            pl.BlockSpec((paths, HALF * FFT_LEN), lambda i: (0, 0)),
-            pl.BlockSpec((paths, HALF * FFT_LEN), lambda i: (0, second_at)),
-            pl.BlockSpec(window.shape, lambda i: (0, 0)),
-            pl.BlockSpec(twiddle.shape, lambda i: (0, 0)),
-            pl.BlockSpec(table.shape, lambda i: (0, 0)),
-            pl.BlockSpec(memory_space=pltpu.SMEM),
-        ],
-        out_specs=[pl.BlockSpec(out.shape, lambda i: (0, 0))] * 2,
+        out_shape=out,
+        in_specs=[whole(x) for x in (volts, window, twiddle, table)] + [pl.BlockSpec(memory_space=pltpu.SMEM)],
+        out_specs=[whole(x) for x in out],
         scratch_shapes=[pltpu.VMEM((lanes, 2 * INNER), jnp.bfloat16)],
-        compiler_params=pltpu.CompilerParams(vmem_limit_bytes=48 * 1024 * 1024),
-        cost_estimate=pl.CostEstimate(
-            flops=2**20, bytes_accessed=2**20, transcendentals=0
-        ),
+        compiler_params=pltpu.CompilerParams(vmem_limit_bytes=VMEM_BYTES),
+        cost_estimate=pl.CostEstimate(flops=2**20, bytes_accessed=20 * 2**20, transcendentals=0),
         name="spectra",
-    )(first, second, window, twiddle, table, side)
+    )(volts, window, twiddle, table, side)
 
 
 def gram_kernel(*refs):
     parts = [refs[4 * n : 4 * n + 4] for n in range(4)]
+    carries = (None, None, parts[3], parts[2])
     place_ref, own_ref, mask_ref, rank_ref = refs[16:20]
     out_ref, g_ref, o_ref = refs[-3:]
     times, rows, width = parts[0][0].shape
@@ -177,13 +170,18 @@
             s = lax.rem(number, HALF)
             low = number // HALF * 4
             lanes = pl.ds(pl.multiple_of(number * LANES, LANES), LANES)
-            left = jnp.concatenate(
-                [
-                    jnp.concatenate([r[:, :, lanes].reshape(times * rows, LANES) for r in sources], axis=1)
-                    for sources in parts
-                ],
-                axis=0,
-            )
+            left = []
+            for sources, extra in zip(parts, carries):
+                pieces = []
+                for e, ref in enumerate(sources):
+                    piece = ref[:times, :, lanes]
+                    if extra is not None:
+                        piece = piece.reshape(times // 4, 4, rows, LANES)
+                        first = piece[:, :1] + extra[e][times:, :, lanes].reshape(times // 4, 1, rows, LANES)
+                        piece = jnp.concatenate([first, piece[:, 1:]], axis=1)
+                    pieces.append(piece.reshape(times * rows, LANES))
+                left.append(jnp.concatenate(pieces, axis=1))
+            left = jnp.concatenate(left, axis=0)
             moved = jnp.dot(left, place_ref[...], preferred_element_type=jnp.float32)
             mine = left[:, :LANES].astype(jnp.float32)
             for n in range(len(parts)):
@@ -243,7 +241,7 @@
 
     def block(x):
         at = part if x.shape[2] > lanes else 0
-        return pl.BlockSpec((times, rows, lanes), lambda j: (0, 0, at))
+        return pl.BlockSpec((x.shape[0], rows, lanes), lambda j: (0, 0, at))
 
     args = (*sources, place, own, mask, rank)
     in_specs = [block(x) for x in sources] + [
@@ -268,18 +266,57 @@
             pltpu.VMEM((lows // 4, rank.shape[0] * rows, LANES), jnp.float32),
         ],
         input_output_aliases=aliases,
-        compiler_params=pltpu.CompilerParams(vmem_limit_bytes=48 * 1024 * 1024),
+        compiler_params=pltpu.CompilerParams(vmem_limit_bytes=VMEM_BYTES),
         cost_estimate=pl.CostEstimate(flops=9 * 2**29, bytes_accessed=15 * 2**20, transcendentals=0),
         name="grams",
     )(*args)
+
+
+def join_kernel(parts, pins, x_ref, side_ref, *refs):
+    out_refs = refs[pins:]
+    width = x_ref.shape[2] // 2
+    for (first, count), out_ref in zip(parts, out_refs):
+        own = slice(first, first + count)
+        carry = slice(width + first, width + first + count)
+        for t in range(16):
+            value = x_ref[t, :, own]
+            if t % 4:
+                value = value.astype(jnp.float32) + x_ref[t - 1, :, carry].astype(jnp.float32)
+            out_ref[t] = value.astype(jnp.bfloat16)
+
+        @pl.when(side_ref[0] == 0)
+        def _():
+            for y in range(4):
+                out_ref[16 + y] = x_ref[4 * y + 3, :, carry]
+
+        @pl.when(side_ref[0] != 0)
+        def _():
+            out_ref[16] = jnp.zeros(out_ref.shape[1:], out_ref.dtype)
+            for y in range(3):
+                out_ref[17 + y] = x_ref[4 * y + 3, :, carry]
+
+
+def joined(x, z_hi, parts, *others):
+    outs = [jax.ShapeDtypeStruct((20, x.shape[1], count), x.dtype) for _, count in parts]
+    return pl.pallas_call(
+        functools.partial(join_kernel, parts, len(others)),
+        grid=(1,),
+        out_shape=outs,
+        in_specs=[pl.BlockSpec(x.shape, lambda i: (0, 0, 0)), pl.BlockSpec(memory_space=pltpu.SMEM)]
+        + [pl.BlockSpec(memory_space=pltpu.HBM)] * len(others),
+        out_specs=[pl.BlockSpec(o.shape, lambda i: (0, 0, 0)) for o in outs],
+        cost_estimate=pl.CostEstimate(flops=2**20, bytes_accessed=2**20, transcendentals=0),
+        compiler_params=pltpu.CompilerParams(vmem_limit_bytes=16 * 1024 * 1024),
+        name="joined",
+    )(x, z_hi, *others)
 
 
 def follows(x, *others):
     return pl.pallas_call(
         lambda *refs: None,
         out_shape=jax.ShapeDtypeStruct(x.shape, x.dtype),
-        in_specs=[pl.BlockSpec(memory_space=pl.ANY)] * (1 + len(others)),
-        out_specs=pl.BlockSpec(memory_space=pl.ANY),
+        in_specs=[pl.BlockSpec(memory_space=pltpu.HBM)] * (1 + len(others)),
+        out_specs=pl.BlockSpec(memory_space=pltpu.HBM),
         input_output_aliases={0: 0},
         cost_estimate=pl.CostEstimate(flops=0, bytes_accessed=0, transcendentals=0),
         name="follows",
@@ -291,13 +328,10 @@
 
 
 def on_device(voltages, phase_bin):
-    paths, samples = voltages.shape
+    paths = voltages.shape[0]
     time_devs = lax.axis_size("tm")
     path_devs = lax.axis_size("pol")
     total = time_devs * 2 * HALF
-    width = HALF * FFT_LEN
-    pairs = [(i, i + 1) for i in range(time_devs - 1)]
-    halo = lax.ppermute(voltages[:, samples - width :], "tm", pairs)
     window = jnp.asarray(filter_window())
     twiddle = jnp.asarray(twiddles())
     table = jnp.asarray(inner_table(time_devs))
@@ -311,9 +345,11 @@
     own = jnp.eye(LANES, dtype=jnp.bfloat16)
     t_at = lax.axis_index("tm")
     side = t_at // 4 % 2
-    labels = phase_bin.reshape(4, 2, 4, 2, HALF)
-    labels = jnp.where(side == 0, labels, labels[:, ::-1])[:, :, :, ::-1]
-    labels = labels.transpose(3, 1, 4, 0, 2).reshape(-1)
+    order = np.arange(total).reshape(4, 2, 4, 2, HALF)[:, :, :, ::-1].transpose(3, 1, 4, 0, 2)
+    order = np.stack([order, order[:, ::-1]]).reshape(2, total)
+    pick = (order[:, :, None] == np.arange(total)).astype(np.float32)
+    pick = jnp.where(side == 0, jnp.asarray(pick[0]), jnp.asarray(pick[1]))
+    labels = jnp.sum(pick * phase_bin.astype(jnp.float32)[None, :], axis=1).astype(jnp.int32)
     number = jnp.arange(total, dtype=jnp.int32)
     ahead = (labels[:, None] == labels[None, :]) & (number[:, None] > number[None, :])
     rank = labels * (total // NBINS) + jnp.sum(ahead.astype(jnp.int32), axis=1)
@@ -346,35 +382,45 @@
         return (z, swapped(z, 1), x, swapped(x, 1))
 
     side = side.reshape(1).astype(jnp.int32)
-    late, late_x = spectra(voltages, voltages, 1, window, twiddle, table, side)
+    full = [[(tap, s + tap) for tap in range(TAPS)] for s in range(HALF)]
+    part = [[(tap, s + tap - HALF) for tap in range(TAPS) if s + tap >= HALF] for s in range(HALF)]
+    carry = [[(tap, s + tap + HALF) for tap in range(TAPS) if s + tap < HALF] for s in range(HALF)]
+
+    wide = RADIX * HALF * paths
+    late, late_x = spectra(voltages, window, twiddle, table, side, full, [(0, 0, wide), (1, 0, wide)])
+    early_side = side + jnp.minimum(rank[:1], 0)
+    early, part_x, carry_x = spectra(
+        voltages, window, twiddle, table, early_side, part + carry,
+        [(0, 0, 2 * wide), (1, 0, wide), (1, wide, wide)],
+    )
     late_x = crossed(late_x)
+    part_x = crossed(part_x)
+    carry_x = crossed(carry_x)
     late = exchanged(late)
     late_z = swapped(late, 2)
     late_c = swapped(late, 1)
-    late_x = exchanged(after(late_x, late))
-    halo = after(halo, late_x)
-    early, early_x = spectra(halo, voltages, 0, window, twiddle, table, side)
+    late_x = exchanged(follows(late_x, late, early))
     late_xz = swapped(late_x, 2)
     late_xc = swapped(late_x, 1)
     late_zc = swapped(late_z, 1)
-    early_x = crossed(early_x)
-    early = exchanged(after(early, late_z))
+    early = exchanged(follows(early, late_x, late_z, part_x))
+    early_x = exchanged(follows(jnp.concatenate([part_x, carry_x], axis=1), early))
+    (early,) = joined(early, side, [(0, wide)], late_xz)
     early_z = swapped(early, 2)
-    early_x = exchanged(after(early_x, early, late_xz, late_c, late_xc, late_zc))
-    half = early_x.shape[2] // 2
-    low_z = swapped(after(early_x[:, :, :half], early_z), 2)
+    low, high = joined(early_x, 1 - side, [(0, wide // 2), (wide // 2, wide // 2)])
+    low_z = swapped(low, 2)
+    low_c = swapped(low, 1)
+    high_c = swapped(high, 1)
     late_xzc = swapped(late_xz, 1)
     early_c = swapped(early, 1)
     early_zc = swapped(early_z, 1)
-    early_xc = swapped(early_x, 1)
-    high_z = swapped(after(early_x[:, :, half:], low_z), 2)
     common = (late, late_c, late_z, late_zc, late_xz, late_xzc, late_x, late_xc)
     common += (early, early_c, early_z, early_zc)
-    low = (low_z, swapped(low_z, 1), early_x, early_xc)
-    out = grams(common + low, place, own, mask, rank, 0, None)
+    high = follows(high, low_z, late_c, late_zc, late_xzc, late_xc, early_c, early_zc, low_c)
+    high_z = swapped(high, 2)
+    out = grams(common + (low_z, swapped(low_z, 1), low, low_c), place, own, mask, rank, 0, None)
     high_z = follows(high_z, out)
-    high = (high_z, swapped(high_z, 1), early_x, early_xc)
-    out = grams(common + high, place, own, mask, rank, 1, out)
+    out = grams(common + (high_z, swapped(high_z, 1), high, high_c), place, own, mask, rank, 1, out)
     return out.reshape(CHANNELS // time_devs, NBINS, 2, paths, paths * path_devs)
 
 

time: 194 us -> 176 us (0.907)
  blocking collectives: 37.3 us -> 0 us
  Pallas kernels: 52.9 us -> 64.6 us
  starting transfers between devices: 33.9 us -> 43 us
  local copies, waits for them, and re-layouts: 10 us -> 6.52 us
  other arithmetic: 0.38 us -> 3.21 us
    all_to_all x1 -> x0, blocking collectives: 37.3 us -> none  [exchanged(): lax.all_to_all(x, 'tm', split_axis=0, concat_axis=0, axis_index_groups=gr...]
    all_to_all x3 -> x4, waiting for transfers between devices: 36.1 us -> 2.05 us  [exchanged(): lax.all_to_all(x, 'tm', split_axis=0, concat_axis=0, axis_index_groups=gr...]
    ppermute x2 -> x3, waiting for transfers between devices: 7.56 us -> 28.4 us  [crossed(): return lax.ppermute(x, ('tm', 'pol'), across)]
    all_to_all x3 -> x4, starting transfers between devices: 13 us -> 25.4 us  [exchanged(): lax.all_to_all(x, 'tm', split_axis=0, concat_axis=0, axis_index_groups=gr...]
    ppermute x14 -> x15, waiting for transfers between devices: 15.2 us -> 26.9 us  [swapped(): return lax.ppermute(x, 'pol', [(i, i ^ by) for i in range(4)])]
    pallas_call x2 -> x4, Pallas kernels: 14.1 us -> 23.7 us  [the longest x2 22 us: spectra(): pl.pallas_call(functools.partial(spectra_kernel, spectra_taps, [o[:2] for...]
    ppermute x1 -> x0, starting transfers between devices: 5.13 us -> none  [on_device(): halo = lax.ppermute(voltages[:, samples - width:], 'tm', pairs)]
    slice x2 -> x1, local copies, waits for them, and re-layouts: 3.87 us -> 0.51 us  [on_device(): early_side = side + jnp.minimum(rank[:1], 0)]
  transfers between devices with their start and end apart: 20 -> 22, of which waited for: 10 -> 8; matrix products, arithmetic and copies ran while one was open for 1% -> 2% of each run, Pallas kernels for 17% -> 20%
where the time goes in v3:
time: 176 us
  Pallas kernels  64.6 us (37%)
  waiting for transfers between devices  57.4 us (33%)
  starting transfers between devices  43 us (24%)
  local copies, waits for them, and re-layouts  6.52 us (4%)
  other arithmetic  3.21 us (2%)
    pallas_call x2, Pallas kernels, grams(): pl.pallas_call(gram_kernel, grid=(chans,), out_shape=jax.ShapeDtypeStruct...  40.9 us
    ppermute x3, waiting for transfers between devices, crossed(): return lax.ppermute(x, ('tm', 'pol'), across)  28.4 us
    ppermute x15, waiting for transfers between devices, swapped(): return lax.ppermute(x, 'pol', [(i, i ^ by) for i in range(4)])  26.9 us
    all_to_all x4, starting transfers between devices, exchanged(): lax.all_to_all(x, 'tm', split_axis=0, concat_axis=0, axis_index_groups=gr...  25.4 us
    pallas_call x2, Pallas kernels, spectra(): pl.pallas_call(functools.partial(spectra_kernel, spectra_taps, [o[:2] for...  22 us
    ppermute x15, starting transfers between devices, swapped(): return lax.ppermute(x, 'pol', [(i, i ^ by) for i in range(4)])  12.2 us
    unnamed x38, local copies, waits for them, and re-layouts  6.01 us
    ppermute x3, starting transfers between devices, crossed(): return lax.ppermute(x, ('tm', 'pol'), across)  5.44 us
  transfers between devices with their start and end apart: 22, of which 8 were waited for; matrix products, arithmetic and copies ran while one was open for 2% of the time, Pallas kernels for 20%

profile of v3, /device:TPU:1, one launch (start us, length us, event | category | flops | bytes accessed | tf_op | source)
XLA Modules:
  0.0 175.7 jit_solution(13894950680037680166)
XLA Ops:
  0.0 9.1 %spectra.2 = (bf16[256,1536]{1,0:T(8,128)(2,1)}, bf16[256,1536]{1,0:T(8,128)(2,1)}) custom-call(bf16[32,49152]{1,0:T(8,128)(2,1)} %volts_ref.3, f32[4,8192]{1,0:T(4,128)} %constant.109.clone.window_ref, f32[32,512]{1,0:T(8,128)} %constant.110.clone.twiddle_ref, bf16[512,1024]{1,0:T(8,128)(2,1)} %constant.111.clone.table_ref, s32[1]{0:T(128)} %bitcast.side_ref), custom_call_target="tpu_custom_call" | custom-call | flops 1048576 | bytes 20971520 | tf_op jit(solution)/shard_map/spectra/pallas_call | solution.py:144
  9.1 4.7 %collective-permute-start.3 = (bf16[256,1536]{1,0:T(8,128)(2,1)}, bf16[256,1536]{1,0:T(8,128)(2,1)S(1)}, u32[]{:S(2)}, u32[]{:S(2)}) collective-permute-start(bf16[256,1536]{1,0:T(8,128)(2,1)} %get-tuple-element.13), channel_id=1, source_target_pairs={{0,18},{1,19},{2,16},{3,17},{4,22},{5,23},{6,20},{7,21},{8,26},{9,... | collective-permute-start | bytes 2359304 | tf_op jit(solution)/shard_map/ppermute | solution.py:373
  13.8 6.8 %all-to-all-start = ((bf16[16,16,1536]{2,1,0:T(8,128)(2,1)}), bf16[16,16,1536]{2,1,0:T(8,128)(2,1)S(1)}, u32[]{:S(2)}, u32[]{:S(2)}) async-start(bf16[16,16,1536]{2,1,0:T(8,128)(2,1)} %bitcast.9), calls=%async_computation | async-start | bytes 1572864 | tf_op jit(solution)/shard_map/all_to_all | solution.py:368
  22.1 12.9 %spectra.3 = (bf16[256,3072]{1,0:T(8,128)(2,1)}, bf16[256,1536]{1,0:T(8,128)(2,1)}, bf16[256,1536]{1,0:T(8,128)(2,1)}) custom-call(bf16[32,49152]{1,0:T(8,128)(2,1)} %volts_ref.3, f32[4,8192]{1,0:T(4,128)} %constant.109.clone.window_ref, f32[32,512]{1,0:T(8,128)} %constant.110.clone.twiddle_ref, bf16[512,1024]{1,0:T(8,128)(2,1)} %constant.111.clone.table_ref, ...), custom_call_target="tpu_custom_call" | custom-call | flops 1048576 | bytes 20971520 | tf_op jit(solution)/shard_map/spectra/pallas_call | solution.py:144
  36.3 6.7 %all-to-all-start.1 = ((bf16[16,16,1536]{2,1,0:T(8,128)(2,1)}), bf16[16,16,1536]{2,1,0:T(8,128)(2,1)}, u32[]{:S(2)}, u32[]{:S(2)}) async-start(bf16[16,16,1536]{2,1,0:T(8,128)(2,1)} %bitcast.8), calls=%async_computation.1 | async-start | bytes 1572864 | tf_op jit(solution)/shard_map/all_to_all | solution.py:368
  43.0 11.3 %collective-permute-done.7.refs_3_ = bf16[256,1536]{1,0:T(8,128)(2,1)S(1)} collective-permute-done((bf16[256,1536]{1,0:T(8,128)(2,1)}, bf16[256,1536]{1,0:T(8,128)(2,1)S(1)}, u32[]{:S(2)}, u32[]{:S(2)}) %collective-permute-start.7) | collective-permute-done | bytes 786464 | tf_op jit(solution)/shard_map/ppermute | solution.py:373
  54.3 1.4 all-to-all-done.1.refs_1_.refs_6_
  55.7 5.9 %all-to-all-start.2 = ((bf16[16,16,3072]{2,1,0:T(8,128)(2,1)}), bf16[16,16,3072]{2,1,0:T(8,128)(2,1)S(1)}, u32[]{:S(2)}, u32[]{:S(2)}) async-start(bf16[16,16,3072]{2,1,0:T(8,128)(2,1)} %bitcast.7), calls=%async_computation.2 | async-start | bytes 3145728 | tf_op jit(solution)/shard_map/all_to_all | solution.py:368
  62.3 17.1 %collective-permute-done.11 = bf16[256,1536]{1,0:T(8,128)(2,1)S(1)} collective-permute-done((bf16[256,1536]{1,0:T(8,128)(2,1)}, bf16[256,1536]{1,0:T(8,128)(2,1)S(1)}, u32[]{:S(2)}, u32[]{:S(2)}) %collective-permute-start.11) | collective-permute-done | bytes 786464 | tf_op jit(solution)/shard_map/ppermute | solution.py:373
  79.4 1.3 pad_maximum_fusion.refs_0_
  81.4 1.1 copy-done
  82.6 6.1 %all-to-all-start.3 = ((bf16[16,16,3072]{2,1,0:T(8,128)(2,1)}), bf16[16,16,3072]{2,1,0:T(8,128)(2,1)}, u32[]{:S(2)}, u32[]{:S(2)}) async-start(bf16[16,16,3072]{2,1,0:T(8,128)(2,1)} %bitcast.6), calls=%async_computation.3 | async-start | bytes 3145728 | tf_op jit(solution)/shard_map/all_to_all | solution.py:368
  89.0 1.3 copy-done.7
  90.3 3.9 %collective-permute-start = (bf16[16,16,1536]{2,1,0:T(8,128)(2,1)S(1)}, bf16[16,16,1536]{2,1,0:T(8,128)(2,1)S(1)}, u32[]{:S(2)}, u32[]{:S(2)}) collective-permute-start(bf16[16,16,1536]{2,1,0:T(8,128)(2,1)S(1)} %copy-done.7), channel_id=1, source_target_pairs={{0,1},{1,0},{2,3},{3,2},{4,5},{5,4},{6,7},{7,6},{8,9},{9,8},{10,11... | collective-permute-start | bytes 2359304 | tf_op jit(solution)/shard_map/ppermute | solution.py:327
  94.7 2.5 %collective-permute-done.refs_2_.refs_1_ = bf16[16,16,1536]{2,1,0:T(8,128)(2,1)S(1)} collective-permute-done((bf16[16,16,1536]{2,1,0:T(8,128)(2,1)S(1)}, bf16[16,16,1536]{2,1,0:T(8,128)(2,1)S(1)}, u32[]{:S(2)}, u32[]{:S(2)}) %collective-permute-start) | collective-permute-done | bytes 786464 | tf_op jit(solution)/shard_map/ppermute | solution.py:327
  97.6 10.8 %collective-permute-done.9.refs_10_ = bf16[20,16,1536]{2,1,0:T(8,128)(2,1)} collective-permute-done((bf16[20,16,1536]{2,1,0:T(8,128)(2,1)S(1)}, bf16[20,16,1536]{2,1,0:T(8,128)(2,1)}, u32[]{:S(2)}, u32[]{:S(2)}) %collective-permute-start.9) | collective-permute-done | bytes 983072 | tf_op jit(solution)/shard_map/ppermute | solution.py:327
  108.4 4.8 %collective-permute-start.10 = (bf16[20,16,1536]{2,1,0:T(8,128)(2,1)}, bf16[20,16,1536]{2,1,0:T(8,128)(2,1)}, u32[]{:S(2)}, u32[]{:S(2)}) collective-permute-start(bf16[20,16,1536]{2,1,0:T(8,128)(2,1)} %collective-permute-done.9.refs_10_), channel_id=1, source_target_pairs={{0,1},{1,0},{2,3},{3,2},{4,5},{5,4},{6,7},{7,6},{8,9},{9,8},{10,11... | collective-permute-start | bytes 2949128 | tf_op jit(solution)/shard_map/ppermute | solution.py:327
  113.2 1.6 joined.3
  115.6 11.8 %collective-permute-done.12.refs_1_.refs_12_ = bf16[20,16,768]{2,1,0:T(8,128)(2,1)} collective-permute-done((bf16[20,16,768]{2,1,0:T(8,128)(2,1)S(1)}, bf16[20,16,768]{2,1,0:T(8,128)(2,1)}, u32[]{:S(2)}, u32[]{:S(2)}) %collective-permute-start.12) | collective-permute-done | bytes 491552 | tf_op jit(solution)/shard_map/ppermute | solution.py:327
  127.4 1.3 collective-permute-start.15
  128.7 0.9 fusion.refs_16_
  131.1 20.4 %grams.2.refs_1_.refs_20_ = bf16[8,16,8,2,32,128]{5,4,3,2,1,0:T(8,128)(2,1)} custom-call(bf16[16,16,1536]{2,1,0:T(8,128)(2,1)} %copy-done.6, bf16[16,16,1536]{2,1,0:T(8,128)(2,1)} %copy-done.8, bf16[16,16,1536]{2,1,0:T(8,128)(2,1)} %collective-permute-done.1.refs_2_, bf16[16,16,1536]{2,1,0:T(8,128)(2,1)} %collective-permute-done.2.refs_3_, ...), custom_call_target="tpu_custom_call" | custom-call | flops 4831838208 | bytes 15728640 | tf_op jit(solution)/shard_map/grams/pallas_call | solution.py:258
  152.6 1.8 %collective-permute-done.16.refs_13_ = bf16[20,16,768]{2,1,0:T(8,128)(2,1)S(1)} collective-permute-done((bf16[20,16,768]{2,1,0:T(8,128)(2,1)}, bf16[20,16,768]{2,1,0:T(8,128)(2,1)S(1)}, u32[]{:S(2)}, u32[]{:S(2)}) %collective-permute-start.16) | collective-permute-done | bytes 491552 | tf_op jit(solution)/shard_map/ppermute | solution.py:327
  155.2 20.5 %grams.3 = bf16[8,16,8,2,32,128]{5,4,3,2,1,0:T(8,128)(2,1)} custom-call(bf16[16,16,1536]{2,1,0:T(8,128)(2,1)} %copy-done.6, bf16[16,16,1536]{2,1,0:T(8,128)(2,1)} %copy-done.8, bf16[16,16,1536]{2,1,0:T(8,128)(2,1)} %collective-permute-done.1.refs_2_, bf16[16,16,1536]{2,1,0:T(8,128)(2,1)} %collective-permute-done.2.refs_3_, ...), custom_call_target="tpu_custom_call", output_to_operand_aliasing={{}: (20, {})} | custom-call | flops 4831838208 | bytes 15728640 | tf_op jit(solution)/shard_map/grams/pallas_call | solution.py:258
  (79 shorter events, 8.8 us)
Async XLA Ops:
  9.1 26.1 %collective-permute-start.3 = (bf16[256,1536]{1,0:T(8,128)(2,1)}, bf16[256,1536]{1,0:T(8,128)(2,1)S(1)}, u32[]{:S(2)}, u32[]{:S(2)}) collective-permute-start(bf16[256,1536]{1,0:T(8,128)(2,1)} %get-tuple-element.13), channel_id=1, source_target_pairs={{0,18},{1,19},{2,16},{3,17},{4,22},{5,23},{6,20},{7,21},{8,26},{9,... | collective-permute-start | bytes 2359304 | tf_op jit(solution)/shard_map/ppermute | solution.py:373
  13.8 21.4 %all-to-all-start = ((bf16[16,16,1536]{2,1,0:T(8,128)(2,1)}), bf16[16,16,1536]{2,1,0:T(8,128)(2,1)S(1)}, u32[]{:S(2)}, u32[]{:S(2)}) async-start(bf16[16,16,1536]{2,1,0:T(8,128)(2,1)} %bitcast.9), calls=%async_computation | async-start | bytes 1572864 | tf_op jit(solution)/shard_map/all_to_all | solution.py:368
  35.0 19.3 %collective-permute-start.7 = (bf16[256,1536]{1,0:T(8,128)(2,1)}, bf16[256,1536]{1,0:T(8,128)(2,1)S(1)}, u32[]{:S(2)}, u32[]{:S(2)}) collective-permute-start(bf16[256,1536]{1,0:T(8,128)(2,1)} %get-tuple-element.15), channel_id=1, source_target_pairs={{0,18},{1,19},{2,16},{3,17},{4,22},{5,23},{6,20},{7,21},{8,26},{9,... | collective-permute-start | bytes 2359304 | tf_op jit(solution)/shard_map/ppermute | solution.py:373
  35.2 19.2 %collective-permute-start.1 = (bf16[16,16,1536]{2,1,0:T(8,128)(2,1)S(1)}, bf16[16,16,1536]{2,1,0:T(8,128)(2,1)}, u32[]{:S(2)}, u32[]{:S(2)}) collective-permute-start(bf16[16,16,1536]{2,1,0:T(8,128)(2,1)S(1)} %all-to-all-done.refs_1_.refs_0_), channel_id=1, source_target_pairs={{0,2},{1,3},{2,0},{3,1},{4,6},{5,7},{6,4},{7,5},{8,10},{9,11},{10,... | collective-permute-start | bytes 2359304 | tf_op jit(solution)/shard_map/ppermute | solution.py:327
  36.3 19.4 %all-to-all-start.1 = ((bf16[16,16,1536]{2,1,0:T(8,128)(2,1)}), bf16[16,16,1536]{2,1,0:T(8,128)(2,1)}, u32[]{:S(2)}, u32[]{:S(2)}) async-start(bf16[16,16,1536]{2,1,0:T(8,128)(2,1)} %bitcast.8), calls=%async_computation.1 | async-start | bytes 1572864 | tf_op jit(solution)/shard_map/all_to_all | solution.py:368
  55.7 25.7 %all-to-all-start.2 = ((bf16[16,16,3072]{2,1,0:T(8,128)(2,1)}), bf16[16,16,3072]{2,1,0:T(8,128)(2,1)S(1)}, u32[]{:S(2)}, u32[]{:S(2)}) async-start(bf16[16,16,3072]{2,1,0:T(8,128)(2,1)} %bitcast.7), calls=%async_computation.2 | async-start | bytes 3145728 | tf_op jit(solution)/shard_map/all_to_all | solution.py:368
  61.6 17.8 %collective-permute-start.11 = (bf16[256,1536]{1,0:T(8,128)(2,1)}, bf16[256,1536]{1,0:T(8,128)(2,1)S(1)}, u32[]{:S(2)}, u32[]{:S(2)}) collective-permute-start(bf16[256,1536]{1,0:T(8,128)(2,1)} %get-tuple-element.16), channel_id=1, source_target_pairs={{0,18},{1,19},{2,16},{3,17},{4,22},{5,23},{6,20},{7,21},{8,26},{9,... | collective-permute-start | bytes 2359304 | tf_op jit(solution)/shard_map/ppermute | solution.py:373
  62.2 26.5 %collective-permute-start.4 = (bf16[16,16,1536]{2,1,0:T(8,128)(2,1)}, bf16[16,16,1536]{2,1,0:T(8,128)(2,1)S(1)}, u32[]{:S(2)}, u32[]{:S(2)}) collective-permute-start(bf16[16,16,1536]{2,1,0:T(8,128)(2,1)} %all-to-all-done.1.refs_1_.refs_6_), channel_id=1, source_target_pairs={{0,2},{1,3},{2,0},{3,1},{4,6},{5,7},{6,4},{7,5},{8,10},{9,11},{10,... | collective-permute-start | bytes 2359304 | tf_op jit(solution)/shard_map/ppermute | solution.py:327
  82.6 30.7 %all-to-all-start.3 = ((bf16[16,16,3072]{2,1,0:T(8,128)(2,1)}), bf16[16,16,3072]{2,1,0:T(8,128)(2,1)}, u32[]{:S(2)}, u32[]{:S(2)}) async-start(bf16[16,16,3072]{2,1,0:T(8,128)(2,1)} %bitcast.6), calls=%async_computation.3 | async-start | bytes 3145728 | tf_op jit(solution)/shard_map/all_to_all | solution.py:368
  88.9 41.6 %copy-start.2 = (bf16[20,16,1536]{2,1,0:T(8,128)(2,1)}, bf16[20,16,1536]{2,1,0:T(8,128)(2,1)S(1)}, u32[]{:S(2)}) copy-start(bf16[20,16,1536]{2,1,0:T(8,128)(2,1)S(1)} %joined.2.refs_8_) | copy-start | bytes 2949124
  88.9 19.5 %collective-permute-start.9 = (bf16[20,16,1536]{2,1,0:T(8,128)(2,1)S(1)}, bf16[20,16,1536]{2,1,0:T(8,128)(2,1)}, u32[]{:S(2)}, u32[]{:S(2)}) collective-permute-start(bf16[20,16,1536]{2,1,0:T(8,128)(2,1)S(1)} %joined.2.refs_8_), channel_id=1, source_target_pairs={{0,2},{1,3},{2,0},{3,1},{4,6},{5,7},{6,4},{7,5},{8,10},{9,11},{10,... | collective-permute-start | bytes 2949128 | tf_op jit(solution)/shard_map/ppermute | solution.py:327
  90.3 6.9 %collective-permute-start = (bf16[16,16,1536]{2,1,0:T(8,128)(2,1)S(1)}, bf16[16,16,1536]{2,1,0:T(8,128)(2,1)S(1)}, u32[]{:S(2)}, u32[]{:S(2)}) collective-permute-start(bf16[16,16,1536]{2,1,0:T(8,128)(2,1)S(1)} %copy-done.7), channel_id=1, source_target_pairs={{0,1},{1,0},{2,3},{3,2},{4,5},{5,4},{6,7},{7,6},{8,9},{9,8},{10,11... | collective-permute-start | bytes 2359304 | tf_op jit(solution)/shard_map/ppermute | solution.py:327
  94.2 20.6 %collective-permute-start.2 = (bf16[16,16,1536]{2,1,0:T(8,128)(2,1)}, bf16[16,16,1536]{2,1,0:T(8,128)(2,1)}, u32[]{:S(2)}, u32[]{:S(2)}) collective-permute-start(bf16[16,16,1536]{2,1,0:T(8,128)(2,1)} %collective-permute-done.1.refs_2_), channel_id=1, source_target_pairs={{0,1},{1,0},{2,3},{3,2},{4,5},{5,4},{6,7},{7,6},{8,9},{9,8},{10,11... | collective-permute-start | bytes 2359304 | tf_op jit(solution)/shard_map/ppermute | solution.py:327
  94.2 20.7 %collective-permute-start.6 = (bf16[16,16,1536]{2,1,0:T(8,128)(2,1)}, bf16[16,16,1536]{2,1,0:T(8,128)(2,1)}, u32[]{:S(2)}, u32[]{:S(2)}) collective-permute-start(bf16[16,16,1536]{2,1,0:T(8,128)(2,1)} %all-to-all-done.1.refs_1_.refs_6_), channel_id=1, source_target_pairs={{0,1},{1,0},{2,3},{3,2},{4,5},{5,4},{6,7},{7,6},{8,9},{9,8},{10,11... | collective-permute-start | bytes 2359304 | tf_op jit(solution)/shard_map/ppermute | solution.py:327
  94.7 20.8 %collective-permute-start.5 = (bf16[16,16,1536]{2,1,0:T(8,128)(2,1)S(1)}, bf16[16,16,1536]{2,1,0:T(8,128)(2,1)}, u32[]{:S(2)}, u32[]{:S(2)}) collective-permute-start(bf16[16,16,1536]{2,1,0:T(8,128)(2,1)S(1)} %collective-permute-done.4.refs_0_.refs_4_), channel_id=1, source_target_pairs={{0,1},{1,0},{2,3},{3,2},{4,5},{5,4},{6,7},{7,6},{8,9},{9,8},{10,11... | collective-permute-start | bytes 2359304 | tf_op jit(solution)/shard_map/ppermute | solution.py:327
  97.2 32.5 %copy-start.8 = (bf16[16,16,1536]{2,1,0:T(8,128)(2,1)}, bf16[16,16,1536]{2,1,0:T(8,128)(2,1)S(1)}, u32[]{:S(2)}) copy-start(bf16[16,16,1536]{2,1,0:T(8,128)(2,1)S(1)} %collective-permute-done.refs_2_.refs_1_) | copy-start | bytes 2359300
  97.2 32.4 %collective-permute-start.8 = (bf16[20,16,1536]{2,1,0:T(8,128)(2,1)S(1)}, bf16[20,16,1536]{2,1,0:T(8,128)(2,1)}, u32[]{:S(2)}, u32[]{:S(2)}) collective-permute-start(bf16[20,16,1536]{2,1,0:T(8,128)(2,1)S(1)} %joined.2.refs_8_), channel_id=1, source_target_pairs={{0,1},{1,0},{2,3},{3,2},{4,5},{5,4},{6,7},{7,6},{8,9},{9,8},{10,11... | collective-permute-start | bytes 2949128 | tf_op jit(solution)/shard_map/ppermute | solution.py:327
  108.4 21.2 %collective-permute-start.10 = (bf16[20,16,1536]{2,1,0:T(8,128)(2,1)}, bf16[20,16,1536]{2,1,0:T(8,128)(2,1)}, u32[]{:S(2)}, u32[]{:S(2)}) collective-permute-start(bf16[20,16,1536]{2,1,0:T(8,128)(2,1)} %collective-permute-done.9.refs_10_), channel_id=1, source_target_pairs={{0,1},{1,0},{2,3},{3,2},{4,5},{5,4},{6,7},{7,6},{8,9},{9,8},{10,11... | collective-permute-start | bytes 2949128 | tf_op jit(solution)/shard_map/ppermute | solution.py:327
  114.9 12.5 %collective-permute-start.12 = (bf16[20,16,768]{2,1,0:T(8,128)(2,1)S(1)}, bf16[20,16,768]{2,1,0:T(8,128)(2,1)}, u32[]{:S(2)}, u32[]{:S(2)}) collective-permute-start(bf16[20,16,768]{2,1,0:T(8,128)(2,1)S(1)} %get-tuple-element.18.refs_14_), channel_id=1, source_target_pairs={{0,2},{1,3},{2,0},{3,1},{4,6},{5,7},{6,4},{7,5},{8,10},{9,11},{10,... | collective-permute-start | bytes 1474568 | tf_op jit(solution)/shard_map/ppermute | solution.py:327
  115.0 14.7 %collective-permute-start.17 = (bf16[20,16,768]{2,1,0:T(8,128)(2,1)S(1)}, bf16[20,16,768]{2,1,0:T(8,128)(2,1)}, u32[]{:S(2)}, u32[]{:S(2)}) collective-permute-start(bf16[20,16,768]{2,1,0:T(8,128)(2,1)S(1)} %get-tuple-element.17.refs_0_), channel_id=1, source_target_pairs={{0,1},{1,0},{2,3},{3,2},{4,5},{5,4},{6,7},{7,6},{8,9},{9,8},{10,11... | collective-permute-start | bytes 1474568 | tf_op jit(solution)/shard_map/ppermute | solution.py:327
  115.5 14.1 %collective-permute-start.13 = (bf16[20,16,768]{2,1,0:T(8,128)(2,1)S(1)}, bf16[20,16,768]{2,1,0:T(8,128)(2,1)S(1)}, u32[]{:S(2)}, u32[]{:S(2)}) collective-permute-start(bf16[20,16,768]{2,1,0:T(8,128)(2,1)S(1)} %get-tuple-element.18.refs_14_), channel_id=1, source_target_pairs={{0,1},{1,0},{2,3},{3,2},{4,5},{5,4},{6,7},{7,6},{8,9},{9,8},{10,11... | collective-permute-start | bytes 1474568 | tf_op jit(solution)/shard_map/ppermute | solution.py:327
  127.4 3.7 %collective-permute-start.15 = (bf16[20,16,768]{2,1,0:T(8,128)(2,1)}, bf16[20,16,768]{2,1,0:T(8,128)(2,1)}, u32[]{:S(2)}, u32[]{:S(2)}) collective-permute-start(bf16[20,16,768]{2,1,0:T(8,128)(2,1)} %collective-permute-done.12.refs_1_.refs_12_), channel_id=1, source_target_pairs={{0,1},{1,0},{2,3},{3,2},{4,5},{5,4},{6,7},{7,6},{8,9},{9,8},{10,11... | collective-permute-start | bytes 1474568 | tf_op jit(solution)/shard_map/ppermute | solution.py:327
  130.4 21.0 %collective-permute-start.14 = (bf16[20,16,768]{2,1,0:T(8,128)(2,1)}, bf16[20,16,768]{2,1,0:T(8,128)(2,1)S(1)}, u32[]{:S(2)}, u32[]{:S(2)}) collective-permute-start(bf16[20,16,768]{2,1,0:T(8,128)(2,1)} %follows.8.refs_14_), channel_id=1, source_target_pairs={{0,2},{1,3},{2,0},{3,1},{4,6},{5,7},{6,4},{7,5},{8,10},{9,11},{10,... | collective-permute-start | bytes 1474568 | tf_op jit(solution)/shard_map/ppermute | solution.py:327
  152.3 2.1 %collective-permute-start.16 = (bf16[20,16,768]{2,1,0:T(8,128)(2,1)}, bf16[20,16,768]{2,1,0:T(8,128)(2,1)S(1)}, u32[]{:S(2)}, u32[]{:S(2)}) collective-permute-start(bf16[20,16,768]{2,1,0:T(8,128)(2,1)} %follows.9.refs_12_), channel_id=1, source_target_pairs={{0,1},{1,0},{2,3},{3,2},{4,5},{5,4},{6,7},{7,6},{8,9},{9,8},{10,11... | collective-permute-start | bytes 1474568 | tf_op jit(solution)/shard_map/ppermute | solution.py:327
  (17 other events, 123.4 us)

commit v4 on v3

--- a/solution.py
+++ b/solution.py
@@ -17,7 +17,8 @@
 RADIX = 16
 INNER = FFT_LEN // RADIX
 LANES = 128
-VMEM_BYTES = 60 * 1024 * 1024
+PITCH = 24
+VMEM_BYTES = 63 * 1024 * 1024
 HALF = 3
 NT = (((1,), (1,)), ((), ()))
 
@@ -187,7 +188,7 @@
             for n in range(len(parts)):
                 for t in range(times):
                     rank = rank_ref[(n * HALF + s) * times + t]
-                    at = pl.ds(pl.multiple_of(rank * rows, rows), rows)
+                    at = pl.ds(pl.multiple_of(rank * PITCH, 8), rows)
                     here = slice((n * times + t) * rows, (n * times + t + 1) * rows)
                     o_ref[number // HALF, at, :] = mine[here]
                     for l in range(4):
@@ -202,8 +203,8 @@
     shape = (NBINS // 2, paths, LANES)
 
     def scaled(ref, low):
-        re = ref[low, pl.ds(chan, total, stride=rows), :]
-        im = ref[low, pl.ds(chans + chan, total, stride=rows), :]
+        re = ref[low, pl.ds(chan, total, stride=PITCH), :]
+        im = ref[low, pl.ds(chans + chan, total, stride=PITCH), :]
         power = jnp.sum(re * re + im * im, axis=0, keepdims=True)
         equalizer = lax.rsqrt(power / total + 1e-06) * math.sqrt(NBINS / total)
         return (re * equalizer).astype(jnp.bfloat16), (im * equalizer).astype(jnp.bfloat16)
@@ -262,8 +263,8 @@
         in_specs=in_specs,
         out_specs=pl.BlockSpec((1, lows, NBINS, 2, paths, LANES), lambda j: (j, part, 0, 0, 0, 0)),
         scratch_shapes=[
-            pltpu.VMEM((lows, rank.shape[0] * rows, LANES), jnp.float32),
-            pltpu.VMEM((lows // 4, rank.shape[0] * rows, LANES), jnp.float32),
+            pltpu.VMEM((lows, rank.shape[0] * PITCH, LANES), jnp.float32),
+            pltpu.VMEM((lows // 4, rank.shape[0] * PITCH, LANES), jnp.float32),
         ],
         input_output_aliases=aliases,
         compiler_params=pltpu.CompilerParams(vmem_limit_bytes=VMEM_BYTES),
@@ -342,7 +343,7 @@
     device = jnp.bitwise_xor(src // LANES, me)
     target = (src % LANES) // paths * LANES + device * paths + src % paths
     place = (target == dst).astype(jnp.bfloat16)
-    own = jnp.eye(LANES, dtype=jnp.bfloat16)
+    own = jnp.asarray(np.eye(LANES).astype(ml_dtypes.bfloat16))
     t_at = lax.axis_index("tm")
     side = t_at // 4 % 2
     order = np.arange(total).reshape(4, 2, 4, 2, HALF)[:, :, :, ::-1].transpose(3, 1, 4, 0, 2)
@@ -388,9 +389,8 @@
 
     wide = RADIX * HALF * paths
     late, late_x = spectra(voltages, window, twiddle, table, side, full, [(0, 0, wide), (1, 0, wide)])
-    early_side = side + jnp.minimum(rank[:1], 0)
     early, part_x, carry_x = spectra(
-        voltages, window, twiddle, table, early_side, part + carry,
+        voltages, window, twiddle, table, side, part + carry,
         [(0, 0, 2 * wide), (1, 0, wide), (1, wide, wide)],
     )
     late_x = crossed(late_x)
@@ -405,7 +405,7 @@
     late_zc = swapped(late_z, 1)
     early = exchanged(follows(early, late_x, late_z, part_x))
     early_x = exchanged(follows(jnp.concatenate([part_x, carry_x], axis=1), early))
-    (early,) = joined(early, side, [(0, wide)], late_xz)
+    (early,) = joined(early, side, [(0, wide)], late_xz, place, rank)
     early_z = swapped(early, 2)
     low, high = joined(early_x, 1 - side, [(0, wide // 2), (wide // 2, wide // 2)])
     low_z = swapped(low, 2)

time: 176 us -> 170 us (0.966)
  Pallas kernels: 64.6 us -> 58.9 us
    pallas_call x2, Pallas kernels: 40.9 us -> 35.2 us  [grams(): pl.pallas_call(gram_kernel, grid=(chans,), out_shape=jax.ShapeDtypeStruct...]
    unnamed x38 -> x40, local copies, waits for them, and re-layouts: 6.01 us -> 6.52 us
  transfers between devices with their start and end apart: 22 -> 22, of which waited for: 8 -> 8; matrix products, arithmetic and copies ran while one was open for 2% -> 2% of each run, Pallas kernels for 20% -> 19%
where the time goes in v4:
time: 170 us; the launch traced here: 169 us
  Pallas kernels  58.9 us (35%)
  waiting for transfers between devices  57.3 us (34%)
  starting transfers between devices  43.5 us (26%)
  local copies, waits for them, and re-layouts  6.52 us (4%)
  other arithmetic  2.93 us (2%)
    pallas_call x2, Pallas kernels, grams(): pl.pallas_call(gram_kernel, grid=(chans,), out_shape=jax.ShapeDtypeStruct...  35.2 us
    ppermute x3, waiting for transfers between devices, crossed(): return lax.ppermute(x, ('tm', 'pol'), across)  28.7 us
    ppermute x15, waiting for transfers between devices, swapped(): return lax.ppermute(x, 'pol', [(i, i ^ by) for i in range(4)])  27.6 us
    all_to_all x4, starting transfers between devices, exchanged(): lax.all_to_all(x, 'tm', split_axis=0, concat_axis=0, axis_index_groups=gr...  26.2 us
    pallas_call x2, Pallas kernels, spectra(): pl.pallas_call(functools.partial(spectra_kernel, spectra_taps, [o[:2] for...  22 us
    ppermute x15, starting transfers between devices, swapped(): return lax.ppermute(x, 'pol', [(i, i ^ by) for i in range(4)])  12.2 us
    unnamed x40, local copies, waits for them, and re-layouts  6.52 us
    ppermute x3, starting transfers between devices, crossed(): return lax.ppermute(x, ('tm', 'pol'), across)  5.05 us
  transfers between devices with their start and end apart: 22, of which 8 were waited for; matrix products, arithmetic and copies ran while one was open for 2% of the time, Pallas kernels for 19%

profile of v4, /device:TPU:1, one launch (start us, length us, event | category | flops | bytes accessed | tf_op | source)
XLA Modules:
  0.0 169.4 jit_solution(13113330750922394674)
XLA Ops:
  0.0 9.1 %spectra.2 = (bf16[256,1536]{1,0:T(8,128)(2,1)}, bf16[256,1536]{1,0:T(8,128)(2,1)}) custom-call(bf16[32,49152]{1,0:T(8,128)(2,1)} %volts_ref.3, f32[4,8192]{1,0:T(4,128)} %constant.109.clone.window_ref, f32[32,512]{1,0:T(8,128)} %constant.110.clone.twiddle_ref, bf16[512,1024]{1,0:T(8,128)(2,1)} %constant.111.clone.table_ref, s32[1]{0:T(128)} %bitcast.side_ref), custom_call_target="tpu_custom_call" | custom-call | flops 1048576 | bytes 20971520 | tf_op jit(solution)/shard_map/spectra/pallas_call | solution.py:145
  9.1 4.6 %collective-permute-start.3 = (bf16[256,1536]{1,0:T(8,128)(2,1)}, bf16[256,1536]{1,0:T(8,128)(2,1)}, u32[]{:S(2)}, u32[]{:S(2)}) collective-permute-start(bf16[256,1536]{1,0:T(8,128)(2,1)} %get-tuple-element.13), channel_id=1, source_target_pairs={{0,18},{1,19},{2,16},{3,17},{4,22},{5,23},{6,20},{7,21},{8,26},{9,... | collective-permute-start | bytes 2359304 | tf_op jit(solution)/shard_map/ppermute | solution.py:374
  13.7 6.8 %all-to-all-start = ((bf16[16,16,1536]{2,1,0:T(8,128)(2,1)}), bf16[16,16,1536]{2,1,0:T(8,128)(2,1)S(1)}, u32[]{:S(2)}, u32[]{:S(2)}) async-start(bf16[16,16,1536]{2,1,0:T(8,128)(2,1)} %bitcast.8), calls=%async_computation | async-start | bytes 1572864 | tf_op jit(solution)/shard_map/all_to_all | solution.py:369
  20.4 12.9 %spectra.3 = (bf16[256,3072]{1,0:T(8,128)(2,1)}, bf16[256,1536]{1,0:T(8,128)(2,1)}, bf16[256,1536]{1,0:T(8,128)(2,1)}) custom-call(bf16[32,49152]{1,0:T(8,128)(2,1)} %volts_ref.3, f32[4,8192]{1,0:T(4,128)} %constant.109.clone.window_ref, f32[32,512]{1,0:T(8,128)} %constant.110.clone.twiddle_ref, bf16[512,1024]{1,0:T(8,128)(2,1)} %constant.111.clone.table_ref, ...), custom_call_target="tpu_custom_call" | custom-call | flops 1048576 | bytes 20971520 | tf_op jit(solution)/shard_map/spectra/pallas_call | solution.py:145
  33.5 0.8 copy-done.8
  34.3 6.7 %all-to-all-start.1 = ((bf16[16,16,1536]{2,1,0:T(8,128)(2,1)}), bf16[16,16,1536]{2,1,0:T(8,128)(2,1)}, u32[]{:S(2)}, u32[]{:S(2)}) async-start(bf16[16,16,1536]{2,1,0:T(8,128)(2,1)} %bitcast.2), calls=%async_computation.1 | async-start | bytes 1572864 | tf_op jit(solution)/shard_map/all_to_all | solution.py:369
  41.0 11.7 %collective-permute-done.7.refs_3_ = bf16[256,1536]{1,0:T(8,128)(2,1)S(1)} collective-permute-done((bf16[256,1536]{1,0:T(8,128)(2,1)}, bf16[256,1536]{1,0:T(8,128)(2,1)S(1)}, u32[]{:S(2)}, u32[]{:S(2)}) %collective-permute-start.7) | collective-permute-done | bytes 786464 | tf_op jit(solution)/shard_map/ppermute | solution.py:374
  52.7 1.0 all-to-all-done.1.refs_1_.refs_6_
  53.7 6.3 %all-to-all-start.2 = ((bf16[16,16,3072]{2,1,0:T(8,128)(2,1)}), bf16[16,16,3072]{2,1,0:T(8,128)(2,1)S(1)}, u32[]{:S(2)}, u32[]{:S(2)}) async-start(bf16[16,16,3072]{2,1,0:T(8,128)(2,1)} %bitcast.7), calls=%async_computation.2 | async-start | bytes 3145728 | tf_op jit(solution)/shard_map/all_to_all | solution.py:369
  60.9 17.0 %collective-permute-done.11 = bf16[256,1536]{1,0:T(8,128)(2,1)} collective-permute-done((bf16[256,1536]{1,0:T(8,128)(2,1)}, bf16[256,1536]{1,0:T(8,128)(2,1)}, u32[]{:S(2)}, u32[]{:S(2)}) %collective-permute-start.11) | collective-permute-done | bytes 786464 | tf_op jit(solution)/shard_map/ppermute | solution.py:374
  77.9 2.5 %pad_maximum_fusion.refs_0_ = bf16[256,3072]{1,0:T(8,128)(2,1)} fusion(bf16[256,1536]{1,0:T(8,128)(2,1)} %collective-permute-done.11, bf16[256,1536]{1,0:T(8,128)(2,1)S(1)} %copy-done.12), kind=kLoop, calls=%fused_computation | loop fusion | flops 3145728 | bytes 3145728 | tf_op jit(solution)/shard_map/concatenate | solution.py:407
  80.4 1.1 copy-done
  81.5 6.5 %all-to-all-start.3 = ((bf16[16,16,3072]{2,1,0:T(8,128)(2,1)}), bf16[16,16,3072]{2,1,0:T(8,128)(2,1)}, u32[]{:S(2)}, u32[]{:S(2)}) async-start(bf16[16,16,3072]{2,1,0:T(8,128)(2,1)} %bitcast.6), calls=%async_computation.3 | async-start | bytes 3145728 | tf_op jit(solution)/shard_map/all_to_all | solution.py:369
  89.0 0.8 copy-done.9
  89.8 4.2 %collective-permute-start = (bf16[16,16,1536]{2,1,0:T(8,128)(2,1)S(1)}, bf16[16,16,1536]{2,1,0:T(8,128)(2,1)S(1)}, u32[]{:S(2)}, u32[]{:S(2)}) collective-permute-start(bf16[16,16,1536]{2,1,0:T(8,128)(2,1)S(1)} %copy-done.9), channel_id=1, source_target_pairs={{0,1},{1,0},{2,3},{3,2},{4,5},{5,4},{6,7},{7,6},{8,9},{9,8},{10,11... | collective-permute-start | bytes 2359304 | tf_op jit(solution)/shard_map/ppermute | solution.py:328
  94.5 2.5 %collective-permute-done.refs_2_.refs_1_ = bf16[16,16,1536]{2,1,0:T(8,128)(2,1)S(1)} collective-permute-done((bf16[16,16,1536]{2,1,0:T(8,128)(2,1)S(1)}, bf16[16,16,1536]{2,1,0:T(8,128)(2,1)S(1)}, u32[]{:S(2)}, u32[]{:S(2)}) %collective-permute-start) | collective-permute-done | bytes 786464 | tf_op jit(solution)/shard_map/ppermute | solution.py:328
  97.4 10.8 %collective-permute-done.9.refs_10_ = bf16[20,16,1536]{2,1,0:T(8,128)(2,1)} collective-permute-done((bf16[20,16,1536]{2,1,0:T(8,128)(2,1)S(1)}, bf16[20,16,1536]{2,1,0:T(8,128)(2,1)}, u32[]{:S(2)}, u32[]{:S(2)}) %collective-permute-start.9) | collective-permute-done | bytes 983072 | tf_op jit(solution)/shard_map/ppermute | solution.py:328
  108.1 5.1 %collective-permute-start.10 = (bf16[20,16,1536]{2,1,0:T(8,128)(2,1)}, bf16[20,16,1536]{2,1,0:T(8,128)(2,1)}, u32[]{:S(2)}, u32[]{:S(2)}) collective-permute-start(bf16[20,16,1536]{2,1,0:T(8,128)(2,1)} %collective-permute-done.9.refs_10_), channel_id=1, source_target_pairs={{0,1},{1,0},{2,3},{3,2},{4,5},{5,4},{6,7},{7,6},{8,9},{9,8},{10,11... | collective-permute-start | bytes 2949128 | tf_op jit(solution)/shard_map/ppermute | solution.py:328
  113.2 1.6 joined.3
  115.6 12.3 %collective-permute-done.12.refs_1_.refs_12_ = bf16[20,16,768]{2,1,0:T(8,128)(2,1)} collective-permute-done((bf16[20,16,768]{2,1,0:T(8,128)(2,1)S(1)}, bf16[20,16,768]{2,1,0:T(8,128)(2,1)}, u32[]{:S(2)}, u32[]{:S(2)}) %collective-permute-start.12) | collective-permute-done | bytes 491552 | tf_op jit(solution)/shard_map/ppermute | solution.py:328
  130.5 17.6 %grams.2.refs_1_.refs_20_ = bf16[8,16,8,2,32,128]{5,4,3,2,1,0:T(8,128)(2,1)} custom-call(bf16[16,16,1536]{2,1,0:T(8,128)(2,1)} %copy-done.8, bf16[16,16,1536]{2,1,0:T(8,128)(2,1)} %copy-done.10, bf16[16,16,1536]{2,1,0:T(8,128)(2,1)} %collective-permute-done.1.refs_2_, bf16[16,16,1536]{2,1,0:T(8,128)(2,1)} %collective-permute-done.2.refs_3_, ...), custom_call_target="tpu_custom_call" | custom-call | flops 4831838208 | bytes 15728640 | tf_op jit(solution)/shard_map/grams/pallas_call | solution.py:259
  149.3 1.7 %collective-permute-done.16.refs_13_ = bf16[20,16,768]{2,1,0:T(8,128)(2,1)S(1)} collective-permute-done((bf16[20,16,768]{2,1,0:T(8,128)(2,1)}, bf16[20,16,768]{2,1,0:T(8,128)(2,1)S(1)}, u32[]{:S(2)}, u32[]{:S(2)}) %collective-permute-start.16) | collective-permute-done | bytes 491552 | tf_op jit(solution)/shard_map/ppermute | solution.py:328
  151.0 0.8 copy-done.16
  151.8 17.6 %grams.3 = bf16[8,16,8,2,32,128]{5,4,3,2,1,0:T(8,128)(2,1)} custom-call(bf16[16,16,1536]{2,1,0:T(8,128)(2,1)} %copy-done.8, bf16[16,16,1536]{2,1,0:T(8,128)(2,1)} %copy-done.10, bf16[16,16,1536]{2,1,0:T(8,128)(2,1)} %collective-permute-done.1.refs_2_, bf16[16,16,1536]{2,1,0:T(8,128)(2,1)} %collective-permute-done.2.refs_3_, ...), custom_call_target="tpu_custom_call", output_to_operand_aliasing={{}: (20, {})} | custom-call | flops 4831838208 | bytes 15728640 | tf_op jit(solution)/shard_map/grams/pallas_call | solution.py:259
  (79 shorter events, 7.3 us)
Async XLA Ops:
  9.1 24.4 %collective-permute-start.3 = (bf16[256,1536]{1,0:T(8,128)(2,1)}, bf16[256,1536]{1,0:T(8,128)(2,1)}, u32[]{:S(2)}, u32[]{:S(2)}) collective-permute-start(bf16[256,1536]{1,0:T(8,128)(2,1)} %get-tuple-element.13), channel_id=1, source_target_pairs={{0,18},{1,19},{2,16},{3,17},{4,22},{5,23},{6,20},{7,21},{8,26},{9,... | collective-permute-start | bytes 2359304 | tf_op jit(solution)/shard_map/ppermute | solution.py:374
  13.7 19.7 %all-to-all-start = ((bf16[16,16,1536]{2,1,0:T(8,128)(2,1)}), bf16[16,16,1536]{2,1,0:T(8,128)(2,1)S(1)}, u32[]{:S(2)}, u32[]{:S(2)}) async-start(bf16[16,16,1536]{2,1,0:T(8,128)(2,1)} %bitcast.8), calls=%async_computation | async-start | bytes 1572864 | tf_op jit(solution)/shard_map/all_to_all | solution.py:369
  33.3 19.3 %collective-permute-start.7 = (bf16[256,1536]{1,0:T(8,128)(2,1)}, bf16[256,1536]{1,0:T(8,128)(2,1)S(1)}, u32[]{:S(2)}, u32[]{:S(2)}) collective-permute-start(bf16[256,1536]{1,0:T(8,128)(2,1)} %get-tuple-element.15), channel_id=1, source_target_pairs={{0,18},{1,19},{2,16},{3,17},{4,22},{5,23},{6,20},{7,21},{8,26},{9,... | collective-permute-start | bytes 2359304 | tf_op jit(solution)/shard_map/ppermute | solution.py:374
  33.3 19.3 %collective-permute-start.1 = (bf16[16,16,1536]{2,1,0:T(8,128)(2,1)S(1)}, bf16[16,16,1536]{2,1,0:T(8,128)(2,1)}, u32[]{:S(2)}, u32[]{:S(2)}) collective-permute-start(bf16[16,16,1536]{2,1,0:T(8,128)(2,1)S(1)} %all-to-all-done.refs_1_.refs_0_), channel_id=1, source_target_pairs={{0,2},{1,3},{2,0},{3,1},{4,6},{5,7},{6,4},{7,5},{8,10},{9,11},{10,... | collective-permute-start | bytes 2359304 | tf_op jit(solution)/shard_map/ppermute | solution.py:328
  34.3 19.4 %all-to-all-start.1 = ((bf16[16,16,1536]{2,1,0:T(8,128)(2,1)}), bf16[16,16,1536]{2,1,0:T(8,128)(2,1)}, u32[]{:S(2)}, u32[]{:S(2)}) async-start(bf16[16,16,1536]{2,1,0:T(8,128)(2,1)} %bitcast.2), calls=%async_computation.1 | async-start | bytes 1572864 | tf_op jit(solution)/shard_map/all_to_all | solution.py:369
  53.7 26.7 %all-to-all-start.2 = ((bf16[16,16,3072]{2,1,0:T(8,128)(2,1)}), bf16[16,16,3072]{2,1,0:T(8,128)(2,1)S(1)}, u32[]{:S(2)}, u32[]{:S(2)}) async-start(bf16[16,16,3072]{2,1,0:T(8,128)(2,1)} %bitcast.7), calls=%async_computation.2 | async-start | bytes 3145728 | tf_op jit(solution)/shard_map/all_to_all | solution.py:369
  60.0 17.9 %collective-permute-start.11 = (bf16[256,1536]{1,0:T(8,128)(2,1)}, bf16[256,1536]{1,0:T(8,128)(2,1)}, u32[]{:S(2)}, u32[]{:S(2)}) collective-permute-start(bf16[256,1536]{1,0:T(8,128)(2,1)} %get-tuple-element.16), channel_id=1, source_target_pairs={{0,18},{1,19},{2,16},{3,17},{4,22},{5,23},{6,20},{7,21},{8,26},{9,... | collective-permute-start | bytes 2359304 | tf_op jit(solution)/shard_map/ppermute | solution.py:374
  60.8 27.4 %collective-permute-start.4 = (bf16[16,16,1536]{2,1,0:T(8,128)(2,1)}, bf16[16,16,1536]{2,1,0:T(8,128)(2,1)S(1)}, u32[]{:S(2)}, u32[]{:S(2)}) collective-permute-start(bf16[16,16,1536]{2,1,0:T(8,128)(2,1)} %all-to-all-done.1.refs_1_.refs_6_), channel_id=1, source_target_pairs={{0,2},{1,3},{2,0},{3,1},{4,6},{5,7},{6,4},{7,5},{8,10},{9,11},{10,... | collective-permute-start | bytes 2359304 | tf_op jit(solution)/shard_map/ppermute | solution.py:328
  81.5 31.8 %all-to-all-start.3 = ((bf16[16,16,3072]{2,1,0:T(8,128)(2,1)}), bf16[16,16,3072]{2,1,0:T(8,128)(2,1)}, u32[]{:S(2)}, u32[]{:S(2)}) async-start(bf16[16,16,3072]{2,1,0:T(8,128)(2,1)} %bitcast.6), calls=%async_computation.3 | async-start | bytes 3145728 | tf_op jit(solution)/shard_map/all_to_all | solution.py:369
  89.0 41.3 %copy-start.2 = (bf16[20,16,1536]{2,1,0:T(8,128)(2,1)}, bf16[20,16,1536]{2,1,0:T(8,128)(2,1)S(1)}, u32[]{:S(2)}) copy-start(bf16[20,16,1536]{2,1,0:T(8,128)(2,1)S(1)} %joined.2.refs_8_) | copy-start | bytes 2949124
  89.0 19.2 %collective-permute-start.9 = (bf16[20,16,1536]{2,1,0:T(8,128)(2,1)S(1)}, bf16[20,16,1536]{2,1,0:T(8,128)(2,1)}, u32[]{:S(2)}, u32[]{:S(2)}) collective-permute-start(bf16[20,16,1536]{2,1,0:T(8,128)(2,1)S(1)} %joined.2.refs_8_), channel_id=1, source_target_pairs={{0,2},{1,3},{2,0},{3,1},{4,6},{5,7},{6,4},{7,5},{8,10},{9,11},{10,... | collective-permute-start | bytes 2949128 | tf_op jit(solution)/shard_map/ppermute | solution.py:328
  89.8 7.2 %collective-permute-start = (bf16[16,16,1536]{2,1,0:T(8,128)(2,1)S(1)}, bf16[16,16,1536]{2,1,0:T(8,128)(2,1)S(1)}, u32[]{:S(2)}, u32[]{:S(2)}) collective-permute-start(bf16[16,16,1536]{2,1,0:T(8,128)(2,1)S(1)} %copy-done.9), channel_id=1, source_target_pairs={{0,1},{1,0},{2,3},{3,2},{4,5},{5,4},{6,7},{7,6},{8,9},{9,8},{10,11... | collective-permute-start | bytes 2359304 | tf_op jit(solution)/shard_map/ppermute | solution.py:328
  94.0 20.9 %collective-permute-start.2 = (bf16[16,16,1536]{2,1,0:T(8,128)(2,1)}, bf16[16,16,1536]{2,1,0:T(8,128)(2,1)}, u32[]{:S(2)}, u32[]{:S(2)}) collective-permute-start(bf16[16,16,1536]{2,1,0:T(8,128)(2,1)} %collective-permute-done.1.refs_2_), channel_id=1, source_target_pairs={{0,1},{1,0},{2,3},{3,2},{4,5},{5,4},{6,7},{7,6},{8,9},{9,8},{10,11... | collective-permute-start | bytes 2359304 | tf_op jit(solution)/shard_map/ppermute | solution.py:328
  94.0 21.0 %collective-permute-start.6 = (bf16[16,16,1536]{2,1,0:T(8,128)(2,1)}, bf16[16,16,1536]{2,1,0:T(8,128)(2,1)}, u32[]{:S(2)}, u32[]{:S(2)}) collective-permute-start(bf16[16,16,1536]{2,1,0:T(8,128)(2,1)} %all-to-all-done.1.refs_1_.refs_6_), channel_id=1, source_target_pairs={{0,1},{1,0},{2,3},{3,2},{4,5},{5,4},{6,7},{7,6},{8,9},{9,8},{10,11... | collective-permute-start | bytes 2359304 | tf_op jit(solution)/shard_map/ppermute | solution.py:328
  94.5 20.7 %collective-permute-start.5 = (bf16[16,16,1536]{2,1,0:T(8,128)(2,1)S(1)}, bf16[16,16,1536]{2,1,0:T(8,128)(2,1)}, u32[]{:S(2)}, u32[]{:S(2)}) collective-permute-start(bf16[16,16,1536]{2,1,0:T(8,128)(2,1)S(1)} %collective-permute-done.4.refs_0_.refs_4_), channel_id=1, source_target_pairs={{0,1},{1,0},{2,3},{3,2},{4,5},{5,4},{6,7},{7,6},{8,9},{9,8},{10,11... | collective-permute-start | bytes 2359304 | tf_op jit(solution)/shard_map/ppermute | solution.py:328
  97.0 32.5 %copy-start.10 = (bf16[16,16,1536]{2,1,0:T(8,128)(2,1)}, bf16[16,16,1536]{2,1,0:T(8,128)(2,1)S(1)}, u32[]{:S(2)}) copy-start(bf16[16,16,1536]{2,1,0:T(8,128)(2,1)S(1)} %collective-permute-done.refs_2_.refs_1_) | copy-start | bytes 2359300
  97.0 31.7 %collective-permute-start.8 = (bf16[20,16,1536]{2,1,0:T(8,128)(2,1)S(1)}, bf16[20,16,1536]{2,1,0:T(8,128)(2,1)}, u32[]{:S(2)}, u32[]{:S(2)}) collective-permute-start(bf16[20,16,1536]{2,1,0:T(8,128)(2,1)S(1)} %joined.2.refs_8_), channel_id=1, source_target_pairs={{0,1},{1,0},{2,3},{3,2},{4,5},{5,4},{6,7},{7,6},{8,9},{9,8},{10,11... | collective-permute-start | bytes 2949128 | tf_op jit(solution)/shard_map/ppermute | solution.py:328
  108.1 21.3 %collective-permute-start.10 = (bf16[20,16,1536]{2,1,0:T(8,128)(2,1)}, bf16[20,16,1536]{2,1,0:T(8,128)(2,1)}, u32[]{:S(2)}, u32[]{:S(2)}) collective-permute-start(bf16[20,16,1536]{2,1,0:T(8,128)(2,1)} %collective-permute-done.9.refs_10_), channel_id=1, source_target_pairs={{0,1},{1,0},{2,3},{3,2},{4,5},{5,4},{6,7},{7,6},{8,9},{9,8},{10,11... | collective-permute-start | bytes 2949128 | tf_op jit(solution)/shard_map/ppermute | solution.py:328
  114.9 13.0 %collective-permute-start.12 = (bf16[20,16,768]{2,1,0:T(8,128)(2,1)S(1)}, bf16[20,16,768]{2,1,0:T(8,128)(2,1)}, u32[]{:S(2)}, u32[]{:S(2)}) collective-permute-start(bf16[20,16,768]{2,1,0:T(8,128)(2,1)S(1)} %get-tuple-element.18.refs_14_), channel_id=1, source_target_pairs={{0,2},{1,3},{2,0},{3,1},{4,6},{5,7},{6,4},{7,5},{8,10},{9,11},{10,... | collective-permute-start | bytes 1474568 | tf_op jit(solution)/shard_map/ppermute | solution.py:328
  115.0 13.7 %collective-permute-start.17 = (bf16[20,16,768]{2,1,0:T(8,128)(2,1)S(1)}, bf16[20,16,768]{2,1,0:T(8,128)(2,1)S(1)}, u32[]{:S(2)}, u32[]{:S(2)}) collective-permute-start(bf16[20,16,768]{2,1,0:T(8,128)(2,1)S(1)} %get-tuple-element.17.refs_0_), channel_id=1, source_target_pairs={{0,1},{1,0},{2,3},{3,2},{4,5},{5,4},{6,7},{7,6},{8,9},{9,8},{10,11... | collective-permute-start | bytes 1474568 | tf_op jit(solution)/shard_map/ppermute | solution.py:328
  115.2 13.5 %collective-permute-start.13 = (bf16[20,16,768]{2,1,0:T(8,128)(2,1)S(1)}, bf16[20,16,768]{2,1,0:T(8,128)(2,1)S(1)}, u32[]{:S(2)}, u32[]{:S(2)}) collective-permute-start(bf16[20,16,768]{2,1,0:T(8,128)(2,1)S(1)} %get-tuple-element.18.refs_14_), channel_id=1, source_target_pairs={{0,1},{1,0},{2,3},{3,2},{4,5},{5,4},{6,7},{7,6},{8,9},{9,8},{10,11... | collective-permute-start | bytes 1474568 | tf_op jit(solution)/shard_map/ppermute | solution.py:328
  127.9 2.6 %collective-permute-start.15 = (bf16[20,16,768]{2,1,0:T(8,128)(2,1)}, bf16[20,16,768]{2,1,0:T(8,128)(2,1)}, u32[]{:S(2)}, u32[]{:S(2)}) collective-permute-start(bf16[20,16,768]{2,1,0:T(8,128)(2,1)} %collective-permute-done.12.refs_1_.refs_12_), channel_id=1, source_target_pairs={{0,1},{1,0},{2,3},{3,2},{4,5},{5,4},{6,7},{7,6},{8,9},{9,8},{10,11... | collective-permute-start | bytes 1474568 | tf_op jit(solution)/shard_map/ppermute | solution.py:328
  130.2 17.8 %collective-permute-start.14 = (bf16[20,16,768]{2,1,0:T(8,128)(2,1)}, bf16[20,16,768]{2,1,0:T(8,128)(2,1)S(1)}, u32[]{:S(2)}, u32[]{:S(2)}) collective-permute-start(bf16[20,16,768]{2,1,0:T(8,128)(2,1)} %follows.8.refs_14_), channel_id=1, source_target_pairs={{0,2},{1,3},{2,0},{3,1},{4,6},{5,7},{6,4},{7,5},{8,10},{9,11},{10,... | collective-permute-start | bytes 1474568 | tf_op jit(solution)/shard_map/ppermute | solution.py:328
  148.9 2.1 %collective-permute-start.16 = (bf16[20,16,768]{2,1,0:T(8,128)(2,1)}, bf16[20,16,768]{2,1,0:T(8,128)(2,1)S(1)}, u32[]{:S(2)}, u32[]{:S(2)}) collective-permute-start(bf16[20,16,768]{2,1,0:T(8,128)(2,1)} %follows.9.refs_12_), channel_id=1, source_target_pairs={{0,1},{1,0},{2,3},{3,2},{4,5},{5,4},{6,7},{7,6},{8,9},{9,8},{10,11... | collective-permute-start | bytes 1474568 | tf_op jit(solution)/shard_map/ppermute | solution.py:328
  (18 other events, 96.7 us)

commit v5 on v4

--- a/solution.py
+++ b/solution.py
@@ -312,6 +312,27 @@
     )(x, z_hi, *others)
 
 
+def beside(x, y):
+    width = x.shape[1]
+    out = jax.ShapeDtypeStruct((x.shape[0], width + y.shape[1]), x.dtype)
+
+    def kernel(x_ref, y_ref, out_ref):
+        out_ref[:, :width] = x_ref[...]
+        out_ref[:, width:] = y_ref[...]
+
+    whole = lambda a: pl.BlockSpec(a.shape, lambda i: (0, 0))
+    return pl.pallas_call(
+        kernel,
+        grid=(1,),
+        out_shape=out,
+        in_specs=[whole(x), whole(y)],
+        out_specs=whole(out),
+        cost_estimate=pl.CostEstimate(flops=0, bytes_accessed=2**20, transcendentals=0),
+        compiler_params=pltpu.CompilerParams(vmem_limit_bytes=16 * 1024 * 1024),
+        name="beside",
+    )(x, y)
+
+
 def follows(x, *others):
     return pl.pallas_call(
         lambda *refs: None,
@@ -404,7 +425,7 @@
     late_xc = swapped(late_x, 1)
     late_zc = swapped(late_z, 1)
     early = exchanged(follows(early, late_x, late_z, part_x))
-    early_x = exchanged(follows(jnp.concatenate([part_x, carry_x], axis=1), early))
+    early_x = exchanged(beside(part_x, carry_x))
     (early,) = joined(early, side, [(0, wide)], late_xz, place, rank)
     early_z = swapped(early, 2)
     low, high = joined(early_x, 1 - side, [(0, wide // 2), (wide // 2, wide // 2)])

time: 170 us -> 170 us (level)
  other arithmetic: 2.93 us -> 0.48 us
    ppermute x15, waiting for transfers between devices: 27.6 us -> 14.2 us  [swapped(): return lax.ppermute(x, 'pol', [(i, i ^ by) for i in range(4)])]
    all_to_all x4, waiting for transfers between devices: 1.01 us -> 14.3 us  [exchanged(): lax.all_to_all(x, 'tm', split_axis=0, concat_axis=0, axis_index_groups=gr...]
    concatenate x1 -> x0, other arithmetic: 2.45 us -> none  [on_device(): jnp.concatenate([part_x, carry_x], axis=1)]
    unnamed x40 -> x38, local copies, waits for them, and re-layouts: 6.52 us -> 6.31 us
  transfers between devices with their start and end apart: 22 -> 22, of which waited for: 8 -> 8; matrix products, arithmetic and copies ran while one was open for 2% -> 0% of each run, Pallas kernels for 19% -> 20%
where the time goes in v5:
time: 170 us; the launch traced here: 169 us
  Pallas kernels  60.2 us (35%)
  waiting for transfers between devices  57.1 us (34%)
  starting transfers between devices  44.7 us (26%)
  local copies, waits for them, and re-layouts  6.31 us (4%)
    pallas_call x2, Pallas kernels, grams(): pl.pallas_call(gram_kernel, grid=(chans,), out_shape=jax.ShapeDtypeStruct...  35.3 us
    ppermute x3, waiting for transfers between devices, crossed(): return lax.ppermute(x, ('tm', 'pol'), across)  28.5 us
    all_to_all x4, starting transfers between devices, exchanged(): lax.all_to_all(x, 'tm', split_axis=0, concat_axis=0, axis_index_groups=gr...  26 us
    pallas_call x2, Pallas kernels, spectra(): pl.pallas_call(functools.partial(spectra_kernel, spectra_taps, [o[:2] for...  21.9 us
    all_to_all x4, waiting for transfers between devices, exchanged(): lax.all_to_all(x, 'tm', split_axis=0, concat_axis=0, axis_index_groups=gr...  14.3 us
    ppermute x15, waiting for transfers between devices, swapped(): return lax.ppermute(x, 'pol', [(i, i ^ by) for i in range(4)])  14.2 us
    ppermute x15, starting transfers between devices, swapped(): return lax.ppermute(x, 'pol', [(i, i ^ by) for i in range(4)])  13.5 us
    unnamed x38, local copies, waits for them, and re-layouts  6.31 us
  transfers between devices with their start and end apart: 22, of which 8 were waited for; matrix products, arithmetic and copies ran while one was open for 0% of the time, Pallas kernels for 20%

profile of v5, /device:TPU:1, one launch (start us, length us, event | category | flops | bytes accessed | tf_op | source)
XLA Modules:
  0.0 169.1 jit_solution(12966463407655022847)
XLA Ops:
  0.0 9.1 %spectra.2 = (bf16[256,1536]{1,0:T(8,128)(2,1)}, bf16[256,1536]{1,0:T(8,128)(2,1)}) custom-call(bf16[32,49152]{1,0:T(8,128)(2,1)} %volts_ref.3, f32[4,8192]{1,0:T(4,128)} %constant.109.clone.window_ref, f32[32,512]{1,0:T(8,128)} %constant.110.clone.twiddle_ref, bf16[512,1024]{1,0:T(8,128)(2,1)} %constant.111.clone.table_ref, s32[1]{0:T(128)} %bitcast.side_ref), custom_call_target="tpu_custom_call" | custom-call | flops 1048576 | bytes 20971520 | tf_op jit(solution)/shard_map/spectra/pallas_call | solution.py:145
  9.1 4.6 %collective-permute-start.3 = (bf16[256,1536]{1,0:T(8,128)(2,1)}, bf16[256,1536]{1,0:T(8,128)(2,1)S(1)}, u32[]{:S(2)}, u32[]{:S(2)}) collective-permute-start(bf16[256,1536]{1,0:T(8,128)(2,1)} %get-tuple-element.13), channel_id=1, source_target_pairs={{0,18},{1,19},{2,16},{3,17},{4,22},{5,23},{6,20},{7,21},{8,26},{9,... | collective-permute-start | bytes 2359304 | tf_op jit(solution)/shard_map/ppermute | solution.py:395
  13.6 6.8 %all-to-all-start = ((bf16[16,16,1536]{2,1,0:T(8,128)(2,1)}), bf16[16,16,1536]{2,1,0:T(8,128)(2,1)}, u32[]{:S(2)}, u32[]{:S(2)}) async-start(bf16[16,16,1536]{2,1,0:T(8,128)(2,1)} %bitcast.9), calls=%async_computation | async-start | bytes 1572864 | tf_op jit(solution)/shard_map/all_to_all | solution.py:390
  20.5 12.9 %spectra.3 = (bf16[256,3072]{1,0:T(8,128)(2,1)}, bf16[256,1536]{1,0:T(8,128)(2,1)}, bf16[256,1536]{1,0:T(8,128)(2,1)}) custom-call(bf16[32,49152]{1,0:T(8,128)(2,1)} %volts_ref.3, f32[4,8192]{1,0:T(4,128)} %constant.109.clone.window_ref, f32[32,512]{1,0:T(8,128)} %constant.110.clone.twiddle_ref, bf16[512,1024]{1,0:T(8,128)(2,1)} %constant.111.clone.table_ref, ...), custom_call_target="tpu_custom_call" | custom-call | flops 1048576 | bytes 20971520 | tf_op jit(solution)/shard_map/spectra/pallas_call | solution.py:145
  33.5 0.9 copy-done.12
  34.4 6.7 %all-to-all-start.1 = ((bf16[16,16,1536]{2,1,0:T(8,128)(2,1)}), bf16[16,16,1536]{2,1,0:T(8,128)(2,1)}, u32[]{:S(2)}, u32[]{:S(2)}) async-start(bf16[16,16,1536]{2,1,0:T(8,128)(2,1)} %bitcast.8), calls=%async_computation.1 | async-start | bytes 1572864 | tf_op jit(solution)/shard_map/all_to_all | solution.py:390
  41.0 11.7 %collective-permute-done.7.refs_3_.x_ref = bf16[256,1536]{1,0:T(8,128)(2,1)S(1)} collective-permute-done((bf16[256,1536]{1,0:T(8,128)(2,1)}, bf16[256,1536]{1,0:T(8,128)(2,1)S(1)}, u32[]{:S(2)}, u32[]{:S(2)}) %collective-permute-start.7) | collective-permute-done | bytes 786464 | tf_op jit(solution)/shard_map/ppermute | solution.py:395
  52.7 1.0 all-to-all-done.1.refs_1_.refs_6_
  53.7 6.2 %all-to-all-start.2 = ((bf16[16,16,3072]{2,1,0:T(8,128)(2,1)}), bf16[16,16,3072]{2,1,0:T(8,128)(2,1)S(1)}, u32[]{:S(2)}, u32[]{:S(2)}) async-start(bf16[16,16,3072]{2,1,0:T(8,128)(2,1)} %bitcast.7), calls=%async_computation.2 | async-start | bytes 3145728 | tf_op jit(solution)/shard_map/all_to_all | solution.py:390
  61.0 16.9 %collective-permute-done.11.y_ref = bf16[256,1536]{1,0:T(8,128)(2,1)} collective-permute-done((bf16[256,1536]{1,0:T(8,128)(2,1)}, bf16[256,1536]{1,0:T(8,128)(2,1)}, u32[]{:S(2)}, u32[]{:S(2)}) %collective-permute-start.11) | collective-permute-done | bytes 786464 | tf_op jit(solution)/shard_map/ppermute | solution.py:395
  77.9 1.2 beside.1
  79.1 1.1 copy-done.3
  80.3 6.3 %all-to-all-start.3 = ((bf16[16,16,3072]{2,1,0:T(8,128)(2,1)}), bf16[16,16,3072]{2,1,0:T(8,128)(2,1)}, u32[]{:S(2)}, u32[]{:S(2)}) async-start(bf16[16,16,3072]{2,1,0:T(8,128)(2,1)} %bitcast.6), calls=%async_computation.3 | async-start | bytes 3145728 | tf_op jit(solution)/shard_map/all_to_all | solution.py:390
  87.7 4.2 %collective-permute-start = (bf16[16,16,1536]{2,1,0:T(8,128)(2,1)}, bf16[16,16,1536]{2,1,0:T(8,128)(2,1)S(1)}, u32[]{:S(2)}, u32[]{:S(2)}) collective-permute-start(bf16[16,16,1536]{2,1,0:T(8,128)(2,1)} %all-to-all-done.refs_1_.refs_0_), channel_id=1, source_target_pairs={{0,1},{1,0},{2,3},{3,2},{4,5},{5,4},{6,7},{7,6},{8,9},{9,8},{10,11... | collective-permute-start | bytes 2359304 | tf_op jit(solution)/shard_map/ppermute | solution.py:349
  92.4 13.3 %all-to-all-done.3.x_ref = bf16[16,16,3072]{2,1,0:T(8,128)(2,1)} async-done(((bf16[16,16,3072]{2,1,0:T(8,128)(2,1)}), bf16[16,16,3072]{2,1,0:T(8,128)(2,1)}, u32[]{:S(2)}, u32[]{:S(2)}) %all-to-all-start.3) | async-done | bytes 1572896 | tf_op jit(solution)/shard_map/all_to_all | solution.py:390
  105.6 1.6 joined.3
  107.2 6.2 %collective-permute-start.17 = (bf16[20,16,768]{2,1,0:T(8,128)(2,1)S(1)}, bf16[20,16,768]{2,1,0:T(8,128)(2,1)}, u32[]{:S(2)}, u32[]{:S(2)}) collective-permute-start(bf16[20,16,768]{2,1,0:T(8,128)(2,1)S(1)} %get-tuple-element.17.refs_0_), channel_id=1, source_target_pairs={{0,1},{1,0},{2,3},{3,2},{4,5},{5,4},{6,7},{7,6},{8,9},{9,8},{10,11... | collective-permute-start | bytes 1474568 | tf_op jit(solution)/shard_map/ppermute | solution.py:349
  114.1 0.9 collective-permute-done.17.refs_15_
  115.4 11.4 %collective-permute-done.12.refs_1_.refs_12_ = bf16[20,16,768]{2,1,0:T(8,128)(2,1)} collective-permute-done((bf16[20,16,768]{2,1,0:T(8,128)(2,1)S(1)}, bf16[20,16,768]{2,1,0:T(8,128)(2,1)}, u32[]{:S(2)}, u32[]{:S(2)}) %collective-permute-start.12) | collective-permute-done | bytes 491552 | tf_op jit(solution)/shard_map/ppermute | solution.py:349
  126.8 0.9 collective-permute-start.15
  128.7 1.0 copy-done.9
  130.0 17.7 %grams.2.refs_1_.refs_20_ = bf16[8,16,8,2,32,128]{5,4,3,2,1,0:T(8,128)(2,1)} custom-call(bf16[16,16,1536]{2,1,0:T(8,128)(2,1)} %all-to-all-done.refs_1_.refs_0_, bf16[16,16,1536]{2,1,0:T(8,128)(2,1)} %copy-done.10, bf16[16,16,1536]{2,1,0:T(8,128)(2,1)} %collective-permute-done.1.refs_2_, bf16[16,16,1536]{2,1,0:T(8,128)(2,1)} %collective-permute-done.2.refs_3_, ...), custom_call_target="tpu_custom_call" | custom-call | flops 4831838208 | bytes 15728640 | tf_op jit(solution)/shard_map/grams/pallas_call | solution.py:259
  148.8 1.9 %collective-permute-done.16.refs_13_ = bf16[20,16,768]{2,1,0:T(8,128)(2,1)S(1)} collective-permute-done((bf16[20,16,768]{2,1,0:T(8,128)(2,1)}, bf16[20,16,768]{2,1,0:T(8,128)(2,1)S(1)}, u32[]{:S(2)}, u32[]{:S(2)}) %collective-permute-start.16) | collective-permute-done | bytes 491552 | tf_op jit(solution)/shard_map/ppermute | solution.py:349
  151.4 17.6 %grams.3 = bf16[8,16,8,2,32,128]{5,4,3,2,1,0:T(8,128)(2,1)} custom-call(bf16[16,16,1536]{2,1,0:T(8,128)(2,1)} %all-to-all-done.refs_1_.refs_0_, bf16[16,16,1536]{2,1,0:T(8,128)(2,1)} %copy-done.10, bf16[16,16,1536]{2,1,0:T(8,128)(2,1)} %collective-permute-done.1.refs_2_, ...), custom_call_target="tpu_custom_call", output_to_operand_aliasing={{}: (20, {})} | custom-call | flops 4831838208 | bytes 15728640 | tf_op jit(solution)/shard_map/grams/pallas_call | solution.py:259
  (76 shorter events, 6.9 us)
Async XLA Ops:
  9.1 24.4 %collective-permute-start.3 = (bf16[256,1536]{1,0:T(8,128)(2,1)}, bf16[256,1536]{1,0:T(8,128)(2,1)S(1)}, u32[]{:S(2)}, u32[]{:S(2)}) collective-permute-start(bf16[256,1536]{1,0:T(8,128)(2,1)} %get-tuple-element.13), channel_id=1, source_target_pairs={{0,18},{1,19},{2,16},{3,17},{4,22},{5,23},{6,20},{7,21},{8,26},{9,... | collective-permute-start | bytes 2359304 | tf_op jit(solution)/shard_map/ppermute | solution.py:395
  13.6 19.8 %all-to-all-start = ((bf16[16,16,1536]{2,1,0:T(8,128)(2,1)}), bf16[16,16,1536]{2,1,0:T(8,128)(2,1)}, u32[]{:S(2)}, u32[]{:S(2)}) async-start(bf16[16,16,1536]{2,1,0:T(8,128)(2,1)} %bitcast.9), calls=%async_computation | async-start | bytes 1572864 | tf_op jit(solution)/shard_map/all_to_all | solution.py:390
  33.3 19.3 %collective-permute-start.7 = (bf16[256,1536]{1,0:T(8,128)(2,1)}, bf16[256,1536]{1,0:T(8,128)(2,1)S(1)}, u32[]{:S(2)}, u32[]{:S(2)}) collective-permute-start(bf16[256,1536]{1,0:T(8,128)(2,1)} %get-tuple-element.15), channel_id=1, source_target_pairs={{0,18},{1,19},{2,16},{3,17},{4,22},{5,23},{6,20},{7,21},{8,26},{9,... | collective-permute-start | bytes 2359304 | tf_op jit(solution)/shard_map/ppermute | solution.py:395
  33.4 19.3 %collective-permute-start.1 = (bf16[16,16,1536]{2,1,0:T(8,128)(2,1)}, bf16[16,16,1536]{2,1,0:T(8,128)(2,1)}, u32[]{:S(2)}, u32[]{:S(2)}) collective-permute-start(bf16[16,16,1536]{2,1,0:T(8,128)(2,1)} %all-to-all-done.refs_1_.refs_0_), channel_id=1, source_target_pairs={{0,2},{1,3},{2,0},{3,1},{4,6},{5,7},{6,4},{7,5},{8,10},{9,11},{10,... | collective-permute-start | bytes 2359304 | tf_op jit(solution)/shard_map/ppermute | solution.py:349
  34.4 19.3 %all-to-all-start.1 = ((bf16[16,16,1536]{2,1,0:T(8,128)(2,1)}), bf16[16,16,1536]{2,1,0:T(8,128)(2,1)}, u32[]{:S(2)}, u32[]{:S(2)}) async-start(bf16[16,16,1536]{2,1,0:T(8,128)(2,1)} %bitcast.8), calls=%async_computation.1 | async-start | bytes 1572864 | tf_op jit(solution)/shard_map/all_to_all | solution.py:390
  53.7 26.5 %all-to-all-start.2 = ((bf16[16,16,3072]{2,1,0:T(8,128)(2,1)}), bf16[16,16,3072]{2,1,0:T(8,128)(2,1)S(1)}, u32[]{:S(2)}, u32[]{:S(2)}) async-start(bf16[16,16,3072]{2,1,0:T(8,128)(2,1)} %bitcast.7), calls=%async_computation.2 | async-start | bytes 3145728 | tf_op jit(solution)/shard_map/all_to_all | solution.py:390
  59.9 17.9 %collective-permute-start.11 = (bf16[256,1536]{1,0:T(8,128)(2,1)}, bf16[256,1536]{1,0:T(8,128)(2,1)}, u32[]{:S(2)}, u32[]{:S(2)}) collective-permute-start(bf16[256,1536]{1,0:T(8,128)(2,1)} %get-tuple-element.16), channel_id=1, source_target_pairs={{0,18},{1,19},{2,16},{3,17},{4,22},{5,23},{6,20},{7,21},{8,26},{9,... | collective-permute-start | bytes 2359304 | tf_op jit(solution)/shard_map/ppermute | solution.py:395
  60.5 26.4 %collective-permute-start.4 = (bf16[16,16,1536]{2,1,0:T(8,128)(2,1)}, bf16[16,16,1536]{2,1,0:T(8,128)(2,1)S(1)}, u32[]{:S(2)}, u32[]{:S(2)}) collective-permute-start(bf16[16,16,1536]{2,1,0:T(8,128)(2,1)} %all-to-all-done.1.refs_1_.refs_6_), channel_id=1, source_target_pairs={{0,2},{1,3},{2,0},{3,1},{4,6},{5,7},{6,4},{7,5},{8,10},{9,11},{10,... | collective-permute-start | bytes 2359304 | tf_op jit(solution)/shard_map/ppermute | solution.py:349
  80.3 25.4 %all-to-all-start.3 = ((bf16[16,16,3072]{2,1,0:T(8,128)(2,1)}), bf16[16,16,3072]{2,1,0:T(8,128)(2,1)}, u32[]{:S(2)}, u32[]{:S(2)}) async-start(bf16[16,16,3072]{2,1,0:T(8,128)(2,1)} %bitcast.6), calls=%async_computation.3 | async-start | bytes 3145728 | tf_op jit(solution)/shard_map/all_to_all | solution.py:390
  86.8 27.1 %copy-start.2 = (bf16[16,16,1536]{2,1,0:T(8,128)(2,1)}, bf16[16,16,1536]{2,1,0:T(8,128)(2,1)S(1)}, u32[]{:S(2)}) copy-start(bf16[16,16,1536]{2,1,0:T(8,128)(2,1)S(1)} %collective-permute-done.4.refs_0_.refs_4_) | copy-start | bytes 2359300
  87.6 42.1 %copy-start = (bf16[20,16,1536]{2,1,0:T(8,128)(2,1)}, bf16[20,16,1536]{2,1,0:T(8,128)(2,1)S(1)}, u32[]{:S(2)}) copy-start(bf16[20,16,1536]{2,1,0:T(8,128)(2,1)S(1)} %joined.2.refs_8_) | copy-start | bytes 2949124
  87.7 25.9 %collective-permute-start.9 = (bf16[20,16,1536]{2,1,0:T(8,128)(2,1)S(1)}, bf16[20,16,1536]{2,1,0:T(8,128)(2,1)}, u32[]{:S(2)}, u32[]{:S(2)}) collective-permute-start(bf16[20,16,1536]{2,1,0:T(8,128)(2,1)S(1)} %joined.2.refs_8_), channel_id=1, source_target_pairs={{0,2},{1,3},{2,0},{3,1},{4,6},{5,7},{6,4},{7,5},{8,10},{9,11},{10,... | collective-permute-start | bytes 2949128 | tf_op jit(solution)/shard_map/ppermute | solution.py:349
  87.7 25.7 %collective-permute-start = (bf16[16,16,1536]{2,1,0:T(8,128)(2,1)}, bf16[16,16,1536]{2,1,0:T(8,128)(2,1)S(1)}, u32[]{:S(2)}, u32[]{:S(2)}) collective-permute-start(bf16[16,16,1536]{2,1,0:T(8,128)(2,1)} %all-to-all-done.refs_1_.refs_0_), channel_id=1, source_target_pairs={{0,1},{1,0},{2,3},{3,2},{4,5},{5,4},{6,7},{7,6},{8,9},{9,8},{10,11... | collective-permute-start | bytes 2359304 | tf_op jit(solution)/shard_map/ppermute | solution.py:349
  91.8 22.1 %collective-permute-start.2 = (bf16[16,16,1536]{2,1,0:T(8,128)(2,1)}, bf16[16,16,1536]{2,1,0:T(8,128)(2,1)}, u32[]{:S(2)}, u32[]{:S(2)}) collective-permute-start(bf16[16,16,1536]{2,1,0:T(8,128)(2,1)} %collective-permute-done.1.refs_2_), channel_id=1, source_target_pairs={{0,1},{1,0},{2,3},{3,2},{4,5},{5,4},{6,7},{7,6},{8,9},{9,8},{10,11... | collective-permute-start | bytes 2359304 | tf_op jit(solution)/shard_map/ppermute | solution.py:349
  91.9 22.0 %collective-permute-start.6 = (bf16[16,16,1536]{2,1,0:T(8,128)(2,1)}, bf16[16,16,1536]{2,1,0:T(8,128)(2,1)}, u32[]{:S(2)}, u32[]{:S(2)}) collective-permute-start(bf16[16,16,1536]{2,1,0:T(8,128)(2,1)} %all-to-all-done.1.refs_1_.refs_6_), channel_id=1, source_target_pairs={{0,1},{1,0},{2,3},{3,2},{4,5},{5,4},{6,7},{7,6},{8,9},{9,8},{10,11... | collective-permute-start | bytes 2359304 | tf_op jit(solution)/shard_map/ppermute | solution.py:349
  107.2 7.8 %collective-permute-start.17 = (bf16[20,16,768]{2,1,0:T(8,128)(2,1)S(1)}, bf16[20,16,768]{2,1,0:T(8,128)(2,1)}, u32[]{:S(2)}, u32[]{:S(2)}) collective-permute-start(bf16[20,16,768]{2,1,0:T(8,128)(2,1)S(1)} %get-tuple-element.17.refs_0_), channel_id=1, source_target_pairs={{0,1},{1,0},{2,3},{3,2},{4,5},{5,4},{6,7},{7,6},{8,9},{9,8},{10,11... | collective-permute-start | bytes 1474568 | tf_op jit(solution)/shard_map/ppermute | solution.py:349
  113.4 14.3 %collective-permute-start.8 = (bf16[20,16,1536]{2,1,0:T(8,128)(2,1)S(1)}, bf16[20,16,1536]{2,1,0:T(8,128)(2,1)S(1)}, u32[]{:S(2)}, u32[]{:S(2)}) collective-permute-start(bf16[20,16,1536]{2,1,0:T(8,128)(2,1)S(1)} %joined.2.refs_8_), channel_id=1, source_target_pairs={{0,1},{1,0},{2,3},{3,2},{4,5},{5,4},{6,7},{7,6},{8,9},{9,8},{10,11... | collective-permute-start | bytes 2949128 | tf_op jit(solution)/shard_map/ppermute | solution.py:349
  113.5 16.2 %collective-permute-start.10 = (bf16[20,16,1536]{2,1,0:T(8,128)(2,1)}, bf16[20,16,1536]{2,1,0:T(8,128)(2,1)}, u32[]{:S(2)}, u32[]{:S(2)}) collective-permute-start(bf16[20,16,1536]{2,1,0:T(8,128)(2,1)} %collective-permute-done.9.refs_10_), channel_id=1, source_target_pairs={{0,1},{1,0},{2,3},{3,2},{4,5},{5,4},{6,7},{7,6},{8,9},{9,8},{10,11... | collective-permute-start | bytes 2949128 | tf_op jit(solution)/shard_map/ppermute | solution.py:349
  113.9 12.9 %collective-permute-start.12 = (bf16[20,16,768]{2,1,0:T(8,128)(2,1)S(1)}, bf16[20,16,768]{2,1,0:T(8,128)(2,1)}, u32[]{:S(2)}, u32[]{:S(2)}) collective-permute-start(bf16[20,16,768]{2,1,0:T(8,128)(2,1)S(1)} %get-tuple-element.18.refs_14_), channel_id=1, source_target_pairs={{0,2},{1,3},{2,0},{3,1},{4,6},{5,7},{6,4},{7,5},{8,10},{9,11},{10,... | collective-permute-start | bytes 1474568 | tf_op jit(solution)/shard_map/ppermute | solution.py:349
  113.9 13.8 %collective-permute-start.5 = (bf16[16,16,1536]{2,1,0:T(8,128)(2,1)S(1)}, bf16[16,16,1536]{2,1,0:T(8,128)(2,1)S(1)}, u32[]{:S(2)}, u32[]{:S(2)}) collective-permute-start(bf16[16,16,1536]{2,1,0:T(8,128)(2,1)S(1)} %collective-permute-done.4.refs_0_.refs_4_), channel_id=1, source_target_pairs={{0,1},{1,0},{2,3},{3,2},{4,5},{5,4},{6,7},{7,6},{8,9},{9,8},{10,11... | collective-permute-start | bytes 2359304 | tf_op jit(solution)/shard_map/ppermute | solution.py:349
  115.0 12.7 %collective-permute-start.13 = (bf16[20,16,768]{2,1,0:T(8,128)(2,1)S(1)}, bf16[20,16,768]{2,1,0:T(8,128)(2,1)S(1)}, u32[]{:S(2)}, u32[]{:S(2)}) collective-permute-start(bf16[20,16,768]{2,1,0:T(8,128)(2,1)S(1)} %get-tuple-element.18.refs_14_), channel_id=1, source_target_pairs={{0,1},{1,0},{2,3},{3,2},{4,5},{5,4},{6,7},{7,6},{8,9},{9,8},{10,11... | collective-permute-start | bytes 1474568 | tf_op jit(solution)/shard_map/ppermute | solution.py:349
  126.8 3.2 %collective-permute-start.15 = (bf16[20,16,768]{2,1,0:T(8,128)(2,1)}, bf16[20,16,768]{2,1,0:T(8,128)(2,1)}, u32[]{:S(2)}, u32[]{:S(2)}) collective-permute-start(bf16[20,16,768]{2,1,0:T(8,128)(2,1)} %collective-permute-done.12.refs_1_.refs_12_), channel_id=1, source_target_pairs={{0,1},{1,0},{2,3},{3,2},{4,5},{5,4},{6,7},{7,6},{8,9},{9,8},{10,11... | collective-permute-start | bytes 1474568 | tf_op jit(solution)/shard_map/ppermute | solution.py:349
  129.7 18.0 %collective-permute-start.14 = (bf16[20,16,768]{2,1,0:T(8,128)(2,1)}, bf16[20,16,768]{2,1,0:T(8,128)(2,1)S(1)}, u32[]{:S(2)}, u32[]{:S(2)}) collective-permute-start(bf16[20,16,768]{2,1,0:T(8,128)(2,1)} %follows.6.refs_14_), channel_id=1, source_target_pairs={{0,2},{1,3},{2,0},{3,1},{4,6},{5,7},{6,4},{7,5},{8,10},{9,11},{10,... | collective-permute-start | bytes 1474568 | tf_op jit(solution)/shard_map/ppermute | solution.py:349
  148.5 2.1 %collective-permute-start.16 = (bf16[20,16,768]{2,1,0:T(8,128)(2,1)}, bf16[20,16,768]{2,1,0:T(8,128)(2,1)S(1)}, u32[]{:S(2)}, u32[]{:S(2)}) collective-permute-start(bf16[20,16,768]{2,1,0:T(8,128)(2,1)} %follows.7.refs_12_), channel_id=1, source_target_pairs={{0,1},{1,0},{2,3},{3,2},{4,5},{5,4},{6,7},{7,6},{8,9},{9,8},{10,11... | collective-permute-start | bytes 1474568 | tf_op jit(solution)/shard_map/ppermute | solution.py:349
  (17 other events, 115.0 us)
